TPU v7x, 32 devices: a whole 2x2x4 slice. The times are simulated.
32 devices in a mesh: art: 16 (over z, y, core), seq: 2 (over x).
Axes of the slice: x: 2, y: 2, z: 4, core: 2. Of those that a mesh axis runs over, the one named last changes fastest.
Arguments:
- queries: bfloat16 [192, 2, 256, 128], P('art', 'seq'), may hold values from -6 to 6
- cand_owner: int32 [384, 16, 4], P(('art', 'seq')), may hold values from 0 to 15, all different within a row; in each aligned block of 192 rows (0 to 191, 192 to 383, ..., all dimensions but the last counted through in order) at most 72 rows name the same one
- cand_local: int32 [384, 16, 4], P(('art', 'seq')), may hold values from 0 to 255, as said below
- companies: bfloat16 [4096, 64, 128], P('art'), may hold values from -6 to 6
Outputs:
- relevance: float32 [384, 64], P(('art', 'seq'))
- probs: float32 [384, 64], P(('art', 'seq'))
Inputs may be any that keep to these rules, and one draw needn't show every extreme that they name: `cand_owner`: each row of four candidates names four different owners. Among the candidates of one device's 12 articles (aligned blocks of 12 articles in the order of the array), no owner is named more than 72 times, a bound that some block reaches. `cand_local`: the candidates of one device's 12 articles (aligned blocks of 12 articles in the order of the array) name exactly 36 different local indices in all.
All inputs are finite; a program needn't handle non-finite values.
Results may differ from a plain program's by a relative error of at most 0.0088.
Values may be sent and summed in bfloat16 or wider, within the bound.
No kernel may reach another device: no remote copies, remote signals or barrier semaphores. Data moves between devices by JAX's collectives and lax.ppermute only.
A program may use at most 128 MiB of HBM per device.

v0:
```python
import jax
import jax.numpy as jnp
from jax import lax
from jax.sharding import PartitionSpec as P

LC = 64
NC = 64


EPS = 1e-06
SHARP = 16.0
TEMPER = 4.0


def unit_rows(values):
    wide = values.astype(jnp.float32)
    return (wide * lax.rsqrt(jnp.sum(wide * wide, axis=-1, keepdims=True) + EPS)).astype(
        jnp.bfloat16
    )


def pool_pair(pair):
    query_pair, block_pair = pair
    sims = jnp.einsum("aqe,ake->aqk", query_pair, block_pair, preferred_element_type=jnp.float32)
    count = query_pair.shape[0]
    tokens = query_pair.shape[1]
    mass = jnp.sum(jnp.exp(sims * SHARP).reshape(count, tokens, NC, LC), axis=-1)
    return jnp.sum(jnp.log(mass), axis=1) / SHARP


def owner_ranks(owner_table, marks):
    return jnp.sum(jnp.cumsum(owner_table * marks[:, None], axis=0) * owner_table, axis=1) - 1


def per_device(queries, cand_owner, cand_local, companies):
    moved = lax.all_to_all(queries, "seq", split_axis=0, concat_axis=1, tiled=True)
    mine = moved.reshape(-1, moved.shape[2], moved.shape[3])
    query_unit = unit_rows(mine)
    catalog = unit_rows(companies)
    articles = mine.shape[0]
    width = mine.shape[2]
    owners = cand_owner.reshape(-1)
    local_ids = cand_local.reshape(-1)
    request_count = owners.shape[0]
    owner_count = lax.axis_size("art")
    cap_slots = 3 * request_count // (2 * owner_count)
    owner_table = (owners[:, None] == jnp.arange(owner_count, dtype=jnp.int32)[None, :]).astype(
        jnp.int32
    )
    every_one = jnp.ones((request_count,), jnp.int32)
    slot_index = owner_ranks(owner_table, every_one)
    table = jnp.zeros((owner_count, cap_slots), jnp.int32).at[owners, slot_index].set(local_ids)
    arrived = lax.all_to_all(
        catalog[lax.all_to_all(table, "art", split_axis=0, concat_axis=0, tiled=True)],
        "art",
        split_axis=0,
        concat_axis=0,
        tiled=True,
    )
    chosen = arrived[owners, slot_index]
    blocks = chosen.reshape(articles // 2, 2, NC * LC, width)
    query_pairs = query_unit.reshape(articles // 2, 2, query_unit.shape[1], width)
    score = lax.map(pool_pair, (query_pairs, blocks)).reshape(articles, NC)
    relevance = score - jnp.mean(score, axis=-1, keepdims=True)
    weights = jnp.exp(TEMPER * relevance)
    probs = weights / jnp.sum(weights, axis=-1, keepdims=True)
    return (relevance, probs)


def solution(mesh):
    placed = (
        P("art", "seq", None, None),
        P(("art", "seq"), None, None),
        P(("art", "seq"), None, None),
        P("art", None, None),
    )
    return jax.shard_map(
        per_device,
        mesh=mesh,
        in_specs=placed,
        out_specs=(P(("art", "seq"), None), P(("art", "seq"), None)),
        check_vma=False,
    )
```

profile of v0, /device:TPU:15, one launch (start us, length us, event | category | flops | bytes accessed | tf_op | source)
XLA Modules:
  0.0 708.7 jit_solution(12762589930854106556)
XLA Ops:
  5.6 104.6 %scatter_fusion = s32[16,72]{1,0:T(8,128)} fusion(s32[16,72]{1,0:T(8,128)} %broadcast.127, s32[768]{0:T(1024)S(1)} %get-tuple-element.34, s32[768]{0:T(1024)S(1)} %reshape.195), kind=kCustom, calls=%fused_computation.2 | custom fusion | bytes 15360 | tf_op jit(solution)/shard_map/scatter | solution.py:52
  110.2 6.3 all-to-all-start.1
  124.8 5.8 fusion.6
  130.7 28.7 %gather_fusion = bf16[1152,64,128]{2,1,0:T(8,128)(2,1)} fusion(bf16[256,64,128]{2,1,0:T(8,128)(2,1)} %fusion.6, s32[2048]{0:T(1024)S(1)} %pad_clamp_fusion), kind=kCustom, calls=%fused_computation | custom fusion | bytes 37753344 | tf_op jit(solution)/shard_map/gather | solution.py:54
  159.5 7.4 %all-to-all-start.2 = ((bf16[16,72,64,128]{3,2,1,0:T(8,128)(2,1)}), bf16[16,72,64,128]{3,2,1,0:T(8,128)(2,1)}, u32[]{:S(2)}, u32[]{:S(2)}) async-start(bf16[16,72,64,128]{3,2,1,0:T(8,128)(2,1)} %bitcast.54), calls=%async_computation.2 | async-start | bytes 37748736 | tf_op jit(solution)/shard_map/all_to_all | solution.py:53
  168.0 405.9 %all-to-all-done.2 = bf16[16,72,64,128]{3,2,1,0:T(8,128)(2,1)} async-done(((bf16[16,72,64,128]{3,2,1,0:T(8,128)(2,1)}), bf16[16,72,64,128]{3,2,1,0:T(8,128)(2,1)}, u32[]{:S(2)}, u32[]{:S(2)}) %all-to-all-start.2) | async-done | bytes 18874400 | tf_op jit(solution)/shard_map/all_to_all | solution.py:53
  573.9 15.1 %gather_fusion.1 = bf16[768,64,128]{2,1,0:T(8,128)(2,1)} fusion(bf16[16,72,64,128]{3,2,1,0:T(8,128)(2,1)} %all-to-all-done.2, s32[768]{0:T(1024)S(1)} %get-tuple-element.33), kind=kCustom, calls=%fused_computation.1 | custom fusion | bytes 25171968 | tf_op jit(solution)/shard_map/gather | solution.py:60
  589.0 118.6 %while.10 = (s32[]{:T(128)}, f32[6,2,64]{2,1,0:T(2,128)S(1)}, bf16[6,2,256,128]{3,2,0,1:T(8,128)(2,1)S(1)}, bf16[6,2,4096,128]{3,2,1,0:T(8,128)(2,1)}, s32[]{:T(128)}) while((s32[]{:T(128)}, f32[6,2,64]{2,1,0:T(2,128)S(1)}, bf16[6,2,256,128]{3,2,0,1:T(8,128)(2,1)S(1)}, bf16[6,2,4096,128]{3,2,1,0:T(8,128)(2,1)}, s32[]{:T(128)}) %tuple.30), condition=%wide.region_9.10_spmd, body=%wide.region_6.9_spmd.sunk | while | flops 541065216 | bytes 36048448 | solution.py:63
  589.0 6.1 multiply_exponential_fusion.2
  595.1 8.9 %copy.27 = f32[2,256,4096]{1,2,0:T(8,128)} copy(f32[2,256,4096]{2,1,0:T(8,128)} %multiply_exponential_fusion.2) | data formatting | bytes 16777216 | tf_op jit(solution)/shard_map/while/body/eval_jaxpr/exp | solution.py:27
  604.0 4.6 bitcast_reduce_fusion.2
  608.7 6.1 multiply_exponential_fusion.2
  614.8 8.9 %copy.27 = f32[2,256,4096]{1,2,0:T(8,128)} copy(f32[2,256,4096]{2,1,0:T(8,128)} %multiply_exponential_fusion.2) | data formatting | bytes 16777216 | tf_op jit(solution)/shard_map/while/body/eval_jaxpr/exp | solution.py:27
  623.7 4.6 bitcast_reduce_fusion.2
  628.5 6.1 multiply_exponential_fusion.2
  634.6 8.9 %copy.27 = f32[2,256,4096]{1,2,0:T(8,128)} copy(f32[2,256,4096]{2,1,0:T(8,128)} %multiply_exponential_fusion.2) | data formatting | bytes 16777216 | tf_op jit(solution)/shard_map/while/body/eval_jaxpr/exp | solution.py:27
  643.5 4.6 bitcast_reduce_fusion.2
  648.3 6.1 multiply_exponential_fusion.2
  654.3 8.9 %copy.27 = f32[2,256,4096]{1,2,0:T(8,128)} copy(f32[2,256,4096]{2,1,0:T(8,128)} %multiply_exponential_fusion.2) | data formatting | bytes 16777216 | tf_op jit(solution)/shard_map/while/body/eval_jaxpr/exp | solution.py:27
  663.3 4.6 bitcast_reduce_fusion.2
  668.0 6.1 multiply_exponential_fusion.2
  674.1 8.9 %copy.27 = f32[2,256,4096]{1,2,0:T(8,128)} copy(f32[2,256,4096]{2,1,0:T(8,128)} %multiply_exponential_fusion.2) | data formatting | bytes 16777216 | tf_op jit(solution)/shard_map/while/body/eval_jaxpr/exp | solution.py:27
  687.8 6.1 multiply_exponential_fusion.2
  693.9 8.9 %copy.27 = f32[2,256,4096]{1,2,0:T(8,128)} copy(f32[2,256,4096]{2,1,0:T(8,128)} %multiply_exponential_fusion.2) | data formatting | bytes 16777216 | tf_op jit(solution)/shard_map/while/body/eval_jaxpr/exp | solution.py:27
  (49 shorter events, 25.5 us)
Async XLA Ops:
  110.2 10.8 %all-to-all-start.1 = ((s32[16,1,72]{2,1,0:T(1,128)}), s32[16,1,72]{2,1,0:T(1,128)S(1)}, u32[]{:S(2)}, u32[]{:S(2)}) async-start(s32[16,1,72]{2,1,0:T(1,128)} %bitcast.11), calls=%async_computation.1 | async-start | bytes 16384 | tf_op jit(solution)/shard_map/all_to_all | solution.py:54
  121.0 38.5 %all-to-all-start = ((bf16[12,1,256,128]{3,2,1,0:T(8,128)(2,1)}), bf16[12,1,256,128]{3,2,1,0:T(8,128)(2,1)S(1)}, u32[]{:S(2)}, u32[]{:S(2)}) async-start(bf16[12,1,256,128]{3,2,1,0:T(8,128)(2,1)} %param.6), calls=%async_computation | async-start | bytes 1572864 | tf_op jit(solution)/shard_map/all_to_all | solution.py:36
  159.5 414.5 %all-to-all-start.2 = ((bf16[16,72,64,128]{3,2,1,0:T(8,128)(2,1)}), bf16[16,72,64,128]{3,2,1,0:T(8,128)(2,1)}, u32[]{:S(2)}, u32[]{:S(2)}) async-start(bf16[16,72,64,128]{3,2,1,0:T(8,128)(2,1)} %bitcast.54), calls=%async_computation.2 | async-start | bytes 37748736 | tf_op jit(solution)/shard_map/all_to_all | solution.py:53
where the time goes:
time: 713 us; the launch traced here: 709 us
  waiting for transfers between devices  406 us (57%)
  local copies, waits for them, and re-layouts  205 us (29%)
  other arithmetic  42.7 us (6%)
  matrix products  36.4 us (5%)
  starting transfers between devices  17.6 us (2%)
    all_to_all x1, waiting for transfers between devices, per_device(): lax.all_to_all(catalog[lax.all_to_all(table, 'art', split_axis=0, concat_...  406 us
    scatter x1, local copies, waits for them, and re-layouts, per_device(): jnp.zeros((owner_count, cap_slots), jnp.int32).at[owners, slot_index]  105 us
    exp x6, local copies, waits for them, and re-layouts, pool_pair(): jnp.exp(sims * SHARP).reshape(count, tokens, NC, LC)  53.5 us
    dot_general x6, matrix products, pool_pair(): jnp.einsum('aqe,ake->aqk', query_pair, block_pair, preferred_element_type...  36.4 us
    gather x1, local copies, waits for them, and re-layouts, per_device(): catalog[lax.all_to_all(table, 'art', split_axis=0, concat_axis=0, tiled=T...  28.7 us
    reduce_sum x6, other arithmetic, pool_pair(): jnp.sum(jnp.exp(sims * SHARP).reshape(count, tokens, NC, LC), axis=-1)  27.7 us
    gather x1, local copies, waits for them, and re-layouts, per_device(): chosen = arrived[owners, slot_index]  15.1 us
  transfers between devices with their start and end apart: 3, of which 1 were waited for; matrix products, arithmetic and copies ran while one was open for 6% of the time, Pallas kernels for 0%

commit v1 on v0

v1 whole, which is shorter than its diff:
```python
import functools
import math

import jax
import jax.numpy as jnp
from jax import lax
from jax.experimental import pallas as pl
from jax.experimental.pallas import tpu as pltpu
from jax.sharding import PartitionSpec as P

NC = 64
EPS = 1e-06
SHARP = 16.0
TEMPER = 4.0
GROUP = 4


def unit_kernel(own_ref, other_ref, out_ref):
    step = pl.program_id(0)

    def unit(ref):
        wide = ref[...].astype(jnp.float32)
        norm = jnp.sum(wide * wide, axis=-1, keepdims=True)
        out_ref[...] = (wide * lax.rsqrt(norm + EPS)).astype(jnp.bfloat16)

    half = pl.num_programs(0) // 2

    @pl.when(step < half)
    def _():
        unit(own_ref)

    @pl.when(step >= half)
    def _():
        unit(other_ref)


def unit_blocks(own, other):
    count, tokens, width = own.shape
    tile = 32
    half = count // tile
    return pl.pallas_call(
        unit_kernel,
        out_shape=jax.ShapeDtypeStruct((2 * count, tokens, width), jnp.bfloat16),
        grid=(2 * half,),
        in_specs=[
            pl.BlockSpec((tile, tokens, width), lambda i: (jnp.minimum(i, half - 1), 0, 0)),
            pl.BlockSpec((tile, tokens, width), lambda i: (jnp.maximum(i - half, 0), 0, 0)),
        ],
        out_specs=pl.BlockSpec((tile, tokens, width), lambda i: (i, 0, 0)),
        cost_estimate=pl.CostEstimate(
            flops=4 * own.size, bytes_accessed=8 * own.size, transcendentals=0
        ),
        name="unit_blocks",
    )(own, other)


def score_article(rows, base, count_ref, list_ref, query_ref, catalog_ref, out_ref, mass_ref):
    query = query_ref[0]
    wide = query.astype(jnp.float32)
    ones = jnp.ones((8, query.shape[1]), jnp.bfloat16)
    norm = lax.dot_general(
        ones,
        (wide * wide).astype(jnp.bfloat16),
        (((1,), (1,)), ((), ())),
        preferred_element_type=jnp.float32,
    )
    scale = lax.rsqrt(norm + EPS)[0:1] * (SHARP * math.log2(math.e))
    turned = query.T
    mass_ref[...] = jnp.ones_like(mass_ref)
    tokens = catalog_ref.shape[1]
    position = base + pl.program_id(0)
    count = count_ref[position]

    def some(step, carry):
        entries = [list_ref[position, step * GROUP + g] for g in range(GROUP)]
        blocks = jnp.concatenate([catalog_ref[e // 128] for e in entries], axis=0)
        sims = jnp.dot(blocks, turned, preferred_element_type=jnp.float32)
        grown = jnp.exp2(sims * scale)
        for g, e in enumerate(entries):
            mass_ref[pl.ds(e % 128, 1), :] = jnp.sum(
                grown[g * tokens : (g + 1) * tokens], axis=0, keepdims=True
            )
        return carry

    lax.fori_loop(0, (count + GROUP - 1) // GROUP, some, 0)
    logs = jnp.log(mass_ref[0:NC, :])
    out_ref[0] = lax.dot_general(
        jnp.full((8, logs.shape[1]), 1.0 / SHARP, jnp.float32),
        logs,
        (((1,), (1,)), ((), ())),
        precision=lax.Precision.HIGHEST,
        preferred_element_type=jnp.float32,
    )


def score_kernel(rows, count_ref, list_ref, first_ref, second_ref, catalog_ref, a_ref, b_ref, mass_ref):
    score_article(rows, 0, count_ref, list_ref, first_ref, catalog_ref, a_ref, mass_ref)
    score_article(rows, rows, count_ref, list_ref, second_ref, catalog_ref, b_ref, mass_ref)


def score_chunks(first, second, rows, begin, counts, lists, catalog):
    _, tokens, width = first.shape
    blocks, keys, _ = catalog.shape
    a, b = pl.pallas_call(
        functools.partial(score_kernel, rows),
        out_shape=[jax.ShapeDtypeStruct((rows, 8, NC), jnp.float32)] * 2,
        grid_spec=pltpu.PrefetchScalarGridSpec(
            num_scalar_prefetch=2,
            grid=(rows,),
            in_specs=[
                pl.BlockSpec((1, tokens, width), lambda i, *_: (i, 0, 0)),
                pl.BlockSpec((1, tokens, width), lambda i, *_: (i + begin, 0, 0)),
                pl.BlockSpec(memory_space=pltpu.VMEM),
            ],
            out_specs=[pl.BlockSpec((1, 8, NC), lambda i, *_: (i, 0, 0))] * 2,
            scratch_shapes=[pltpu.VMEM((NC + 8, tokens), jnp.float32)],
        ),
        compiler_params=pltpu.CompilerParams(vmem_limit_bytes=40 * 1024 * 1024),
        cost_estimate=pl.CostEstimate(
            flops=2 * 2 * rows * 8 * tokens * keys * width,
            bytes_accessed=2 * catalog.size,
            transcendentals=2 * rows * 8 * tokens * keys,
        ),
        name="score_chunks",
    )(counts, lists, first, second, catalog)
    return a[:, 0], b[:, 0]


def per_device(chips, ring, queries, cand_owner, cand_local, companies):
    articles = queries.shape[0]
    seqs = lax.axis_size("seq")
    arts = lax.axis_size("art")
    art, seq = lax.axis_index("art"), lax.axis_index("seq")
    chip, core = art // 2, art % 2
    blocks = companies.shape[0]
    mine = queries.reshape(articles, queries.shape[2], queries.shape[3])

    def turn(step):
        return [
            (2 * ring[i] + c, 2 * ring[(i + step) % chips] + c) for i in range(chips) for c in (0, 1)
        ]

    ahead = [mine]
    behind = [mine]
    half = chips // 2
    rows = articles // 2
    for _ in range(half - 1):
        ahead.append(lax.ppermute(ahead[-1], "art", turn(1)))
        behind.append(lax.ppermute(behind[-1], "art", turn(-1)))
    ahead.append(lax.ppermute(ahead[-1][:rows], "art", turn(1)))
    behind.append(lax.ppermute(behind[-1][rows:], "art", turn(-1)))

    other = lax.ppermute(companies, "art", [(i, i ^ 1) for i in range(arts)])
    catalog = unit_blocks(companies, other)

    ids = (cand_owner * blocks + cand_local).reshape(1, articles, NC)
    every = lax.all_to_all(
        jnp.broadcast_to(ids, (arts * seqs, articles, NC)),
        ("art", "seq"),
        split_axis=0,
        concat_axis=0,
        tiled=True,
    )
    every = every.reshape(chips, 2, articles, seqs, NC)
    needed = lax.dynamic_index_in_dim(
        lax.dynamic_index_in_dim(every, seq, 3, keepdims=False), core, 1, keepdims=False
    )
    order = jnp.array(ring, jnp.int32)
    spot = jnp.sum(jnp.where(order == chip, jnp.arange(chips), 0))
    needed = needed[jnp.array(ring)]
    needed = lax.dynamic_slice_in_dim(jnp.concatenate([needed, needed]), spot, chips)
    owners = needed // blocks
    here = owners // 2 == chip
    rank = jnp.cumsum(here.astype(jnp.int32), axis=-1) - 1
    counts = rank[..., -1] + 1
    entry = ((owners % 2 != core) * blocks + needed % blocks) * 128 + jnp.arange(NC)
    places = jnp.arange(NC)
    filled = jnp.sum(
        jnp.where(
            here[..., None, :] & (rank[..., None, :] == places[:, None]), entry[..., None, :], 0
        ),
        axis=-1,
    )
    lists = jnp.where(places < counts[..., None], filled, NC)

    def some(first, second, count, begin, j, k):
        ca, cb = counts[j][:count], counts[k][articles - count :]
        la, lb = lists[j][:count], lists[k][articles - count :]
        return score_chunks(
            first, second, count, begin, jnp.concatenate([ca, cb]), jnp.concatenate([la, lb]), catalog
        )

    scores = [None] * chips
    a, b = some(mine, mine, rows, rows, 0, 0)
    scores[0] = jnp.concatenate([a, b])
    for d in range(1, half):
        scores[chips - d], scores[d] = some(ahead[d], behind[d], articles, 0, chips - d, d)
    a, b = some(ahead[half], behind[half], rows, 0, half, half)
    scores[half] = jnp.concatenate([a, b])
    scores = jnp.stack(scores)
    scores = lax.dynamic_slice_in_dim(jnp.concatenate([scores, scores]), chips - spot, chips)
    back = [0] * chips
    for i, c in enumerate(ring):
        back[c] = i
    scores = scores[jnp.array(back)]
    scores = jnp.where(
        (jnp.arange(2) == core)[None, :, None, None], scores[:, None], 0.0
    ).reshape(arts * seqs, articles // seqs, NC)
    parts = lax.all_to_all(scores, ("art", "seq"), split_axis=0, concat_axis=0, tiled=True)
    parts = parts.reshape(arts, seqs, articles // seqs, NC).sum(0)
    score = parts.transpose(1, 0, 2).reshape(articles, NC)
    relevance = score - jnp.mean(score, axis=-1, keepdims=True)
    weights = jnp.exp(TEMPER * relevance)
    probs = weights / jnp.sum(weights, axis=-1, keepdims=True)
    return (relevance, probs)


def solution(mesh):
    arts, seqs = mesh.shape["art"], mesh.shape["seq"]
    chips = arts // 2
    wide = math.gcd(seqs, chips)
    deep = chips // wide
    ring = []
    for y in range(wide):
        for z in range(deep) if y % 2 == 0 else reversed(range(deep)):
            ring.append(z * wide + y)
    placed = (
        P("art", "seq", None, None),
        P(("art", "seq"), None, None),
        P(("art", "seq"), None, None),
        P("art", None, None),
    )
    return jax.shard_map(
        functools.partial(per_device, chips, tuple(ring)),
        mesh=mesh,
        in_specs=placed,
        out_specs=(P(("art", "seq"), None), P(("art", "seq"), None)),
        check_vma=False,
    )
```

time: 713 us -> 202 us (0.28)
  the two profiles are of different devices: /device:TPU:15 before, /device:TPU:0 now
where the time goes in v1:
time: 202 us; the launch traced here: 205 us
  Pallas kernels  99.1 us (49%)
  waiting for transfers between devices  37.1 us (18%)
  blocking collectives  21.2 us (10%)
  starting transfers between devices  15.6 us (8%)
  other arithmetic  15.2 us (8%)
  local copies, waits for them, and re-layouts  12.5 us (6%)
  between operations  4.52 us (2%)
    pallas_call x5, Pallas kernels, score_chunks(): pl.pallas_call(functools.partial(score_kernel, rows), out_shape=[jax.Shap...  84.8 us
    ppermute x3, waiting for transfers between devices, per_device(): ahead.append(lax.ppermute(ahead[-1], 'art', turn(1)))  27.8 us
    all_to_all x1, blocking collectives, per_device(): lax.all_to_all(scores, ('art', 'seq'), split_axis=0, concat_axis=0, tiled...  21.2 us
    pallas_call x1, Pallas kernels, unit_blocks(): pl.pallas_call(unit_kernel, out_shape=jax.ShapeDtypeStruct((2 * count, to...  14.4 us
    all_to_all x1, waiting for transfers between devices, per_device(): lax.all_to_all(jnp.broadcast_to(ids, (arts * seqs, articles, NC)), ('art'...  9.29 us
    unnamed x50, local copies, waits for them, and re-layouts  6.73 us
    all_to_all x1, starting transfers between devices, per_device(): lax.all_to_all(jnp.broadcast_to(ids, (arts * seqs, articles, NC)), ('art'...  6.27 us
  transfers between devices with their start and end apart: 10, of which 3 were waited for; matrix products, arithmetic and copies ran while one was open for 9% of the time, Pallas kernels for 43%

profile of v1, /device:TPU:0, one launch (start us, length us, event | category | flops | bytes accessed | tf_op | source)
XLA Modules:
  0.0 205.3 jit_solution(6271831063521286633)
XLA Ops:
  1.1 2.6 %collective-permute-start.1 = (bf16[12,256,128]{2,1,0:T(8,128)(2,1)}, bf16[12,256,128]{2,1,0:T(8,128)(2,1)S(1)}, u32[]{:S(2)}, u32[]{:S(2)}) collective-permute-start(bf16[12,256,128]{2,1,0:T(8,128)(2,1)} %bitcast.95), channel_id=1, source_target_pairs={{0,8},{2,10},{8,16},{10,18},{16,24},{18,26},{24,28},{26,30},{28,20... | collective-permute-start | bytes 2359304 | tf_op jit(solution)/shard_map/ppermute | solution.py:148
  5.6 6.3 %all-to-all-start = ((s32[32,1,768]{2,1,0:T(1,128)}), s32[32,1,768]{2,1,0:T(1,128)S(1)}, u32[]{:S(2)}, u32[]{:S(2)}) async-start(s32[32,1,768]{2,1,0:T(1,128)} %reshape.100), calls=%async_computation | async-start | bytes 196608 | tf_op jit(solution)/shard_map/all_to_all | solution.py:157
  11.9 1.3 fusion.12
  17.2 1.3 pad_clamp_fusion
  18.5 9.3 %all-to-all-done = s32[32,1,768]{2,1,0:T(1,128)S(1)} async-done(((s32[32,1,768]{2,1,0:T(1,128)}), s32[32,1,768]{2,1,0:T(1,128)S(1)}, u32[]{:S(2)}, u32[]{:S(2)}) %all-to-all-start) | async-done | bytes 98336 | tf_op jit(solution)/shard_map/all_to_all | solution.py:157
  28.3 0.9 reduce.16
  30.2 1.8 reduce_window_sum.11
  34.6 1.4 collective-permute-start.4
  36.6 1.7 select_reduce_fusion
  39.0 14.3 %collective-permute-done.3.first_ref = bf16[12,256,128]{2,1,0:T(8,128)(2,1)S(1)} collective-permute-done((bf16[12,256,128]{2,1,0:T(8,128)(2,1)S(1)}, bf16[12,256,128]{2,1,0:T(8,128)(2,1)S(1)}, u32[]{:S(2)}, u32[]{:S(2)}) %collective-permute-start.3) | collective-permute-done | bytes 786464 | tf_op jit(solution)/shard_map/ppermute | solution.py:148
  53.7 1.7 collective-permute-start.6
  55.4 0.9 copy-done.6
  58.7 13.6 %collective-permute-done.5.first_ref = bf16[12,256,128]{2,1,0:T(8,128)(2,1)S(1)} collective-permute-done((bf16[12,256,128]{2,1,0:T(8,128)(2,1)S(1)}, bf16[12,256,128]{2,1,0:T(8,128)(2,1)S(1)}, u32[]{:S(2)}, u32[]{:S(2)}) %collective-permute-start.5) | collective-permute-done | bytes 786464 | tf_op jit(solution)/shard_map/ppermute | solution.py:148
  72.3 0.8 slice.212
  73.1 0.8 slice.213
  73.9 2.0 collective-permute-start.8
  75.9 14.4 %unit_blocks.1.catalog_ref = bf16[512,64,128]{2,1,0:T(8,128)(2,1)} custom-call(bf16[256,64,128]{2,1,0:T(8,128)(2,1)} %own_ref.1, bf16[256,64,128]{2,1,0:T(8,128)(2,1)} %collective-permute-done.other_ref), custom_call_target="tpu_custom_call" | custom-call | flops 8388608 | bytes 16777216 | tf_op jit(solution)/shard_map/unit_blocks/pallas_call | solution.py:41
  90.3 3.4 %copy-done = bf16[512,64,128]{2,1,0:T(8,128)(2,1)S(1)} copy-done((bf16[512,64,128]{2,1,0:T(8,128)(2,1)S(1)}, bf16[512,64,128]{2,1,0:T(8,128)(2,1)}, u32[]{:S(2)}) %copy-start) | copy-done | bytes 8388632
  95.0 10.6 %score_chunks.5 = (f32[6,8,64]{2,1,0:T(8,128)S(1)}, f32[6,8,64]{2,1,0:T(8,128)S(1)}) custom-call(s32[12]{0:T(128)S(1)} %copy-done.12, s32[12,64]{1,0:T(8,128)S(1)} %copy-done.11, bf16[12,256,128]{2,1,0:T(8,128)(2,1)S(1)} %bitcast.97, bf16[12,256,128]{2,1,0:T(8,128)(2,1)S(1)} %bitcast.98, bf16[512,64,128]{2,1,0:T(8,128)(2,1)S(1)} %copy-done), custom_call_target="tpu_custom_call" | custom-call | flops 402653184 | bytes 8388608 | tf_op jit(solution)/shard_map/score_chunks/pallas_call | solution.py:104
  105.7 20.2 %score_chunks.6 = (f32[12,8,64]{2,1,0:T(8,128)S(1)}, f32[12,8,64]{2,1,0:T(8,128)S(1)}) custom-call(s32[24]{0:T(128)S(1)} %copy-done.13, s32[24,64]{1,0:T(8,128)S(1)} %copy-done.9, bf16[12,256,128]{2,1,0:T(8,128)(2,1)S(1)} %collective-permute-done.1.first_ref, bf16[12,256,128]{2,1,0:T(8,128)(2,1)S(1)} %copy-done.3, bf16[512,64,128]{2,1,0:T(8,128)(2,1)S(1)} %copy-done), custom_call_target="tpu_custom_call" | custom-call | flops 805306368 | bytes 8388608 | tf_op jit(solution)/shard_map/score_chunks/pallas_call | solution.py:104
  126.0 21.3 %score_chunks.7 = (f32[12,8,64]{2,1,0:T(8,128)S(1)}, f32[12,8,64]{2,1,0:T(8,128)S(1)}) custom-call(s32[24]{0:T(128)S(1)} %pad_add_fusion.7.count_ref, s32[24,64]{1,0:T(8,128)S(1)} %copy-done.8, bf16[12,256,128]{2,1,0:T(8,128)(2,1)S(1)} %copy-done.5, bf16[12,256,128]{2,1,0:T(8,128)(2,1)S(1)} %copy-done.7, bf16[512,64,128]{2,1,0:T(8,128)(2,1)S(1)} %copy-done), custom_call_target="tpu_custom_call" | custom-call | flops 805306368 | bytes 8388608 | tf_op jit(solution)/shard_map/score_chunks/pallas_call | solution.py:104
  147.4 21.1 %score_chunks.8 = (f32[12,8,64]{2,1,0:T(8,128)S(1)}, f32[12,8,64]{2,1,0:T(8,128)S(1)}) custom-call(s32[24]{0:T(128)S(1)} %copy-done.14, s32[24,64]{1,0:T(8,128)S(1)} %pad_add_fusion.2.list_ref, bf16[12,256,128]{2,1,0:T(8,128)(2,1)S(1)} %collective-permute-done.5.first_ref, bf16[12,256,128]{2,1,0:T(8,128)(2,1)S(1)} %collective-permute-done.6.second_ref, ...), custom_call_target="tpu_custom_call" | custom-call | flops 805306368 | bytes 8388608 | tf_op jit(solution)/shard_map/score_chunks/pallas_call | solution.py:104
  168.6 11.5 %score_chunks.9 = (f32[6,8,64]{2,1,0:T(8,128)S(1)}, f32[6,8,64]{2,1,0:T(8,128)S(1)}) custom-call(s32[12]{0:T(128)S(1)} %copy-done.15, s32[12,64]{1,0:T(8,128)S(1)} %copy-done.10, bf16[6,256,128]{2,1,0:T(8,128)(2,1)S(1)} %collective-permute-done.7.first_ref, bf16[6,256,128]{2,1,0:T(8,128)(2,1)} %collective-permute-done.8.second_ref, ...), custom_call_target="tpu_custom_call" | custom-call | flops 402653184 | bytes 8388608 | tf_op jit(solution)/shard_map/score_chunks/pallas_call | solution.py:104
  181.4 21.2 %all_to_all.10 = f32[32,1,384]{2,1,0:T(1,128)S(1)} all-to-all(f32[32,1,384]{2,1,0:T(1,128)S(1)} %reshape.102), channel_id=1, replica_groups=mesh['art'=16,'seq'=2] {'art','seq'}, dimensions={0} | all-to-all | bytes 98304 | tf_op jit(solution)/shard_map/all_to_all | solution.py:209
  (127 shorter events, 16.6 us)
Async XLA Ops:
  0.6 75.3 %collective-permute-start = (bf16[256,64,128]{2,1,0:T(8,128)(2,1)}, bf16[256,64,128]{2,1,0:T(8,128)(2,1)}, u32[]{:S(2)}, u32[]{:S(2)}) collective-permute-start(bf16[256,64,128]{2,1,0:T(8,128)(2,1)} %own_ref.1), channel_id=1, source_target_pairs={{0,2},{2,0},{4,6},{6,4},{8,10},{10,8},{12,14},{14,12},{16,18},{18,... | collective-permute-start | bytes 12582920 | tf_op jit(solution)/shard_map/ppermute | solution.py:153
  1.1 32.8 %collective-permute-start.1 = (bf16[12,256,128]{2,1,0:T(8,128)(2,1)}, bf16[12,256,128]{2,1,0:T(8,128)(2,1)S(1)}, u32[]{:S(2)}, u32[]{:S(2)}) collective-permute-start(bf16[12,256,128]{2,1,0:T(8,128)(2,1)} %bitcast.95), channel_id=1, source_target_pairs={{0,8},{2,10},{8,16},{10,18},{16,24},{18,26},{24,28},{26,30},{28,20... | collective-permute-start | bytes 2359304 | tf_op jit(solution)/shard_map/ppermute | solution.py:148
  3.8 30.8 %collective-permute-start.2 = (bf16[12,256,128]{2,1,0:T(8,128)(2,1)}, bf16[12,256,128]{2,1,0:T(8,128)(2,1)S(1)}, u32[]{:S(2)}, u32[]{:S(2)}) collective-permute-start(bf16[12,256,128]{2,1,0:T(8,128)(2,1)} %bitcast.96), channel_id=1, source_target_pairs={{0,4},{2,6},{8,0},{10,2},{16,8},{18,10},{24,16},{26,18},{28,24},{3... | collective-permute-start | bytes 2359304 | tf_op jit(solution)/shard_map/ppermute | solution.py:149
  5.6 22.2 %all-to-all-start = ((s32[32,1,768]{2,1,0:T(1,128)}), s32[32,1,768]{2,1,0:T(1,128)S(1)}, u32[]{:S(2)}, u32[]{:S(2)}) async-start(s32[32,1,768]{2,1,0:T(1,128)} %reshape.100), calls=%async_computation | async-start | bytes 196608 | tf_op jit(solution)/shard_map/all_to_all | solution.py:157
  33.9 19.4 %collective-permute-start.3 = (bf16[12,256,128]{2,1,0:T(8,128)(2,1)S(1)}, bf16[12,256,128]{2,1,0:T(8,128)(2,1)S(1)}, u32[]{:S(2)}, u32[]{:S(2)}) collective-permute-start(bf16[12,256,128]{2,1,0:T(8,128)(2,1)S(1)} %collective-permute-done.1.first_ref), channel_id=1, source_target_pairs={{0,8},{2,10},{8,16},{10,18},{16,24},{18,26},{24,28},{26,30},{28,20... | collective-permute-start | bytes 2359304 | tf_op jit(solution)/shard_map/ppermute | solution.py:148
  34.6 38.5 %copy-start.2 = (bf16[12,256,128]{2,1,0:T(8,128)(2,1)}, bf16[12,256,128]{2,1,0:T(8,128)(2,1)S(1)}, u32[]{:S(2)}) copy-start(bf16[12,256,128]{2,1,0:T(8,128)(2,1)S(1)} %collective-permute-done.2.second_ref) | copy-start | bytes 2359300
  34.6 19.1 %collective-permute-start.4 = (bf16[12,256,128]{2,1,0:T(8,128)(2,1)S(1)}, bf16[12,256,128]{2,1,0:T(8,128)(2,1)S(1)}, u32[]{:S(2)}, u32[]{:S(2)}) collective-permute-start(bf16[12,256,128]{2,1,0:T(8,128)(2,1)S(1)} %collective-permute-done.2.second_ref), channel_id=1, source_target_pairs={{0,4},{2,6},{8,0},{10,2},{16,8},{18,10},{24,16},{26,18},{28,24},{3... | collective-permute-start | bytes 2359304 | tf_op jit(solution)/shard_map/ppermute | solution.py:149
  53.3 20.5 %copy-start.4 = (bf16[12,256,128]{2,1,0:T(8,128)(2,1)}, bf16[12,256,128]{2,1,0:T(8,128)(2,1)S(1)}, u32[]{:S(2)}) copy-start(bf16[12,256,128]{2,1,0:T(8,128)(2,1)S(1)} %collective-permute-done.3.first_ref) | copy-start | bytes 2359300
  53.3 19.0 %collective-permute-start.5 = (bf16[12,256,128]{2,1,0:T(8,128)(2,1)S(1)}, bf16[12,256,128]{2,1,0:T(8,128)(2,1)S(1)}, u32[]{:S(2)}, u32[]{:S(2)}) collective-permute-start(bf16[12,256,128]{2,1,0:T(8,128)(2,1)S(1)} %collective-permute-done.3.first_ref), channel_id=1, source_target_pairs={{0,8},{2,10},{8,16},{10,18},{16,24},{18,26},{24,28},{26,30},{28,20... | collective-permute-start | bytes 2359304 | tf_op jit(solution)/shard_map/ppermute | solution.py:148
  53.7 19.4 %collective-permute-start.6 = (bf16[12,256,128]{2,1,0:T(8,128)(2,1)S(1)}, bf16[12,256,128]{2,1,0:T(8,128)(2,1)S(1)}, u32[]{:S(2)}, u32[]{:S(2)}) collective-permute-start(bf16[12,256,128]{2,1,0:T(8,128)(2,1)S(1)} %collective-permute-done.4.second_ref), channel_id=1, source_target_pairs={{0,4},{2,6},{8,0},{10,2},{16,8},{18,10},{24,16},{26,18},{28,24},{3... | collective-permute-start | bytes 2359304 | tf_op jit(solution)/shard_map/ppermute | solution.py:149
  73.1 95.5 %collective-permute-start.7 = (bf16[6,256,128]{2,1,0:T(8,128)(2,1)}, bf16[6,256,128]{2,1,0:T(8,128)(2,1)S(1)}, u32[]{:S(2)}, u32[]{:S(2)}) collective-permute-start(bf16[6,256,128]{2,1,0:T(8,128)(2,1)} %slice.212), channel_id=1, source_target_pairs={{0,8},{2,10},{8,16},{10,18},{16,24},{18,26},{24,28},{26,30},{28,20... | collective-permute-start | bytes 1179656 | tf_op jit(solution)/shard_map/ppermute | solution.py:150
  73.9 16.4 %copy-start.1 = (bf16[12,1,256,128]{3,2,1,0:T(8,128)(2,1)S(1)}, bf16[12,1,256,128]{3,2,1,0:T(8,128)(2,1)}, u32[]{:S(2)}) copy-start(bf16[12,1,256,128]{3,2,1,0:T(8,128)(2,1)} %param.7) | copy-start | bytes 2359300
  73.9 94.7 %collective-permute-start.8 = (bf16[6,256,128]{2,1,0:T(8,128)(2,1)}, bf16[6,256,128]{2,1,0:T(8,128)(2,1)}, u32[]{:S(2)}, u32[]{:S(2)}) collective-permute-start(bf16[6,256,128]{2,1,0:T(8,128)(2,1)} %slice.213), channel_id=1, source_target_pairs={{0,4},{2,6},{8,0},{10,2},{16,8},{18,10},{24,16},{26,18},{28,24},{3... | collective-permute-start | bytes 1179656 | tf_op jit(solution)/shard_map/ppermute | solution.py:151
  90.3 3.4 %copy-start = (bf16[512,64,128]{2,1,0:T(8,128)(2,1)S(1)}, bf16[512,64,128]{2,1,0:T(8,128)(2,1)}, u32[]{:S(2)}) copy-start(bf16[512,64,128]{2,1,0:T(8,128)(2,1)} %unit_blocks.1.catalog_ref) | copy-start | bytes 25165828
  95.0 10.7 %copy-start.3 = (bf16[12,256,128]{2,1,0:T(8,128)(2,1)S(1)}, bf16[12,256,128]{2,1,0:T(8,128)(2,1)}, u32[]{:S(2)}) copy-start(bf16[12,256,128]{2,1,0:T(8,128)(2,1)} %copy-done.2) | copy-start | bytes 2359300
  95.0 10.7 %copy-start.9 = (s32[24,64]{1,0:T(8,128)S(1)}, s32[24,64]{1,0:T(8,128)}, u32[]{:S(2)}) copy-start(s32[24,64]{1,0:T(8,128)} %pad_add_fusion.list_ref) | copy-start | bytes 18436
  95.0 10.7 %copy-start.13 = (s32[24]{0:T(128)S(1)}, s32[24]{0:T(128)}, u32[]{:S(2)}) copy-start(s32[24]{0:T(128)} %pad_add_fusion.6.count_ref) | copy-start | bytes 292
  105.7 20.3 %copy-start.5 = (bf16[12,256,128]{2,1,0:T(8,128)(2,1)S(1)}, bf16[12,256,128]{2,1,0:T(8,128)(2,1)}, u32[]{:S(2)}) copy-start(bf16[12,256,128]{2,1,0:T(8,128)(2,1)} %copy-done.4) | copy-start | bytes 2359300
  105.7 20.3 %copy-start.7 = (bf16[12,256,128]{2,1,0:T(8,128)(2,1)S(1)}, bf16[12,256,128]{2,1,0:T(8,128)(2,1)}, u32[]{:S(2)}) copy-start(bf16[12,256,128]{2,1,0:T(8,128)(2,1)} %copy-done.6) | copy-start | bytes 2359300
  105.7 20.3 %copy-start.8 = (s32[24,64]{1,0:T(8,128)S(1)}, s32[24,64]{1,0:T(8,128)}, u32[]{:S(2)}) copy-start(s32[24,64]{1,0:T(8,128)} %pad_add_fusion.1.list_ref) | copy-start | bytes 18436
  126.0 21.4 %copy-start.14 = (s32[24]{0:T(128)S(1)}, s32[24]{0:T(128)}, u32[]{:S(2)}) copy-start(s32[24]{0:T(128)} %pad_add_fusion.8.count_ref) | copy-start | bytes 292
  147.4 21.2 %copy-start.10 = (s32[12,64]{1,0:T(8,128)S(1)}, s32[12,64]{1,0:T(8,128)}, u32[]{:S(2)}) copy-start(s32[12,64]{1,0:T(8,128)} %pad_add_fusion.4.list_ref) | copy-start | bytes 9220
  147.4 21.2 %copy-start.15 = (s32[12]{0:T(128)S(1)}, s32[12]{0:T(128)}, u32[]{:S(2)}) copy-start(s32[12]{0:T(128)} %pad_add_fusion.9.count_ref) | copy-start | bytes 148
  168.6 12.6 %copy-start.16 = (pred[32,6]{1,0:T(8,128)(4,1)S(1)}, pred[32,6]{1,0:T(8,128)(4,1)}, u32[]{:S(2)}) copy-start(pred[32,6]{1,0:T(8,128)(4,1)} %broadcast_in_dim.68) | copy-start | bytes 580
  (3 other events, 2.2 us)

commit v2 on v0

v2 whole, which is shorter than its diff:
```python
import functools
import math

import jax
import jax.numpy as jnp
from jax import lax
from jax.experimental import pallas as pl
from jax.experimental.pallas import tpu as pltpu
from jax.sharding import PartitionSpec as P

NC = 64
EPS = 1e-06
SHARP = 16.0
TEMPER = 4.0
GROUP = 4
UNROLL = 12
LAST = (((1,), (1,)), ((), ()))


def unit_kernel(blocks_ref, out_ref):
    count, tokens, width = blocks_ref.shape

    def some(i, carry):
        wide = blocks_ref[pl.ds(2 * i, 2)].astype(jnp.float32)
        norm = jnp.sum(wide * wide, axis=-1, keepdims=True)
        out_ref[pl.ds(2 * i, 2)] = (wide * lax.rsqrt(norm + EPS)).astype(jnp.bfloat16)
        return carry

    lax.fori_loop(0, count // 2, some, 0, unroll=16)


def unit_blocks(blocks):
    return pl.pallas_call(
        unit_kernel,
        out_shape=jax.ShapeDtypeStruct(blocks.shape, jnp.bfloat16),
        in_specs=[pl.BlockSpec(memory_space=pltpu.VMEM)],
        out_specs=pl.BlockSpec(memory_space=pltpu.VMEM),
        compiler_params=pltpu.CompilerParams(vmem_limit_bytes=32 * 1024 * 1024),
        cost_estimate=pl.CostEstimate(flops=1, bytes_accessed=1, transcendentals=0),
        name="unit_blocks",
    )(blocks)


def mask(m):
    return m.astype(jnp.float32).astype(jnp.bfloat16)


def plan_rows(chips, articles):
    entries = -(-(articles * NC + chips * articles * (GROUP - 1)) // 128)
    return entries, -(-(3 * entries + 1) // 16) * 16


def pack_kernel(chips, blocks, me_ref, *refs):
    id_refs, query_ref, out_ref = refs[:-2], refs[-2], refs[-1]
    seqs = len(id_refs)
    core, seq = me_ref[1], me_ref[2]
    per_home, width = id_refs[0].shape
    rows = query_ref.shape[0]
    out_ref[0:rows, :] = query_ref[...]

    lane = lax.broadcasted_iota(jnp.int32, (per_home, width), 1)
    ids = jnp.zeros((per_home, width), jnp.int32)
    for d in range(seqs):
        table = id_refs[d][...]
        for p in range(seqs):
            k = (p + seqs - d) % seqs
            turned = table if k == p else pltpu.roll(table, (k - p) % seqs * NC, 1)
            ids = jnp.where((seq == p) & (lane // NC == k), turned, ids)
    ids = jnp.concatenate([ids[i : i + 1] for i in range(per_home)], axis=1)
    lanes = per_home * width
    articles = lanes // NC
    owner, local = ids // blocks, ids % blocks
    other = jnp.where(owner % 2 != core, 1, 0)
    here = owner // 2 == lax.broadcasted_iota(jnp.int32, (chips, lanes), 0)
    hot = mask(here)
    a = lax.broadcasted_iota(jnp.int32, (lanes, lanes), 0)
    b = lax.broadcasted_iota(jnp.int32, (lanes, lanes), 1)
    same = a // NC == b // NC
    rank = jnp.dot(hot, mask(same & (a <= b)), preferred_element_type=jnp.float32)
    amount = jnp.dot(hot, mask(same), preferred_element_type=jnp.float32).astype(jnp.int32)
    groups = (amount + (GROUP - 1)) // GROUP
    lead = lax.broadcasted_iota(jnp.int32, (chips, lanes), 1) % NC == 0
    tops = jnp.where(lead, groups, 0).astype(jnp.float32)
    ahead = jnp.dot(
        tops.astype(jnp.bfloat16), mask(a // NC < b // NC), preferred_element_type=jnp.float32
    )
    totals = jnp.sum(tops, axis=1, keepdims=True)
    lane = lax.broadcasted_iota(jnp.int32, (chips, 128), 1)
    before = lax.broadcasted_iota(jnp.int32, (chips, 128), 0) < lane % NC
    starts = jnp.sum(jnp.where(before, totals, 0.0), axis=0, keepdims=True).astype(jnp.int32)
    starts = jnp.where(lane[0:1] < NC, starts // 16, starts % 16).astype(jnp.float32)
    fence = mask(
        lax.broadcasted_iota(jnp.int32, (chips, chips), 1)
        < lax.broadcasted_iota(jnp.int32, (chips, chips), 0)
    )
    base = jnp.dot(fence, tops.astype(jnp.bfloat16), preferred_element_type=jnp.float32)
    base = jnp.sum(base, axis=1, keepdims=True)
    spot = jnp.where(here, GROUP * (base + ahead) + rank - 1.0, 0.0)
    spot = jnp.sum(spot, axis=0, keepdims=True).astype(jnp.int32)
    lane = lax.broadcasted_iota(jnp.int32, (1, lanes), 1)
    article = lane // NC % seqs * per_home + lane // width
    kinds = lax.broadcasted_iota(jnp.int32, (8, lanes), 0)
    fields = jnp.ones((8, lanes), jnp.int32)
    for k, row in enumerate((local, other * 128 + lane % NC, article)):
        fields = jnp.where(kinds == k, row, fields)
    entries, extra = plan_rows(chips, articles)
    slots = lax.broadcasted_iota(jnp.int32, (entries * 128, lanes), 0)
    got = lax.dot_general(
        fields.astype(jnp.float32).astype(jnp.bfloat16),
        mask(slots == spot),
        LAST,
        preferred_element_type=jnp.float32,
    )
    code = jnp.where(got[3:4] > 0.5, got[1:2], float(NC))
    lists = jnp.concatenate([got[0:1], code, got[2:3]], axis=1)
    lists = [lists[:, i * 128 : (i + 1) * 128] for i in range(3 * entries)]
    lists += [starts, jnp.zeros((extra - 3 * entries - 1, 128), jnp.float32)]
    out_ref[rows : rows + extra, :] = jnp.concatenate(lists, axis=0).astype(jnp.bfloat16)


def pack_stream(me, ids, query, chips, blocks):
    vmem = pl.BlockSpec(memory_space=pltpu.VMEM)
    articles = len(ids) * ids[0].shape[0]
    rows = query.shape[0] + plan_rows(chips, articles)[1]
    return pl.pallas_call(
        functools.partial(pack_kernel, chips, blocks),
        out_shape=jax.ShapeDtypeStruct((rows, query.shape[1]), jnp.bfloat16),
        in_specs=[pl.BlockSpec(memory_space=pltpu.SMEM)] + [vmem] * (len(ids) + 1),
        out_specs=vmem,
        compiler_params=pltpu.CompilerParams(vmem_limit_bytes=32 * 1024 * 1024),
        cost_estimate=pl.CostEstimate(flops=1, bytes_accessed=1, transcendentals=0),
        name="pack_stream",
    )(me, *ids, query)


def score_kernel(dims, me_ref, *refs):
    plans, others, seqs, blocks, wide, deep = dims
    chips = wide * deep
    pair_refs, refs = refs[: 2 * plans], refs[2 * plans :]
    other_refs, refs = refs[:others], refs[others:]
    own_ref, other_ref, *refs = refs
    out_refs = refs[:-6]
    turned_ref, scale_ref, mass_ref, words_ref, lists_ref, sems = refs[-6:]
    articles = turned_ref.shape[0] // plans
    tokens = mass_ref.shape[1]
    keys = own_ref.shape[1]
    half = mass_ref.shape[0] // plans
    entries, extra = plan_rows(chips, articles)
    bits = (2 * blocks - 1).bit_length()
    begin = articles // 2 * tokens

    copies = []
    for p in range(plans):
        rows = pair_refs[2 * p + 1][begin : begin + extra, :].astype(jnp.float32).astype(jnp.int32)
        local, code, article, starts = (rows[k * entries : (k + 1) * entries] for k in range(4))
        place = code % 128
        row = jnp.where(place < NC, article * NC + place, articles * NC)
        word = local + blocks * (code // 128) + 2 * blocks * row + (1 << 20) * article
        words_ref[p, 0:entries, :] = word
        words_ref[p, entries : entries + 1, :] = starts[0:1]
        copy = pltpu.make_async_copy(words_ref.at[p], lists_ref.at[p], sems.at[p])
        copy.start()
        copies.append(copy)

    for p, ref in enumerate(pair_refs):

        def prepare(i, carry, p=p, ref=ref):
            query = ref[pl.ds(pl.multiple_of(i * tokens, tokens), tokens), :]
            wide = query.astype(jnp.float32)
            norm = lax.dot_general(
                jnp.ones((8, query.shape[1]), jnp.bfloat16),
                (wide * wide).astype(jnp.bfloat16),
                LAST,
                preferred_element_type=jnp.float32,
            )
            at = p * (articles // 2) + i
            scale_ref[at] = lax.rsqrt(norm + EPS) * (SHARP * math.log2(math.e))
            turned_ref[at] = query.T
            return carry

        lax.fori_loop(0, articles // 2, prepare, 0, unroll=2)
    mass_ref[...] = jnp.ones_like(mass_ref)
    for copy in copies:
        copy.wait()

    chip = me_ref[0]
    begins = []
    counts = []
    for p in range(plans):
        low = lists_ref[p, entries, chip] * 16 + lists_ref[p, entries, NC + chip]
        high = lists_ref[p, entries, chip + 1] * 16 + lists_ref[p, entries, NC + chip + 1]
        begins.append(low)
        counts.append(high - low)
    total = sum(counts)

    def task(k):
        k = jnp.minimum(k, total - 1)
        if plans == 1:
            late, at = 0, (k + begins[0]) * GROUP
        else:
            late = (k >= counts[0]).astype(jnp.int32)
            at = (k + begins[0] + late * (begins[1] - begins[0] - counts[0])) * GROUP
        at = jnp.maximum(at, 0)
        line, spot = lax.shift_right_logical(at, 7), at & 127
        words = [lists_ref[late, line, spot + g] for g in range(GROUP)]
        article = lax.shift_right_logical(words[0], 20) + late * articles
        rows = [(lax.shift_right_logical(w, bits) & 2047) + late * half for w in words]
        return article, [w & (2 * blocks - 1) for w in words], rows

    def block(c):
        spot = c & (blocks - 1)
        return jnp.where(c >= blocks, other_ref[spot], own_ref[spot])

    def some(step, carry):
        for u in range(UNROLL):
            article, picks, rows = task(step * UNROLL + u)
            chosen = jnp.concatenate([block(c) for c in picks], axis=0)
            sims = jnp.dot(chosen, turned_ref[article], preferred_element_type=jnp.float32)
            grown = jnp.exp2(sims * scale_ref[article][0:1])
            for g, row in enumerate(rows):
                mass_ref[pl.ds(row, 1), :] = jnp.sum(
                    grown[g * keys : (g + 1) * keys], axis=0, keepdims=True
                )
        return carry

    lax.fori_loop(0, (total + UNROLL - 1) // UNROLL, some, 0)

    per_home = articles // seqs
    ones = jnp.ones((8, tokens), jnp.bfloat16)
    for p in range(plans):
        for i in range(articles):
            logs = jnp.log2(mass_ref[p * half + i * NC : p * half + (i + 1) * NC, :])
            high = logs.astype(jnp.bfloat16)
            low = (logs - high.astype(jnp.float32)).astype(jnp.bfloat16)
            sums = lax.dot_general(
                ones, high, LAST, preferred_element_type=jnp.float32
            ) + lax.dot_general(ones, low, LAST, preferred_element_type=jnp.float32)
            out_refs[p][i : i + 1, 0:NC] = sums[0:1] * (math.log(2) / SHARP)
    if not others:
        return

    spread_ref = out_refs[-1]
    spread_ref[...] = jnp.zeros_like(spread_ref)
    block_rows = spread_ref.shape[0] // (2 * chips * seqs)
    side, rest = chip & (wide - 1), chip >> (wide.bit_length() - 1)
    place = side * deep + jnp.where(side & 1 == 0, rest, deep - 1 - rest)
    spots = [0] + [x for d in range(1, chips // 2) for x in (-d, d)] + [chips // 2]
    for spot, ref in zip(spots, [*other_refs, out_refs[0]]):
        at = (place + spot + chips) & (chips - 1)
        side, rest = at >> (deep.bit_length() - 1), at & (deep - 1)
        home = jnp.where(side & 1 == 0, rest, deep - 1 - rest) * wide + side
        for k in range(seqs):
            peer = (2 * home + me_ref[1]) * seqs + k
            rows = pl.ds(pl.multiple_of(peer * block_rows, 8), per_home)
            spread_ref[rows, :] = ref[k * per_home : (k + 1) * per_home, :]


def score_chunks(me, pairs, others, own, other, tokens, wide, deep, seqs):
    chips = wide * deep
    plans = len(pairs)
    blocks, keys, width = own.shape
    articles = 2 * pairs[0][0].shape[0] // tokens
    shapes = [jax.ShapeDtypeStruct((articles, 128), jnp.float32)] * plans
    if others:
        rows = -(-(articles // seqs) // 8) * 8 * 2 * chips * seqs
        shapes.append(jax.ShapeDtypeStruct((rows, 128), jnp.float32))
    lines = -(-(plan_rows(chips, articles)[0] + 1) // 8) * 8
    work = plans * articles * 8
    smem, vmem = pl.BlockSpec(memory_space=pltpu.SMEM), pl.BlockSpec(memory_space=pltpu.VMEM)
    return pl.pallas_call(
        functools.partial(score_kernel, (plans, len(others), seqs, blocks, wide, deep)),
        out_shape=shapes,
        in_specs=[smem] + [vmem] * (2 * plans + len(others) + 2),
        out_specs=[vmem] * len(shapes),
        scratch_shapes=[
            pltpu.VMEM((plans * articles, width, tokens), jnp.bfloat16),
            pltpu.VMEM((plans * articles, 8, tokens), jnp.float32),
            pltpu.VMEM((plans * (articles * NC + 8), tokens), jnp.float32),
            pltpu.VMEM((plans, lines, 128), jnp.int32),
            pltpu.SMEM((plans, lines, 128), jnp.int32),
            pltpu.SemaphoreType.DMA((plans,)),
        ],
        compiler_params=pltpu.CompilerParams(vmem_limit_bytes=32 * 1024 * 1024),
        cost_estimate=pl.CostEstimate(
            flops=2 * work * tokens * keys * width,
            bytes_accessed=4 * own.size,
            transcendentals=work * tokens * keys,
        ),
        name="score_chunks",
    )(me, *[x for pair in pairs for x in pair], *others, own, other)


def close_kernel(seqs, parts_ref, relevance_ref, probs_ref, score_ref):
    peers = parts_ref.shape[0]
    rows = relevance_ref.shape[0] // seqs
    for d in range(seqs):
        part = parts_ref[d]
        for j in range(d + seqs, peers, seqs):
            part = part + parts_ref[j]
        for i in range(rows):
            score_ref[i * seqs + d : i * seqs + d + 1, :] = part[i : i + 1]
    score = score_ref[:, 0:NC]
    relevance = score - jnp.mean(score, axis=-1, keepdims=True)
    weights = jnp.exp(TEMPER * relevance)
    relevance_ref[...] = relevance
    probs_ref[...] = weights / jnp.sum(weights, axis=-1, keepdims=True)


def close(parts, articles, seqs):
    vmem = pl.BlockSpec(memory_space=pltpu.VMEM)
    return pl.pallas_call(
        functools.partial(close_kernel, seqs),
        out_shape=[jax.ShapeDtypeStruct((articles, NC), jnp.float32)] * 2,
        in_specs=[vmem],
        out_specs=[vmem] * 2,
        scratch_shapes=[pltpu.VMEM((articles, 128), jnp.float32)],
        name="close",
    )(parts)


def per_device(wide, deep, queries, cand_owner, cand_local, companies):
    articles = queries.shape[0]
    seqs, arts = lax.axis_size("seq"), lax.axis_size("art")
    art, seq = lax.axis_index("art"), lax.axis_index("seq")
    chips = wide * deep
    half = chips // 2
    per_home = articles // seqs
    blocks = companies.shape[0]
    tokens = queries.shape[2]
    mine = queries.reshape(articles * tokens, queries.shape[3])
    ring = []
    for y in range(wide):
        for z in range(deep) if y % 2 == 0 else reversed(range(deep)):
            ring.append(z * wide + y)

    def turn(step, across=0):
        return [
            (
                (2 * ring[i] + c) * seqs + s,
                (2 * ring[(i + step) % chips] + c) * seqs + (s + across) % seqs,
            )
            for i in range(chips)
            for c in range(2)
            for s in range(seqs)
        ]

    def send(array, step, across=0):
        return lax.ppermute(array, ("art", "seq"), turn(step, across))

    cut = articles // 2 * tokens
    one = mine[:cut]
    ahead, behind = [[one, None]], [[one, None]]
    first = [send(one, 1), send(one, -1)]

    ids = (cand_owner * blocks + cand_local).reshape(per_home, seqs * NC)
    ids = [ids] + [send(ids, 0, d) for d in range(1, seqs)]
    me = jnp.stack([art // 2, art % 2, seq]).astype(jnp.int32)
    two = pack_stream(me, ids, mine[cut:], chips, blocks)
    second = [send(two, 1), send(two, -1)]
    ahead.append([first[0], second[0]])
    behind.append([first[1], second[1]])
    own = unit_blocks(companies)
    other = unit_blocks(lax.ppermute(companies, "art", [(i, i ^ 1) for i in range(arts)]))

    def score(*pairs, others=()):
        return score_chunks(me, pairs, others, own, other, tokens, wide, deep, seqs)

    done = score((one, two))
    early = list(done)
    for d in range(1, half):
        for side in (ahead, behind):
            side[d] = [lax.optimization_barrier((x, done[0]))[0] for x in side[d]]
        if d + 1 < half:
            ahead.append([send(x, 1) for x in ahead[d]])
            behind.append([send(x, -1) for x in behind[d]])
        else:
            last = (send(ahead[d][0], 1), send(behind[d][1], -1))
        done = score(ahead[d], behind[d])
        early += done
    spread = score(last, others=early)[1]
    parts = lax.all_to_all(spread, ("art", "seq"), split_axis=0, concat_axis=0, tiled=True)
    return tuple(close(parts.reshape(arts * seqs, -1, 128), articles, seqs))


def solution(mesh):
    chips = mesh.shape["art"] // 2
    wide = math.gcd(mesh.shape["seq"], chips)
    placed = (
        P("art", "seq", None, None),
        P(("art", "seq"), None, None),
        P(("art", "seq"), None, None),
        P("art", None, None),
    )
    return jax.shard_map(
        functools.partial(per_device, wide, chips // wide),
        mesh=mesh,
        in_specs=placed,
        out_specs=(P(("art", "seq"), None), P(("art", "seq"), None)),
        check_vma=False,
    )
```

time: 713 us -> 93.5 us (0.13)
  the two profiles are of different devices: /device:TPU:15 before, /device:TPU:0 now
where the time goes in v2:
time: 93.5 us; the launch traced here: 92.8 us
  Pallas kernels  39.8 us (43%)
  starting transfers between devices  17.3 us (19%)
  waiting for transfers between devices  16 us (17%)
  blocking collectives  14.5 us (16%)
  local copies, waits for them, and re-layouts  3.61 us (4%)
    pallas_call x5, Pallas kernels, score_chunks(): pl.pallas_call(functools.partial(score_kernel, (plans, len(others), seqs,...  28.4 us
    ppermute x15, starting transfers between devices, send(): return lax.ppermute(array, ('art', 'seq'), turn(step, across))  16.8 us
    ppermute x15, waiting for transfers between devices, send(): return lax.ppermute(array, ('art', 'seq'), turn(step, across))  16 us
    all_to_all x1, blocking collectives, per_device(): lax.all_to_all(spread, ('art', 'seq'), split_axis=0, concat_axis=0, tiled...  14.5 us
    pallas_call x2, Pallas kernels, unit_blocks(): pl.pallas_call(unit_kernel, out_shape=jax.ShapeDtypeStruct(blocks.shape,...  7.86 us
    unnamed x2, local copies, waits for them, and re-layouts  2.19 us
  transfers between devices with their start and end apart: 16, of which 7 were waited for; matrix products, arithmetic and copies ran while one was open for 2% of the time, Pallas kernels for 36%

profile of v2, /device:TPU:0, one launch (start us, length us, event | category | flops | bytes accessed | tf_op | source)
XLA Modules:
  0.0 92.8 jit_solution(13935858793216890131)
XLA Ops:
  2.2 2.6 %collective-permute-start.1 = (s32[6,128]{1,0:T(8,128)S(1)}, s32[6,128]{1,0:T(8,128)S(1)}, u32[]{:S(2)}, u32[]{:S(2)}) collective-permute-start(s32[6,128]{1,0:T(8,128)S(1)} %reshape.14.refs_0_), channel_id=1, source_target_pairs={{0,1},{1,0},{2,3},{3,2},{8,9},{9,8},{10,11},{11,10},{16,17},{17,16... | collective-permute-start | bytes 9224 | tf_op jit(solution)/shard_map/ppermute | solution.py:348
  4.7 1.2 %fusion = (bf16[6,1,256,128]{3,2,1,0:T(8,128)(2,1)S(1)}, bf16[6,1,256,128]{3,2,1,0:T(8,128)(2,1)S(1)}) fusion(bf16[12,1,256,128]{3,2,1,0:T(8,128)(2,1)} %param.4), kind=kLoop, calls=%fused_computation.2 | loop fusion | bytes 1572864 | tf_op jit(solution)/shard_map/slice | solution.py:358
  6.3 1.8 %pack_stream.1.refs_1_ = bf16[1568,128]{1,0:T(8,128)(2,1)S(1)} custom-call(s32[3]{0:T(128)S(1)} %pad_add_fusion.me_ref, s32[6,128]{1,0:T(8,128)S(1)} %reshape.14.refs_0_, s32[6,128]{1,0:T(8,128)S(1)} %collective-permute-done.1.refs_1_, bf16[1536,128]{1,0:T(8,128)(2,1)S(1)} %bitcast.9), custom_call_target="tpu_custom_call" | custom-call | flops 1 | bytes 1 | tf_op jit(solution)/shard_map/pack_stream/pallas_call | solution.py:125
  8.2 2.1 %collective-permute-start.6 = (bf16[1568,128]{1,0:T(8,128)(2,1)S(1)}, bf16[1568,128]{1,0:T(8,128)(2,1)S(1)}, u32[]{:S(2)}, u32[]{:S(2)}) collective-permute-start(bf16[1568,128]{1,0:T(8,128)(2,1)S(1)} %pack_stream.1.refs_1_), channel_id=1, source_target_pairs={{0,4},{1,5},{2,6},{3,7},{8,0},{9,1},{10,2},{11,3},{16,8},{17,9},{1... | collective-permute-start | bytes 1204232 | tf_op jit(solution)/shard_map/ppermute | solution.py:348
  10.3 2.0 %collective-permute-start.4 = (bf16[1568,128]{1,0:T(8,128)(2,1)S(1)}, bf16[1568,128]{1,0:T(8,128)(2,1)S(1)}, u32[]{:S(2)}, u32[]{:S(2)}) collective-permute-start(bf16[1568,128]{1,0:T(8,128)(2,1)S(1)} %pack_stream.1.refs_1_), channel_id=1, source_target_pairs={{0,8},{1,9},{2,10},{3,11},{8,16},{9,17},{10,18},{11,19},{16,24},{1... | collective-permute-start | bytes 1204232 | tf_op jit(solution)/shard_map/ppermute | solution.py:348
  12.4 2.2 %copy-done = bf16[256,64,128]{2,1,0:T(8,128)(2,1)S(1)} copy-done((bf16[256,64,128]{2,1,0:T(8,128)(2,1)S(1)}, bf16[256,64,128]{2,1,0:T(8,128)(2,1)}, u32[]{:S(2)}) %copy-start) | copy-done | bytes 4194328
  14.6 2.8 %unit_blocks.2.refs_2_.refs_4_.refs_9_ = bf16[256,64,128]{2,1,0:T(8,128)(2,1)S(1)} custom-call(bf16[256,64,128]{2,1,0:T(8,128)(2,1)S(1)} %copy-done), custom_call_target="tpu_custom_call" | custom-call | flops 1 | bytes 1 | tf_op jit(solution)/shard_map/unit_blocks/pallas_call | solution.py:33
  17.4 5.0 %unit_blocks.3.refs_3_.refs_5_.refs_10_ = bf16[256,64,128]{2,1,0:T(8,128)(2,1)S(1)} custom-call(bf16[256,64,128]{2,1,0:T(8,128)(2,1)} %collective-permute-done.2.blocks_ref), custom_call_target="tpu_custom_call" | custom-call | flops 1 | bytes 1 | tf_op jit(solution)/shard_map/unit_blocks/pallas_call | solution.py:33
  22.4 3.9 %score_chunks.5.refs_2_ = f32[12,128]{1,0:T(8,128)S(1)} custom-call(s32[3]{0:T(128)S(1)} %pad_add_fusion.me_ref, bf16[1536,128]{1,0:T(8,128)(2,1)S(1)} %bitcast.8, bf16[1568,128]{1,0:T(8,128)(2,1)S(1)} %pack_stream.1.refs_1_, bf16[256,64,128]{2,1,0:T(8,128)(2,1)S(1)} %unit_blocks.2.refs_2_.refs_4_.refs_9_, ...), custom_call_target="tpu_custom_call" | custom-call | flops 402653184 | bytes 8388608 | tf_op jit(solution)/shard_map/score_chunks/pallas_call | solution.py:270
  26.4 1.3 %collective-permute-start.10 = (bf16[1568,128]{1,0:T(8,128)(2,1)S(1)}, bf16[1568,128]{1,0:T(8,128)(2,1)S(1)}, u32[]{:S(2)}, u32[]{:S(2)}) collective-permute-start(bf16[1568,128]{1,0:T(8,128)(2,1)S(1)} %collective-permute-done.6.refs_3_), channel_id=1, source_target_pairs={{0,4},{1,5},{2,6},{3,7},{8,0},{9,1},{10,2},{11,3},{16,8},{17,9},{1... | collective-permute-start | bytes 1204232 | tf_op jit(solution)/shard_map/ppermute | solution.py:348
  29.1 1.4 %collective-permute-start.9 = (bf16[1536,128]{1,0:T(8,128)(2,1)S(1)}, bf16[1536,128]{1,0:T(8,128)(2,1)S(1)}, u32[]{:S(2)}, u32[]{:S(2)}) collective-permute-start(bf16[1536,128]{1,0:T(8,128)(2,1)S(1)} %collective-permute-done.5.refs_2_), channel_id=1, source_target_pairs={{0,4},{1,5},{2,6},{3,7},{8,0},{9,1},{10,2},{11,3},{16,8},{17,9},{1... | collective-permute-start | bytes 1179656 | tf_op jit(solution)/shard_map/ppermute | solution.py:348
  31.1 6.4 %score_chunks.6 = (f32[12,128]{1,0:T(8,128)S(1)}, f32[12,128]{1,0:T(8,128)S(1)}) custom-call(s32[3]{0:T(128)S(1)} %pad_add_fusion.me_ref, bf16[1536,128]{1,0:T(8,128)(2,1)S(1)} %collective-permute-done.refs_0_, bf16[1568,128]{1,0:T(8,128)(2,1)S(1)} %collective-permute-done.4.refs_1_, bf16[1536,128]{1,0:T(8,128)(2,1)S(1)} %collective-permute-done.5.refs_2_, ...), custom_call_target="tpu_custom_call" | custom-call | flops 805306368 | bytes 8388608 | tf_op jit(solution)/shard_map/score_chunks/pallas_call | solution.py:270
  37.5 1.1 %collective-permute-done.10.refs_3_ = bf16[1568,128]{1,0:T(8,128)(2,1)S(1)} collective-permute-done((bf16[1568,128]{1,0:T(8,128)(2,1)S(1)}, bf16[1568,128]{1,0:T(8,128)(2,1)S(1)}, u32[]{:S(2)}, u32[]{:S(2)}) %collective-permute-start.10) | collective-permute-done | bytes 401440 | tf_op jit(solution)/shard_map/ppermute | solution.py:348
  38.6 1.2 %collective-permute-start.12 = (bf16[1568,128]{1,0:T(8,128)(2,1)S(1)}, bf16[1568,128]{1,0:T(8,128)(2,1)S(1)}, u32[]{:S(2)}, u32[]{:S(2)}) collective-permute-start(bf16[1568,128]{1,0:T(8,128)(2,1)S(1)} %collective-permute-done.10.refs_3_), channel_id=1, source_target_pairs={{0,4},{1,5},{2,6},{3,7},{8,0},{9,1},{10,2},{11,3},{16,8},{17,9},{1... | collective-permute-start | bytes 1204232 | tf_op jit(solution)/shard_map/ppermute | solution.py:348
  40.7 6.4 %collective-permute-done.9.refs_2_ = bf16[1536,128]{1,0:T(8,128)(2,1)S(1)} collective-permute-done((bf16[1536,128]{1,0:T(8,128)(2,1)S(1)}, bf16[1536,128]{1,0:T(8,128)(2,1)S(1)}, u32[]{:S(2)}, u32[]{:S(2)}) %collective-permute-start.9) | collective-permute-done | bytes 393248 | tf_op jit(solution)/shard_map/ppermute | solution.py:348
  47.1 1.2 %collective-permute-start.15 = (bf16[1536,128]{1,0:T(8,128)(2,1)S(1)}, bf16[1536,128]{1,0:T(8,128)(2,1)S(1)}, u32[]{:S(2)}, u32[]{:S(2)}) collective-permute-start(bf16[1536,128]{1,0:T(8,128)(2,1)S(1)} %collective-permute-done.9.refs_2_), channel_id=1, source_target_pairs={{0,4},{1,5},{2,6},{3,7},{8,0},{9,1},{10,2},{11,3},{16,8},{17,9},{1... | collective-permute-start | bytes 1179656 | tf_op jit(solution)/shard_map/ppermute | solution.py:348
  49.1 7.1 %score_chunks.7 = (f32[12,128]{1,0:T(8,128)S(1)}, f32[12,128]{1,0:T(8,128)S(1)}) custom-call(s32[3]{0:T(128)S(1)} %pad_add_fusion.me_ref, bf16[1536,128]{1,0:T(8,128)(2,1)S(1)} %collective-permute-done.3.refs_0_, bf16[1568,128]{1,0:T(8,128)(2,1)S(1)} %collective-permute-done.8.refs_1_, bf16[1536,128]{1,0:T(8,128)(2,1)S(1)} %collective-permute-done.9.refs_2_, ...), custom_call_target="tpu_custom_call" | custom-call | flops 805306368 | bytes 8388608 | tf_op jit(solution)/shard_map/score_chunks/pallas_call | solution.py:270
  57.0 1.4 %collective-permute-start.11 = (bf16[1536,128]{1,0:T(8,128)(2,1)S(1)}, bf16[1536,128]{1,0:T(8,128)(2,1)S(1)}, u32[]{:S(2)}, u32[]{:S(2)}) collective-permute-start(bf16[1536,128]{1,0:T(8,128)(2,1)S(1)} %collective-permute-done.7.refs_0_), channel_id=1, source_target_pairs={{0,8},{1,9},{2,10},{3,11},{8,16},{9,17},{10,18},{11,19},{16,24},{1... | collective-permute-start | bytes 1179656 | tf_op jit(solution)/shard_map/ppermute | solution.py:348
  58.3 5.8 %collective-permute-done.15.refs_2_ = bf16[1536,128]{1,0:T(8,128)(2,1)S(1)} collective-permute-done((bf16[1536,128]{1,0:T(8,128)(2,1)S(1)}, bf16[1536,128]{1,0:T(8,128)(2,1)S(1)}, u32[]{:S(2)}, u32[]{:S(2)}) %collective-permute-start.15) | collective-permute-done | bytes 393248 | tf_op jit(solution)/shard_map/ppermute | solution.py:348
  64.1 1.5 %collective-permute-done.14.refs_1_ = bf16[1568,128]{1,0:T(8,128)(2,1)S(1)} collective-permute-done((bf16[1568,128]{1,0:T(8,128)(2,1)S(1)}, bf16[1568,128]{1,0:T(8,128)(2,1)S(1)}, u32[]{:S(2)}, u32[]{:S(2)}) %collective-permute-start.14) | collective-permute-done | bytes 401440 | tf_op jit(solution)/shard_map/ppermute | solution.py:348
  65.6 6.5 %score_chunks.8 = (f32[12,128]{1,0:T(8,128)S(1)}, f32[12,128]{1,0:T(8,128)S(1)}) custom-call(s32[3]{0:T(128)S(1)} %pad_add_fusion.me_ref, bf16[1536,128]{1,0:T(8,128)(2,1)S(1)} %collective-permute-done.7.refs_0_, bf16[1568,128]{1,0:T(8,128)(2,1)S(1)} %collective-permute-done.14.refs_1_, bf16[1536,128]{1,0:T(8,128)(2,1)S(1)} %collective-permute-done.15.refs_2_, ...), custom_call_target="tpu_custom_call" | custom-call | flops 805306368 | bytes 8388608 | tf_op jit(solution)/shard_map/score_chunks/pallas_call | solution.py:270
  72.0 4.5 %score_chunks.9 = (f32[12,128]{1,0:T(8,128)}, f32[256,128]{1,0:T(8,128)S(1)}) custom-call(s32[3]{0:T(128)S(1)} %pad_add_fusion.me_ref, bf16[1536,128]{1,0:T(8,128)(2,1)S(1)} %collective-permute-done.11.refs_0_, bf16[1568,128]{1,0:T(8,128)(2,1)S(1)} %collective-permute-done.13.refs_1_, f32[12,128]{1,0:T(8,128)S(1)} %score_chunks.5.refs_2_, ...), custom_call_target="tpu_custom_call" | custom-call | flops 402653184 | bytes 8388608 | tf_op jit(solution)/shard_map/score_chunks/pallas_call | solution.py:270
  76.5 14.5 %all_to_all.9.parts_ref = f32[32,8,128]{2,1,0:T(8,128)} all-to-all(f32[32,8,128]{2,1,0:T(8,128)S(1)} %bitcast.10), channel_id=1, replica_groups=mesh['art'=16,'seq'=2] {'art','seq'}, dimensions={0} | all-to-all | bytes 262144 | tf_op jit(solution)/shard_map/all_to_all | solution.py:381
  91.1 1.7 %close.1 = (f32[12,64]{1,0:T(8,128)}, f32[12,64]{1,0:T(8,128)}) custom-call(f32[32,8,128]{2,1,0:T(8,128)} %all_to_all.9.parts_ref), custom_call_target="tpu_custom_call" | custom-call | tf_op jit(solution)/shard_map/close/pallas_call | solution.py:311
  (25 shorter events, 6.5 us)
Async XLA Ops:
  0.6 16.8 %collective-permute-start.2 = (bf16[256,64,128]{2,1,0:T(8,128)(2,1)}, bf16[256,64,128]{2,1,0:T(8,128)(2,1)}, u32[]{:S(2)}, u32[]{:S(2)}) collective-permute-start(bf16[256,64,128]{2,1,0:T(8,128)(2,1)} %blocks_ref.1), channel_id=1, source_target_pairs={{0,2},{2,0},{4,6},{6,4},{8,10},{10,8},{12,14},{14,12},{16,18},{18,... | collective-permute-start | bytes 12582920 | tf_op jit(solution)/shard_map/ppermute | solution.py:363
  2.2 4.2 %collective-permute-start.1 = (s32[6,128]{1,0:T(8,128)S(1)}, s32[6,128]{1,0:T(8,128)S(1)}, u32[]{:S(2)}, u32[]{:S(2)}) collective-permute-start(s32[6,128]{1,0:T(8,128)S(1)} %reshape.14.refs_0_), channel_id=1, source_target_pairs={{0,1},{1,0},{2,3},{3,2},{8,9},{9,8},{10,11},{11,10},{16,17},{17,16... | collective-permute-start | bytes 9224 | tf_op jit(solution)/shard_map/ppermute | solution.py:348
  8.2 18.2 %collective-permute-start.6 = (bf16[1568,128]{1,0:T(8,128)(2,1)S(1)}, bf16[1568,128]{1,0:T(8,128)(2,1)S(1)}, u32[]{:S(2)}, u32[]{:S(2)}) collective-permute-start(bf16[1568,128]{1,0:T(8,128)(2,1)S(1)} %pack_stream.1.refs_1_), channel_id=1, source_target_pairs={{0,4},{1,5},{2,6},{3,7},{8,0},{9,1},{10,2},{11,3},{16,8},{17,9},{1... | collective-permute-start | bytes 1204232 | tf_op jit(solution)/shard_map/ppermute | solution.py:348
  10.2 17.4 %collective-permute-start = (bf16[1536,128]{1,0:T(8,128)(2,1)S(1)}, bf16[1536,128]{1,0:T(8,128)(2,1)S(1)}, u32[]{:S(2)}, u32[]{:S(2)}) collective-permute-start(bf16[1536,128]{1,0:T(8,128)(2,1)S(1)} %bitcast.6), channel_id=1, source_target_pairs={{0,8},{1,9},{2,10},{3,11},{8,16},{9,17},{10,18},{11,19},{16,24},{1... | collective-permute-start | bytes 1179656 | tf_op jit(solution)/shard_map/ppermute | solution.py:348
  10.3 18.7 %collective-permute-start.4 = (bf16[1568,128]{1,0:T(8,128)(2,1)S(1)}, bf16[1568,128]{1,0:T(8,128)(2,1)S(1)}, u32[]{:S(2)}, u32[]{:S(2)}) collective-permute-start(bf16[1568,128]{1,0:T(8,128)(2,1)S(1)} %pack_stream.1.refs_1_), channel_id=1, source_target_pairs={{0,8},{1,9},{2,10},{3,11},{8,16},{9,17},{10,18},{11,19},{16,24},{1... | collective-permute-start | bytes 1204232 | tf_op jit(solution)/shard_map/ppermute | solution.py:348
  12.3 16.1 %collective-permute-start.5 = (bf16[1536,128]{1,0:T(8,128)(2,1)S(1)}, bf16[1536,128]{1,0:T(8,128)(2,1)S(1)}, u32[]{:S(2)}, u32[]{:S(2)}) collective-permute-start(bf16[1536,128]{1,0:T(8,128)(2,1)S(1)} %bitcast.7), channel_id=1, source_target_pairs={{0,4},{1,5},{2,6},{3,7},{8,0},{9,1},{10,2},{11,3},{16,8},{17,9},{1... | collective-permute-start | bytes 1179656 | tf_op jit(solution)/shard_map/ppermute | solution.py:348
  12.4 2.2 %copy-start = (bf16[256,64,128]{2,1,0:T(8,128)(2,1)S(1)}, bf16[256,64,128]{2,1,0:T(8,128)(2,1)}, u32[]{:S(2)}) copy-start(bf16[256,64,128]{2,1,0:T(8,128)(2,1)} %blocks_ref.1) | copy-start | bytes 12582916
  26.4 12.3 %collective-permute-start.10 = (bf16[1568,128]{1,0:T(8,128)(2,1)S(1)}, bf16[1568,128]{1,0:T(8,128)(2,1)S(1)}, u32[]{:S(2)}, u32[]{:S(2)}) collective-permute-start(bf16[1568,128]{1,0:T(8,128)(2,1)S(1)} %collective-permute-done.6.refs_3_), channel_id=1, source_target_pairs={{0,4},{1,5},{2,6},{3,7},{8,0},{9,1},{10,2},{11,3},{16,8},{17,9},{1... | collective-permute-start | bytes 1204232 | tf_op jit(solution)/shard_map/ppermute | solution.py:348
  27.7 12.3 %collective-permute-start.3 = (bf16[1536,128]{1,0:T(8,128)(2,1)S(1)}, bf16[1536,128]{1,0:T(8,128)(2,1)S(1)}, u32[]{:S(2)}, u32[]{:S(2)}) collective-permute-start(bf16[1536,128]{1,0:T(8,128)(2,1)S(1)} %collective-permute-done.refs_0_), channel_id=1, source_target_pairs={{0,8},{1,9},{2,10},{3,11},{8,16},{9,17},{10,18},{11,19},{16,24},{1... | collective-permute-start | bytes 1179656 | tf_op jit(solution)/shard_map/ppermute | solution.py:348
  29.1 18.0 %collective-permute-start.9 = (bf16[1536,128]{1,0:T(8,128)(2,1)S(1)}, bf16[1536,128]{1,0:T(8,128)(2,1)S(1)}, u32[]{:S(2)}, u32[]{:S(2)}) collective-permute-start(bf16[1536,128]{1,0:T(8,128)(2,1)S(1)} %collective-permute-done.5.refs_2_), channel_id=1, source_target_pairs={{0,4},{1,5},{2,6},{3,7},{8,0},{9,1},{10,2},{11,3},{16,8},{17,9},{1... | collective-permute-start | bytes 1179656 | tf_op jit(solution)/shard_map/ppermute | solution.py:348
  30.5 18.0 %collective-permute-start.8 = (bf16[1568,128]{1,0:T(8,128)(2,1)S(1)}, bf16[1568,128]{1,0:T(8,128)(2,1)S(1)}, u32[]{:S(2)}, u32[]{:S(2)}) collective-permute-start(bf16[1568,128]{1,0:T(8,128)(2,1)S(1)} %collective-permute-done.4.refs_1_), channel_id=1, source_target_pairs={{0,8},{1,9},{2,10},{3,11},{8,16},{9,17},{10,18},{11,19},{16,24},{1... | collective-permute-start | bytes 1204232 | tf_op jit(solution)/shard_map/ppermute | solution.py:348
  38.6 17.6 %collective-permute-start.12 = (bf16[1568,128]{1,0:T(8,128)(2,1)S(1)}, bf16[1568,128]{1,0:T(8,128)(2,1)S(1)}, u32[]{:S(2)}, u32[]{:S(2)}) collective-permute-start(bf16[1568,128]{1,0:T(8,128)(2,1)S(1)} %collective-permute-done.10.refs_3_), channel_id=1, source_target_pairs={{0,4},{1,5},{2,6},{3,7},{8,0},{9,1},{10,2},{11,3},{16,8},{17,9},{1... | collective-permute-start | bytes 1204232 | tf_op jit(solution)/shard_map/ppermute | solution.py:348
  39.9 17.0 %collective-permute-start.7 = (bf16[1536,128]{1,0:T(8,128)(2,1)S(1)}, bf16[1536,128]{1,0:T(8,128)(2,1)S(1)}, u32[]{:S(2)}, u32[]{:S(2)}) collective-permute-start(bf16[1536,128]{1,0:T(8,128)(2,1)S(1)} %collective-permute-done.3.refs_0_), channel_id=1, source_target_pairs={{0,8},{1,9},{2,10},{3,11},{8,16},{9,17},{10,18},{11,19},{16,24},{1... | collective-permute-start | bytes 1179656 | tf_op jit(solution)/shard_map/ppermute | solution.py:348
  47.1 17.0 %collective-permute-start.15 = (bf16[1536,128]{1,0:T(8,128)(2,1)S(1)}, bf16[1536,128]{1,0:T(8,128)(2,1)S(1)}, u32[]{:S(2)}, u32[]{:S(2)}) collective-permute-start(bf16[1536,128]{1,0:T(8,128)(2,1)S(1)} %collective-permute-done.9.refs_2_), channel_id=1, source_target_pairs={{0,4},{1,5},{2,6},{3,7},{8,0},{9,1},{10,2},{11,3},{16,8},{17,9},{1... | collective-permute-start | bytes 1179656 | tf_op jit(solution)/shard_map/ppermute | solution.py:348
  48.5 17.0 %collective-permute-start.14 = (bf16[1568,128]{1,0:T(8,128)(2,1)S(1)}, bf16[1568,128]{1,0:T(8,128)(2,1)S(1)}, u32[]{:S(2)}, u32[]{:S(2)}) collective-permute-start(bf16[1568,128]{1,0:T(8,128)(2,1)S(1)} %collective-permute-done.8.refs_1_), channel_id=1, source_target_pairs={{0,8},{1,9},{2,10},{3,11},{8,16},{9,17},{10,18},{11,19},{16,24},{1... | collective-permute-start | bytes 1204232 | tf_op jit(solution)/shard_map/ppermute | solution.py:348
  56.2 15.8 %collective-permute-start.13 = (bf16[1568,128]{1,0:T(8,128)(2,1)S(1)}, bf16[1568,128]{1,0:T(8,128)(2,1)S(1)}, u32[]{:S(2)}, u32[]{:S(2)}) collective-permute-start(bf16[1568,128]{1,0:T(8,128)(2,1)S(1)} %collective-permute-done.12.refs_3_), channel_id=1, source_target_pairs={{0,4},{1,5},{2,6},{3,7},{8,0},{9,1},{10,2},{11,3},{16,8},{17,9},{1... | collective-permute-start | bytes 1204232 | tf_op jit(solution)/shard_map/ppermute | solution.py:348
  57.0 15.1 %collective-permute-start.11 = (bf16[1536,128]{1,0:T(8,128)(2,1)S(1)}, bf16[1536,128]{1,0:T(8,128)(2,1)S(1)}, u32[]{:S(2)}, u32[]{:S(2)}) collective-permute-start(bf16[1536,128]{1,0:T(8,128)(2,1)S(1)} %collective-permute-done.7.refs_0_), channel_id=1, source_target_pairs={{0,8},{1,9},{2,10},{3,11},{8,16},{9,17},{10,18},{11,19},{16,24},{1... | collective-permute-start | bytes 1179656 | tf_op jit(solution)/shard_map/ppermute | solution.py:348

commit v3 on v2

--- a/solution.py
+++ b/solution.py
@@ -13,30 +13,46 @@
 SHARP = 16.0
 TEMPER = 4.0
 GROUP = 4
-UNROLL = 12
+UCOST = 4000000000
+SCOST = 2.0
+UNROLL = 16
+PREP = 3
 LAST = (((1,), (1,)), ((), ()))
 
 
-def unit_kernel(blocks_ref, out_ref):
-    count, tokens, width = blocks_ref.shape
-
-    def some(i, carry):
-        wide = blocks_ref[pl.ds(2 * i, 2)].astype(jnp.float32)
-        norm = jnp.sum(wide * wide, axis=-1, keepdims=True)
-        out_ref[pl.ds(2 * i, 2)] = (wide * lax.rsqrt(norm + EPS)).astype(jnp.bfloat16)
-        return carry
-
-    lax.fori_loop(0, count // 2, some, 0, unroll=16)
+def unit_kernel(parts, blocks_ref, out_ref, held_ref, sems):
+    part = blocks_ref.shape[0] // parts
+    copies = []
+    for p in range(parts):
+        rows = pl.ds(p * part, part)
+        copies.append(pltpu.make_async_copy(blocks_ref.at[rows], held_ref.at[rows], sems.at[p]))
+        copies[-1].start()
+    for p in range(parts):
+        copies[p].wait()
+
+        def some(i, carry, p=p):
+            rows = pl.ds(p * part + 2 * i, 2)
+            wide = held_ref[rows].astype(jnp.float32)
+            norm = jnp.sum(wide * wide, axis=-1, keepdims=True)
+            out_ref[rows] = (wide * lax.rsqrt(norm + EPS)).astype(jnp.bfloat16)
+            return carry
+
+        lax.fori_loop(0, part // 2, some, 0, unroll=16)
 
 
 def unit_blocks(blocks):
+    parts = 4
     return pl.pallas_call(
-        unit_kernel,
+        functools.partial(unit_kernel, parts),
         out_shape=jax.ShapeDtypeStruct(blocks.shape, jnp.bfloat16),
-        in_specs=[pl.BlockSpec(memory_space=pltpu.VMEM)],
+        in_specs=[pl.BlockSpec(memory_space=pltpu.HBM)],
         out_specs=pl.BlockSpec(memory_space=pltpu.VMEM),
+        scratch_shapes=[
+            pltpu.VMEM(blocks.shape, jnp.bfloat16),
+            pltpu.SemaphoreType.DMA((parts,)),
+        ],
         compiler_params=pltpu.CompilerParams(vmem_limit_bytes=32 * 1024 * 1024),
-        cost_estimate=pl.CostEstimate(flops=1, bytes_accessed=1, transcendentals=0),
+        cost_estimate=pl.CostEstimate(flops=UCOST, bytes_accessed=1, transcendentals=0),
         name="unit_blocks",
     )(blocks)
 
@@ -121,11 +137,15 @@
 def pack_stream(me, ids, query, chips, blocks):
     vmem = pl.BlockSpec(memory_space=pltpu.VMEM)
     articles = len(ids) * ids[0].shape[0]
-    rows = query.shape[0] + plan_rows(chips, articles)[1]
+    half = query.shape[0] // 2
+    rows = half + plan_rows(chips, articles)[1]
     return pl.pallas_call(
         functools.partial(pack_kernel, chips, blocks),
         out_shape=jax.ShapeDtypeStruct((rows, query.shape[1]), jnp.bfloat16),
-        in_specs=[pl.BlockSpec(memory_space=pltpu.SMEM)] + [vmem] * (len(ids) + 1),
+        grid=(1,),
+        in_specs=[pl.BlockSpec(memory_space=pltpu.SMEM)]
+        + [vmem] * len(ids)
+        + [pl.BlockSpec((half, query.shape[1]), lambda i: (1, 0))],
         out_specs=vmem,
         compiler_params=pltpu.CompilerParams(vmem_limit_bytes=32 * 1024 * 1024),
         cost_estimate=pl.CostEstimate(flops=1, bytes_accessed=1, transcendentals=0),
@@ -162,9 +182,8 @@
         copy.start()
         copies.append(copy)
 
-    for p, ref in enumerate(pair_refs):
-
-        def prepare(i, carry, p=p, ref=ref):
+    def prepare(i, carry):
+        for p, ref in enumerate(pair_refs):
             query = ref[pl.ds(pl.multiple_of(i * tokens, tokens), tokens), :]
             wide = query.astype(jnp.float32)
             norm = lax.dot_general(
@@ -176,9 +195,9 @@
             at = p * (articles // 2) + i
             scale_ref[at] = lax.rsqrt(norm + EPS) * (SHARP * math.log2(math.e))
             turned_ref[at] = query.T
-            return carry
-
-        lax.fori_loop(0, articles // 2, prepare, 0, unroll=2)
+        return carry
+
+    lax.fori_loop(0, articles // 2, prepare, 0, unroll=PREP)
     mass_ref[...] = jnp.ones_like(mass_ref)
     for copy in copies:
         copy.wait()
@@ -226,16 +245,13 @@
     lax.fori_loop(0, (total + UNROLL - 1) // UNROLL, some, 0)
 
     per_home = articles // seqs
-    ones = jnp.ones((8, tokens), jnp.bfloat16)
+    lane = lax.broadcasted_iota(jnp.int32, (NC, 128), 1)
     for p in range(plans):
+        sums = jnp.zeros((NC, 128), jnp.float32)
         for i in range(articles):
             logs = jnp.log2(mass_ref[p * half + i * NC : p * half + (i + 1) * NC, :])
-            high = logs.astype(jnp.bfloat16)
-            low = (logs - high.astype(jnp.float32)).astype(jnp.bfloat16)
-            sums = lax.dot_general(
-                ones, high, LAST, preferred_element_type=jnp.float32
-            ) + lax.dot_general(ones, low, LAST, preferred_element_type=jnp.float32)
-            out_refs[p][i : i + 1, 0:NC] = sums[0:1] * (math.log(2) / SHARP)
+            sums = jnp.where(lane == i, jnp.sum(logs, axis=1, keepdims=True), sums)
+        out_refs[p][:, 0:NC] = (sums * (math.log(2) / SHARP)).T[0:articles]
     if not others:
         return
 
@@ -282,9 +298,9 @@
         ],
         compiler_params=pltpu.CompilerParams(vmem_limit_bytes=32 * 1024 * 1024),
         cost_estimate=pl.CostEstimate(
-            flops=2 * work * tokens * keys * width,
+            flops=int(SCOST * work * tokens * keys * width),
             bytes_accessed=4 * own.size,
-            transcendentals=work * tokens * keys,
+            transcendentals=int(SCOST / 2 * work * tokens * keys),
         ),
         name="score_chunks",
     )(me, *[x for pair in pairs for x in pair], *others, own, other)
@@ -355,28 +371,42 @@
     ids = (cand_owner * blocks + cand_local).reshape(per_home, seqs * NC)
     ids = [ids] + [send(ids, 0, d) for d in range(1, seqs)]
     me = jnp.stack([art // 2, art % 2, seq]).astype(jnp.int32)
-    two = pack_stream(me, ids, mine[cut:], chips, blocks)
+    two = pack_stream(me, ids, mine, chips, blocks)
     second = [send(two, 1), send(two, -1)]
     ahead.append([first[0], second[0]])
     behind.append([first[1], second[1]])
-    own = unit_blocks(companies)
-    other = unit_blocks(lax.ppermute(companies, "art", [(i, i ^ 1) for i in range(arts)]))
+    own = unit_blocks(lax.optimization_barrier((companies, *first))[0])
+    other = lax.ppermute(companies, "art", [(i, i ^ 1) for i in range(arts)])
+    other = unit_blocks(lax.optimization_barrier((other, *first))[0])
 
     def score(*pairs, others=()):
         return score_chunks(me, pairs, others, own, other, tokens, wide, deep, seqs)
 
-    done = score((one, two))
-    early = list(done)
+    def after(array, *things):
+        return lax.optimization_barrier((array, *things))[0]
+
+    early = list(score((after(one, *second), two)))
+    done = early[0]
     for d in range(1, half):
-        for side in (ahead, behind):
-            side[d] = [lax.optimization_barrier((x, done[0]))[0] for x in side[d]]
+        a, b = [ahead[d][0], behind[d][0]], [ahead[d][1], behind[d][1]]
+        if d == 1:
+            b = [after(x, other) for x in b]
+        else:
+            fresh = after(ahead[d - 1][0], done, *a)
+            more = score((fresh, ahead[d - 1][1]), behind[d - 1])
+            early += more
+            a = [after(x, done if d + 1 < half else more[0]) for x in a]
+            b = [after(x, more[0]) for x in b]
+            done = more[0]
+        a, b = lax.optimization_barrier(a), lax.optimization_barrier(b)
+        if d + 1 == half:
+            ahead[d], behind[d] = [a[0], b[0]], [a[1], b[1]]
         if d + 1 < half:
-            ahead.append([send(x, 1) for x in ahead[d]])
-            behind.append([send(x, -1) for x in behind[d]])
+            ahead.append([send(a[0], 1), send(b[0], 1)])
+            behind.append([send(a[1], -1), send(b[1], -1)])
         else:
-            last = (send(ahead[d][0], 1), send(behind[d][1], -1))
-        done = score(ahead[d], behind[d])
-        early += done
+            last = (send(a[0], 1), send(b[1], -1))
+    early += score(ahead[half - 1], behind[half - 1])
     spread = score(last, others=early)[1]
     parts = lax.all_to_all(spread, ("art", "seq"), split_axis=0, concat_axis=0, tiled=True)
     return tuple(close(parts.reshape(arts * seqs, -1, 128), articles, seqs))

time: 93.5 us -> 88 us (0.941)
  Pallas kernels: 39.8 us -> 33.3 us
  waiting for transfers between devices: 16 us -> 18.8 us
  local copies, waits for them, and re-layouts: 3.61 us -> 2.42 us
    pallas_call x5, Pallas kernels: 28.4 us -> 22.5 us  [score_chunks(): pl.pallas_call(functools.partial(score_kernel, (plans, len(others), seqs,...]
    ppermute x15, waiting for transfers between devices: 16 us -> 18.8 us  [send(): return lax.ppermute(array, ('art', 'seq'), turn(step, across))]
    unnamed x2 -> x4, local copies, waits for them, and re-layouts: 2.19 us -> 1.14 us
  transfers between devices with their start and end apart: 16 -> 16, of which waited for: 7 -> 10; matrix products, arithmetic and copies ran while one was open for 2% -> 2% of each run, Pallas kernels for 36% -> 32%
where the time goes in v3:
time: 88 us; the launch traced here: 87.7 us
  Pallas kernels  33.3 us (38%)
  waiting for transfers between devices  18.8 us (21%)
  starting transfers between devices  17.4 us (20%)
  blocking collectives  14.3 us (16%)
  local copies, waits for them, and re-layouts  2.42 us (3%)
    pallas_call x5, Pallas kernels, score_chunks(): pl.pallas_call(functools.partial(score_kernel, (plans, len(others), seqs,...  22.5 us
    ppermute x15, waiting for transfers between devices, send(): return lax.ppermute(array, ('art', 'seq'), turn(step, across))  18.8 us
    ppermute x15, starting transfers between devices, send(): return lax.ppermute(array, ('art', 'seq'), turn(step, across))  16.9 us
    all_to_all x1, blocking collectives, per_device(): lax.all_to_all(spread, ('art', 'seq'), split_axis=0, concat_axis=0, tiled...  14.3 us
    pallas_call x2, Pallas kernels, unit_blocks(): pl.pallas_call(functools.partial(unit_kernel, parts), out_shape=jax.Shape...  7.26 us
    pallas_call x1, Pallas kernels, pack_stream(): pl.pallas_call(functools.partial(pack_kernel, chips, blocks), out_shape=j...  1.83 us
  transfers between devices with their start and end apart: 16, of which 10 were waited for; matrix products, arithmetic and copies ran while one was open for 2% of the time, Pallas kernels for 32%

profile of v3, /device:TPU:0, one launch (start us, length us, event | category | flops | bytes accessed | tf_op | source)
XLA Modules:
  0.0 87.7 jit_solution(5494263293012285316)
XLA Ops:
  2.2 2.6 %collective-permute-start = (bf16[1536,128]{1,0:T(8,128)(2,1)S(1)}, bf16[1536,128]{1,0:T(8,128)(2,1)S(1)}, u32[]{:S(2)}, u32[]{:S(2)}) collective-permute-start(bf16[1536,128]{1,0:T(8,128)(2,1)S(1)} %bitcast.7), channel_id=1, source_target_pairs={{0,8},{1,9},{2,10},{3,11},{8,16},{9,17},{10,18},{11,19},{16,24},{1... | collective-permute-start | bytes 1179656 | tf_op jit(solution)/shard_map/ppermute | solution.py:364
  5.8 2.0 %collective-permute-start.3 = (s32[6,128]{1,0:T(8,128)S(1)}, s32[6,128]{1,0:T(8,128)S(1)}, u32[]{:S(2)}, u32[]{:S(2)}) collective-permute-start(s32[6,128]{1,0:T(8,128)S(1)} %reshape.15.refs_0_), channel_id=1, source_target_pairs={{0,1},{1,0},{2,3},{3,2},{8,9},{9,8},{10,11},{11,10},{16,17},{17,16... | collective-permute-start | bytes 9224 | tf_op jit(solution)/shard_map/ppermute | solution.py:364
  7.9 1.6 %collective-permute-done.3.refs_1_ = s32[6,128]{1,0:T(8,128)S(1)} collective-permute-done((s32[6,128]{1,0:T(8,128)S(1)}, s32[6,128]{1,0:T(8,128)S(1)}, u32[]{:S(2)}, u32[]{:S(2)}) %collective-permute-start.3) | collective-permute-done | bytes 3104 | tf_op jit(solution)/shard_map/ppermute | solution.py:364
  10.7 1.8 %pack_stream.1.refs_1_ = bf16[1568,128]{1,0:T(8,128)(2,1)S(1)} custom-call(s32[3]{0:T(128)S(1)} %pad_add_fusion.me_ref, s32[6,128]{1,0:T(8,128)S(1)} %reshape.15.refs_0_, s32[6,128]{1,0:T(8,128)S(1)} %collective-permute-done.3.refs_1_, bf16[3072,128]{1,0:T(8,128)(2,1)S(1)} %bitcast.6), custom_call_target="tpu_custom_call" | custom-call | flops 1 | bytes 1 | tf_op jit(solution)/shard_map/pack_stream/pallas_call | solution.py:142
  12.5 2.1 %collective-permute-start.4 = (bf16[1568,128]{1,0:T(8,128)(2,1)S(1)}, bf16[1568,128]{1,0:T(8,128)(2,1)S(1)}, u32[]{:S(2)}, u32[]{:S(2)}) collective-permute-start(bf16[1568,128]{1,0:T(8,128)(2,1)S(1)} %pack_stream.1.refs_1_), channel_id=1, source_target_pairs={{0,8},{1,9},{2,10},{3,11},{8,16},{9,17},{10,18},{11,19},{16,24},{1... | collective-permute-start | bytes 1204232 | tf_op jit(solution)/shard_map/ppermute | solution.py:364
  16.1 1.6 %collective-permute-start.2 = (bf16[1536,128]{1,0:T(8,128)(2,1)S(1)}, bf16[1536,128]{1,0:T(8,128)(2,1)S(1)}, u32[]{:S(2)}, u32[]{:S(2)}) collective-permute-start(bf16[1536,128]{1,0:T(8,128)(2,1)S(1)} %collective-permute-done.refs_0_), channel_id=1, source_target_pairs={{0,8},{1,9},{2,10},{3,11},{8,16},{9,17},{10,18},{11,19},{16,24},{1... | collective-permute-start | bytes 1179656 | tf_op jit(solution)/shard_map/ppermute | solution.py:364
  18.1 4.1 %unit_blocks.3.refs_3_.refs_5_.refs_10_ = bf16[256,64,128]{2,1,0:T(8,128)(2,1)S(1)} custom-call(bf16[256,64,128]{2,1,0:T(8,128)(2,1)} %collective-permute-done.6.blocks_ref), custom_call_target="tpu_custom_call" | custom-call | flops 4000000000 | bytes 1 | tf_op jit(solution)/shard_map/unit_blocks/pallas_call | solution.py:45
  22.2 2.6 %collective-permute-done.4.refs_1_ = bf16[1568,128]{1,0:T(8,128)(2,1)S(1)} collective-permute-done((bf16[1568,128]{1,0:T(8,128)(2,1)S(1)}, bf16[1568,128]{1,0:T(8,128)(2,1)S(1)}, u32[]{:S(2)}, u32[]{:S(2)}) %collective-permute-start.4) | collective-permute-done | bytes 401440 | tf_op jit(solution)/shard_map/ppermute | solution.py:364
  24.8 2.0 %collective-permute-done.5.refs_3_ = bf16[1568,128]{1,0:T(8,128)(2,1)S(1)} collective-permute-done((bf16[1568,128]{1,0:T(8,128)(2,1)S(1)}, bf16[1568,128]{1,0:T(8,128)(2,1)S(1)}, u32[]{:S(2)}, u32[]{:S(2)}) %collective-permute-start.5) | collective-permute-done | bytes 401440 | tf_op jit(solution)/shard_map/ppermute | solution.py:364
  26.8 2.0 %collective-permute-start.10 = (bf16[1568,128]{1,0:T(8,128)(2,1)S(1)}, bf16[1568,128]{1,0:T(8,128)(2,1)S(1)}, u32[]{:S(2)}, u32[]{:S(2)}) collective-permute-start(bf16[1568,128]{1,0:T(8,128)(2,1)S(1)} %collective-permute-done.4.refs_1_), channel_id=1, source_target_pairs={{0,8},{1,9},{2,10},{3,11},{8,16},{9,17},{10,18},{11,19},{16,24},{1... | collective-permute-start | bytes 1204232 | tf_op jit(solution)/shard_map/ppermute | solution.py:364
  28.8 3.2 %unit_blocks.2.refs_2_.refs_4_.refs_9_ = bf16[256,64,128]{2,1,0:T(8,128)(2,1)S(1)} custom-call(bf16[256,64,128]{2,1,0:T(8,128)(2,1)S(1)} %copy-done.1), custom_call_target="tpu_custom_call" | custom-call | flops 4000000000 | bytes 1 | tf_op jit(solution)/shard_map/unit_blocks/pallas_call | solution.py:45
  32.0 3.2 %score_chunks.5.refs_2_ = f32[12,128]{1,0:T(8,128)S(1)} custom-call(s32[3]{0:T(128)S(1)} %pad_add_fusion.me_ref, bf16[1536,128]{1,0:T(8,128)(2,1)S(1)} %bitcast.9, bf16[1568,128]{1,0:T(8,128)(2,1)S(1)} %pack_stream.1.refs_1_, bf16[256,64,128]{2,1,0:T(8,128)(2,1)S(1)} %unit_blocks.2.refs_2_.refs_4_.refs_9_, ...), custom_call_target="tpu_custom_call" | custom-call | flops 402653184 | bytes 8388608 | tf_op jit(solution)/shard_map/score_chunks/pallas_call | solution.py:286
  35.2 1.6 %collective-permute-start.8 = (bf16[1536,128]{1,0:T(8,128)(2,1)S(1)}, bf16[1536,128]{1,0:T(8,128)(2,1)S(1)}, u32[]{:S(2)}, u32[]{:S(2)}) collective-permute-start(bf16[1536,128]{1,0:T(8,128)(2,1)S(1)} %collective-permute-done.2.refs_0_), channel_id=1, source_target_pairs={{0,8},{1,9},{2,10},{3,11},{8,16},{9,17},{10,18},{11,19},{16,24},{1... | collective-permute-start | bytes 1179656 | tf_op jit(solution)/shard_map/ppermute | solution.py:364
  37.3 5.2 %score_chunks.6 = (f32[12,128]{1,0:T(8,128)S(1)}, f32[12,128]{1,0:T(8,128)S(1)}) custom-call(s32[3]{0:T(128)S(1)} %pad_add_fusion.me_ref, bf16[1536,128]{1,0:T(8,128)(2,1)S(1)} %collective-permute-done.refs_0_, bf16[1568,128]{1,0:T(8,128)(2,1)S(1)} %collective-permute-done.4.refs_1_, bf16[1536,128]{1,0:T(8,128)(2,1)S(1)} %collective-permute-done.1.refs_2_, ...), custom_call_target="tpu_custom_call" | custom-call | flops 805306368 | bytes 8388608 | tf_op jit(solution)/shard_map/score_chunks/pallas_call | solution.py:286
  43.8 2.0 %collective-permute-start.13 = (bf16[1568,128]{1,0:T(8,128)(2,1)S(1)}, bf16[1568,128]{1,0:T(8,128)(2,1)S(1)}, u32[]{:S(2)}, u32[]{:S(2)}) collective-permute-start(bf16[1568,128]{1,0:T(8,128)(2,1)S(1)} %collective-permute-done.10.refs_1_), channel_id=1, source_target_pairs={{0,8},{1,9},{2,10},{3,11},{8,16},{9,17},{10,18},{11,19},{16,24},{1... | collective-permute-start | bytes 1204232 | tf_op jit(solution)/shard_map/ppermute | solution.py:364
  45.9 4.4 %collective-permute-done.8.refs_0_ = bf16[1536,128]{1,0:T(8,128)(2,1)S(1)} collective-permute-done((bf16[1536,128]{1,0:T(8,128)(2,1)S(1)}, bf16[1536,128]{1,0:T(8,128)(2,1)S(1)}, u32[]{:S(2)}, u32[]{:S(2)}) %collective-permute-start.8) | collective-permute-done | bytes 393248 | tf_op jit(solution)/shard_map/ppermute | solution.py:364
  50.2 2.0 %collective-permute-done.9.refs_2_ = bf16[1536,128]{1,0:T(8,128)(2,1)S(1)} collective-permute-done((bf16[1536,128]{1,0:T(8,128)(2,1)S(1)}, bf16[1536,128]{1,0:T(8,128)(2,1)S(1)}, u32[]{:S(2)}, u32[]{:S(2)}) %collective-permute-start.9) | collective-permute-done | bytes 393248 | tf_op jit(solution)/shard_map/ppermute | solution.py:364
  52.3 5.2 %score_chunks.7 = (f32[12,128]{1,0:T(8,128)S(1)}, f32[12,128]{1,0:T(8,128)S(1)}) custom-call(s32[3]{0:T(128)S(1)} %pad_add_fusion.me_ref, bf16[1536,128]{1,0:T(8,128)(2,1)S(1)} %collective-permute-done.2.refs_0_, bf16[1568,128]{1,0:T(8,128)(2,1)S(1)} %collective-permute-done.10.refs_1_, bf16[1536,128]{1,0:T(8,128)(2,1)S(1)} %collective-permute-done.7.refs_2_, ...), custom_call_target="tpu_custom_call" | custom-call | flops 805306368 | bytes 8388608 | tf_op jit(solution)/shard_map/score_chunks/pallas_call | solution.py:286
  59.0 1.7 %collective-permute-start.12 = (bf16[1536,128]{1,0:T(8,128)(2,1)S(1)}, bf16[1536,128]{1,0:T(8,128)(2,1)S(1)}, u32[]{:S(2)}, u32[]{:S(2)}) collective-permute-start(bf16[1536,128]{1,0:T(8,128)(2,1)S(1)} %collective-permute-done.8.refs_0_), channel_id=1, source_target_pairs={{0,8},{1,9},{2,10},{3,11},{8,16},{9,17},{10,18},{11,19},{16,24},{1... | collective-permute-start | bytes 1179656 | tf_op jit(solution)/shard_map/ppermute | solution.py:364
  60.7 5.2 %score_chunks.8 = (f32[12,128]{1,0:T(8,128)S(1)}, f32[12,128]{1,0:T(8,128)S(1)}) custom-call(s32[3]{0:T(128)S(1)} %pad_add_fusion.me_ref, bf16[1536,128]{1,0:T(8,128)(2,1)S(1)} %collective-permute-done.8.refs_0_, bf16[1568,128]{1,0:T(8,128)(2,1)S(1)} %collective-permute-done.13.refs_1_, bf16[1536,128]{1,0:T(8,128)(2,1)S(1)} %collective-permute-done.9.refs_2_, ...), custom_call_target="tpu_custom_call" | custom-call | flops 805306368 | bytes 8388608 | tf_op jit(solution)/shard_map/score_chunks/pallas_call | solution.py:286
  65.9 2.0 %collective-permute-done.12.refs_0_ = bf16[1536,128]{1,0:T(8,128)(2,1)S(1)} collective-permute-done((bf16[1536,128]{1,0:T(8,128)(2,1)S(1)}, bf16[1536,128]{1,0:T(8,128)(2,1)S(1)}, u32[]{:S(2)}, u32[]{:S(2)}) %collective-permute-start.12) | collective-permute-done | bytes 393248 | tf_op jit(solution)/shard_map/ppermute | solution.py:364
  68.0 3.8 %score_chunks.9 = (f32[12,128]{1,0:T(8,128)}, f32[256,128]{1,0:T(8,128)S(1)}) custom-call(s32[3]{0:T(128)S(1)} %pad_add_fusion.me_ref, bf16[1536,128]{1,0:T(8,128)(2,1)S(1)} %collective-permute-done.12.refs_0_, bf16[1568,128]{1,0:T(8,128)(2,1)S(1)} %collective-permute-done.15.refs_1_, f32[12,128]{1,0:T(8,128)S(1)} %score_chunks.5.refs_2_, ...), custom_call_target="tpu_custom_call" | custom-call | flops 402653184 | bytes 8388608 | tf_op jit(solution)/shard_map/score_chunks/pallas_call | solution.py:286
  71.7 14.3 %all_to_all.9.parts_ref = f32[32,8,128]{2,1,0:T(8,128)} all-to-all(f32[32,8,128]{2,1,0:T(8,128)S(1)} %bitcast.10), channel_id=1, replica_groups=mesh['art'=16,'seq'=2] {'art','seq'}, dimensions={0} | all-to-all | bytes 262144 | tf_op jit(solution)/shard_map/all_to_all | solution.py:411
  86.0 1.7 %close.1 = (f32[12,64]{1,0:T(8,128)}, f32[12,64]{1,0:T(8,128)}) custom-call(f32[32,8,128]{2,1,0:T(8,128)} %all_to_all.9.parts_ref), custom_call_target="tpu_custom_call" | custom-call | tf_op jit(solution)/shard_map/close/pallas_call | solution.py:327
  (27 shorter events, 9.2 us)
Async XLA Ops:
  0.6 17.5 %collective-permute-start.6 = (bf16[256,64,128]{2,1,0:T(8,128)(2,1)}, bf16[256,64,128]{2,1,0:T(8,128)(2,1)}, u32[]{:S(2)}, u32[]{:S(2)}) collective-permute-start(bf16[256,64,128]{2,1,0:T(8,128)(2,1)} %blocks_ref), channel_id=1, source_target_pairs={{0,2},{2,0},{4,6},{6,4},{8,10},{10,8},{12,14},{14,12},{16,18},{18,... | collective-permute-start | bytes 12582920 | tf_op jit(solution)/shard_map/ppermute | solution.py:379
  2.2 12.4 %collective-permute-start = (bf16[1536,128]{1,0:T(8,128)(2,1)S(1)}, bf16[1536,128]{1,0:T(8,128)(2,1)S(1)}, u32[]{:S(2)}, u32[]{:S(2)}) collective-permute-start(bf16[1536,128]{1,0:T(8,128)(2,1)S(1)} %bitcast.7), channel_id=1, source_target_pairs={{0,8},{1,9},{2,10},{3,11},{8,16},{9,17},{10,18},{11,19},{16,24},{1... | collective-permute-start | bytes 1179656 | tf_op jit(solution)/shard_map/ppermute | solution.py:364
  4.8 11.2 %collective-permute-start.1 = (bf16[1536,128]{1,0:T(8,128)(2,1)S(1)}, bf16[1536,128]{1,0:T(8,128)(2,1)S(1)}, u32[]{:S(2)}, u32[]{:S(2)}) collective-permute-start(bf16[1536,128]{1,0:T(8,128)(2,1)S(1)} %bitcast.8), channel_id=1, source_target_pairs={{0,4},{1,5},{2,6},{3,7},{8,0},{9,1},{10,2},{11,3},{16,8},{17,9},{1... | collective-permute-start | bytes 1179656 | tf_op jit(solution)/shard_map/ppermute | solution.py:364
  5.8 3.7 %collective-permute-start.3 = (s32[6,128]{1,0:T(8,128)S(1)}, s32[6,128]{1,0:T(8,128)S(1)}, u32[]{:S(2)}, u32[]{:S(2)}) collective-permute-start(s32[6,128]{1,0:T(8,128)S(1)} %reshape.15.refs_0_), channel_id=1, source_target_pairs={{0,1},{1,0},{2,3},{3,2},{8,9},{9,8},{10,11},{11,10},{16,17},{17,16... | collective-permute-start | bytes 9224 | tf_op jit(solution)/shard_map/ppermute | solution.py:364
  9.5 1.1 %copy-start = (bf16[12,1,256,128]{3,2,1,0:T(8,128)(2,1)S(1)}, bf16[12,1,256,128]{3,2,1,0:T(8,128)(2,1)}, u32[]{:S(2)}) copy-start(bf16[12,1,256,128]{3,2,1,0:T(8,128)(2,1)} %param.4) | copy-start | bytes 2359300
  12.5 16.3 %copy-start.1 = (bf16[256,64,128]{2,1,0:T(8,128)(2,1)S(1)}, bf16[256,64,128]{2,1,0:T(8,128)(2,1)}, u32[]{:S(2)}) copy-start(bf16[256,64,128]{2,1,0:T(8,128)(2,1)} %blocks_ref) | copy-start | bytes 12582916
  12.5 12.3 %collective-permute-start.4 = (bf16[1568,128]{1,0:T(8,128)(2,1)S(1)}, bf16[1568,128]{1,0:T(8,128)(2,1)S(1)}, u32[]{:S(2)}, u32[]{:S(2)}) collective-permute-start(bf16[1568,128]{1,0:T(8,128)(2,1)S(1)} %pack_stream.1.refs_1_), channel_id=1, source_target_pairs={{0,8},{1,9},{2,10},{3,11},{8,16},{9,17},{10,18},{11,19},{16,24},{1... | collective-permute-start | bytes 1204232 | tf_op jit(solution)/shard_map/ppermute | solution.py:364
  14.6 12.2 %collective-permute-start.5 = (bf16[1568,128]{1,0:T(8,128)(2,1)S(1)}, bf16[1568,128]{1,0:T(8,128)(2,1)S(1)}, u32[]{:S(2)}, u32[]{:S(2)}) collective-permute-start(bf16[1568,128]{1,0:T(8,128)(2,1)S(1)} %pack_stream.1.refs_1_), channel_id=1, source_target_pairs={{0,4},{1,5},{2,6},{3,7},{8,0},{9,1},{10,2},{11,3},{16,8},{17,9},{1... | collective-permute-start | bytes 1204232 | tf_op jit(solution)/shard_map/ppermute | solution.py:364
  16.1 19.1 %collective-permute-start.2 = (bf16[1536,128]{1,0:T(8,128)(2,1)S(1)}, bf16[1536,128]{1,0:T(8,128)(2,1)S(1)}, u32[]{:S(2)}, u32[]{:S(2)}) collective-permute-start(bf16[1536,128]{1,0:T(8,128)(2,1)S(1)} %collective-permute-done.refs_0_), channel_id=1, source_target_pairs={{0,8},{1,9},{2,10},{3,11},{8,16},{9,17},{10,18},{11,19},{16,24},{1... | collective-permute-start | bytes 1179656 | tf_op jit(solution)/shard_map/ppermute | solution.py:364
  17.6 17.6 %collective-permute-start.7 = (bf16[1536,128]{1,0:T(8,128)(2,1)S(1)}, bf16[1536,128]{1,0:T(8,128)(2,1)S(1)}, u32[]{:S(2)}, u32[]{:S(2)}) collective-permute-start(bf16[1536,128]{1,0:T(8,128)(2,1)S(1)} %collective-permute-done.1.refs_2_), channel_id=1, source_target_pairs={{0,4},{1,5},{2,6},{3,7},{8,0},{9,1},{10,2},{11,3},{16,8},{17,9},{1... | collective-permute-start | bytes 1179656 | tf_op jit(solution)/shard_map/ppermute | solution.py:364
  26.8 17.0 %collective-permute-start.11 = (bf16[1568,128]{1,0:T(8,128)(2,1)S(1)}, bf16[1568,128]{1,0:T(8,128)(2,1)S(1)}, u32[]{:S(2)}, u32[]{:S(2)}) collective-permute-start(bf16[1568,128]{1,0:T(8,128)(2,1)S(1)} %collective-permute-done.5.refs_3_), channel_id=1, source_target_pairs={{0,4},{1,5},{2,6},{3,7},{8,0},{9,1},{10,2},{11,3},{16,8},{17,9},{1... | collective-permute-start | bytes 1204232 | tf_op jit(solution)/shard_map/ppermute | solution.py:364
  26.8 17.0 %collective-permute-start.10 = (bf16[1568,128]{1,0:T(8,128)(2,1)S(1)}, bf16[1568,128]{1,0:T(8,128)(2,1)S(1)}, u32[]{:S(2)}, u32[]{:S(2)}) collective-permute-start(bf16[1568,128]{1,0:T(8,128)(2,1)S(1)} %collective-permute-done.4.refs_1_), channel_id=1, source_target_pairs={{0,8},{1,9},{2,10},{3,11},{8,16},{9,17},{10,18},{11,19},{16,24},{1... | collective-permute-start | bytes 1204232 | tf_op jit(solution)/shard_map/ppermute | solution.py:364
  35.2 15.0 %collective-permute-start.8 = (bf16[1536,128]{1,0:T(8,128)(2,1)S(1)}, bf16[1536,128]{1,0:T(8,128)(2,1)S(1)}, u32[]{:S(2)}, u32[]{:S(2)}) collective-permute-start(bf16[1536,128]{1,0:T(8,128)(2,1)S(1)} %collective-permute-done.2.refs_0_), channel_id=1, source_target_pairs={{0,8},{1,9},{2,10},{3,11},{8,16},{9,17},{10,18},{11,19},{16,24},{1... | collective-permute-start | bytes 1179656 | tf_op jit(solution)/shard_map/ppermute | solution.py:364
  36.8 15.4 %collective-permute-start.9 = (bf16[1536,128]{1,0:T(8,128)(2,1)S(1)}, bf16[1536,128]{1,0:T(8,128)(2,1)S(1)}, u32[]{:S(2)}, u32[]{:S(2)}) collective-permute-start(bf16[1536,128]{1,0:T(8,128)(2,1)S(1)} %collective-permute-done.7.refs_2_), channel_id=1, source_target_pairs={{0,4},{1,5},{2,6},{3,7},{8,0},{9,1},{10,2},{11,3},{16,8},{17,9},{1... | collective-permute-start | bytes 1179656 | tf_op jit(solution)/shard_map/ppermute | solution.py:364
  43.8 14.9 %collective-permute-start.14 = (bf16[1568,128]{1,0:T(8,128)(2,1)S(1)}, bf16[1568,128]{1,0:T(8,128)(2,1)S(1)}, u32[]{:S(2)}, u32[]{:S(2)}) collective-permute-start(bf16[1568,128]{1,0:T(8,128)(2,1)S(1)} %collective-permute-done.11.refs_3_), channel_id=1, source_target_pairs={{0,4},{1,5},{2,6},{3,7},{8,0},{9,1},{10,2},{11,3},{16,8},{17,9},{1... | collective-permute-start | bytes 1204232 | tf_op jit(solution)/shard_map/ppermute | solution.py:364
  43.8 14.9 %collective-permute-start.13 = (bf16[1568,128]{1,0:T(8,128)(2,1)S(1)}, bf16[1568,128]{1,0:T(8,128)(2,1)S(1)}, u32[]{:S(2)}, u32[]{:S(2)}) collective-permute-start(bf16[1568,128]{1,0:T(8,128)(2,1)S(1)} %collective-permute-done.10.refs_1_), channel_id=1, source_target_pairs={{0,8},{1,9},{2,10},{3,11},{8,16},{9,17},{10,18},{11,19},{16,24},{1... | collective-permute-start | bytes 1204232 | tf_op jit(solution)/shard_map/ppermute | solution.py:364
  58.7 9.3 %collective-permute-start.15 = (bf16[1568,128]{1,0:T(8,128)(2,1)S(1)}, bf16[1568,128]{1,0:T(8,128)(2,1)S(1)}, u32[]{:S(2)}, u32[]{:S(2)}) collective-permute-start(bf16[1568,128]{1,0:T(8,128)(2,1)S(1)} %collective-permute-done.14.refs_3_), channel_id=1, source_target_pairs={{0,4},{1,5},{2,6},{3,7},{8,0},{9,1},{10,2},{11,3},{16,8},{17,9},{1... | collective-permute-start | bytes 1204232 | tf_op jit(solution)/shard_map/ppermute | solution.py:364
  59.0 9.0 %collective-permute-start.12 = (bf16[1536,128]{1,0:T(8,128)(2,1)S(1)}, bf16[1536,128]{1,0:T(8,128)(2,1)S(1)}, u32[]{:S(2)}, u32[]{:S(2)}) collective-permute-start(bf16[1536,128]{1,0:T(8,128)(2,1)S(1)} %collective-permute-done.8.refs_0_), channel_id=1, source_target_pairs={{0,8},{1,9},{2,10},{3,11},{8,16},{9,17},{10,18},{11,19},{16,24},{1... | collective-permute-start | bytes 1179656 | tf_op jit(solution)/shard_map/ppermute | solution.py:364

commit v4 on v3

--- a/solution.py
+++ b/solution.py
@@ -15,7 +15,7 @@
 GROUP = 4
 UCOST = 4000000000
 SCOST = 2.0
-UNROLL = 16
+UNROLL = 20
 PREP = 3
 LAST = (((1,), (1,)), ((), ()))
 

time: 88 us -> 88.3 us (level)
  Pallas kernels: 33.3 us -> 36.2 us
  waiting for transfers between devices: 18.8 us -> 16.2 us
    pallas_call x5, Pallas kernels: 22.5 us -> 25.4 us  [score_chunks(): pl.pallas_call(functools.partial(score_kernel, (plans, len(others), seqs,...]
    ppermute x15, waiting for transfers between devices: 18.8 us -> 16.2 us  [send(): return lax.ppermute(array, ('art', 'seq'), turn(step, across))]
  transfers between devices with their start and end apart: 16 -> 16, of which waited for: 10 -> 9; matrix products, arithmetic and copies ran while one was open for 2% -> 2% of each run, Pallas kernels for 32% -> 35%
where the time goes in v4:
time: 88.3 us; the launch traced here: 88 us
  Pallas kernels  36.2 us (41%)
  starting transfers between devices  17.4 us (20%)
  waiting for transfers between devices  16.2 us (18%)
  blocking collectives  14.3 us (16%)
  local copies, waits for them, and re-layouts  2.42 us (3%)
    pallas_call x5, Pallas kernels, score_chunks(): pl.pallas_call(functools.partial(score_kernel, (plans, len(others), seqs,...  25.4 us
    ppermute x15, starting transfers between devices, send(): return lax.ppermute(array, ('art', 'seq'), turn(step, across))  16.9 us
    ppermute x15, waiting for transfers between devices, send(): return lax.ppermute(array, ('art', 'seq'), turn(step, across))  16.2 us
    all_to_all x1, blocking collectives, per_device(): lax.all_to_all(spread, ('art', 'seq'), split_axis=0, concat_axis=0, tiled...  14.3 us
    pallas_call x2, Pallas kernels, unit_blocks(): pl.pallas_call(functools.partial(unit_kernel, parts), out_shape=jax.Shape...  7.26 us
    pallas_call x1, Pallas kernels, pack_stream(): pl.pallas_call(functools.partial(pack_kernel, chips, blocks), out_shape=j...  1.83 us
  transfers between devices with their start and end apart: 16, of which 9 were waited for; matrix products, arithmetic and copies ran while one was open for 2% of the time, Pallas kernels for 35%

profile of v4, /device:TPU:0, one launch (start us, length us, event | category | flops | bytes accessed | tf_op | source)
XLA Modules:
  0.0 88.0 jit_solution(4951241630545795005)
XLA Ops:
  2.2 2.6 %collective-permute-start = (bf16[1536,128]{1,0:T(8,128)(2,1)S(1)}, bf16[1536,128]{1,0:T(8,128)(2,1)S(1)}, u32[]{:S(2)}, u32[]{:S(2)}) collective-permute-start(bf16[1536,128]{1,0:T(8,128)(2,1)S(1)} %bitcast.7), channel_id=1, source_target_pairs={{0,8},{1,9},{2,10},{3,11},{8,16},{9,17},{10,18},{11,19},{16,24},{1... | collective-permute-start | bytes 1179656 | tf_op jit(solution)/shard_map/ppermute | solution.py:364
  5.8 2.0 %collective-permute-start.3 = (s32[6,128]{1,0:T(8,128)S(1)}, s32[6,128]{1,0:T(8,128)S(1)}, u32[]{:S(2)}, u32[]{:S(2)}) collective-permute-start(s32[6,128]{1,0:T(8,128)S(1)} %reshape.15.refs_0_), channel_id=1, source_target_pairs={{0,1},{1,0},{2,3},{3,2},{8,9},{9,8},{10,11},{11,10},{16,17},{17,16... | collective-permute-start | bytes 9224 | tf_op jit(solution)/shard_map/ppermute | solution.py:364
  7.9 1.6 %collective-permute-done.3.refs_1_ = s32[6,128]{1,0:T(8,128)S(1)} collective-permute-done((s32[6,128]{1,0:T(8,128)S(1)}, s32[6,128]{1,0:T(8,128)S(1)}, u32[]{:S(2)}, u32[]{:S(2)}) %collective-permute-start.3) | collective-permute-done | bytes 3104 | tf_op jit(solution)/shard_map/ppermute | solution.py:364
  10.7 1.8 %pack_stream.1.refs_1_ = bf16[1568,128]{1,0:T(8,128)(2,1)S(1)} custom-call(s32[3]{0:T(128)S(1)} %pad_add_fusion.me_ref, s32[6,128]{1,0:T(8,128)S(1)} %reshape.15.refs_0_, s32[6,128]{1,0:T(8,128)S(1)} %collective-permute-done.3.refs_1_, bf16[3072,128]{1,0:T(8,128)(2,1)S(1)} %bitcast.6), custom_call_target="tpu_custom_call" | custom-call | flops 1 | bytes 1 | tf_op jit(solution)/shard_map/pack_stream/pallas_call | solution.py:142
  12.5 2.1 %collective-permute-start.4 = (bf16[1568,128]{1,0:T(8,128)(2,1)S(1)}, bf16[1568,128]{1,0:T(8,128)(2,1)S(1)}, u32[]{:S(2)}, u32[]{:S(2)}) collective-permute-start(bf16[1568,128]{1,0:T(8,128)(2,1)S(1)} %pack_stream.1.refs_1_), channel_id=1, source_target_pairs={{0,8},{1,9},{2,10},{3,11},{8,16},{9,17},{10,18},{11,19},{16,24},{1... | collective-permute-start | bytes 1204232 | tf_op jit(solution)/shard_map/ppermute | solution.py:364
  14.6 1.5 %collective-permute-done.1.refs_2_ = bf16[1536,128]{1,0:T(8,128)(2,1)S(1)} collective-permute-done((bf16[1536,128]{1,0:T(8,128)(2,1)S(1)}, bf16[1536,128]{1,0:T(8,128)(2,1)S(1)}, u32[]{:S(2)}, u32[]{:S(2)}) %collective-permute-start.1) | collective-permute-done | bytes 393248 | tf_op jit(solution)/shard_map/ppermute | solution.py:364
  16.1 1.6 %collective-permute-start.2 = (bf16[1536,128]{1,0:T(8,128)(2,1)S(1)}, bf16[1536,128]{1,0:T(8,128)(2,1)S(1)}, u32[]{:S(2)}, u32[]{:S(2)}) collective-permute-start(bf16[1536,128]{1,0:T(8,128)(2,1)S(1)} %collective-permute-done.refs_0_), channel_id=1, source_target_pairs={{0,8},{1,9},{2,10},{3,11},{8,16},{9,17},{10,18},{11,19},{16,24},{1... | collective-permute-start | bytes 1179656 | tf_op jit(solution)/shard_map/ppermute | solution.py:364
  18.1 4.1 %unit_blocks.3.refs_3_.refs_5_.refs_10_ = bf16[256,64,128]{2,1,0:T(8,128)(2,1)S(1)} custom-call(bf16[256,64,128]{2,1,0:T(8,128)(2,1)} %collective-permute-done.6.blocks_ref), custom_call_target="tpu_custom_call" | custom-call | flops 4000000000 | bytes 1 | tf_op jit(solution)/shard_map/unit_blocks/pallas_call | solution.py:45
  22.2 2.6 %collective-permute-done.4.refs_1_ = bf16[1568,128]{1,0:T(8,128)(2,1)S(1)} collective-permute-done((bf16[1568,128]{1,0:T(8,128)(2,1)S(1)}, bf16[1568,128]{1,0:T(8,128)(2,1)S(1)}, u32[]{:S(2)}, u32[]{:S(2)}) %collective-permute-start.4) | collective-permute-done | bytes 401440 | tf_op jit(solution)/shard_map/ppermute | solution.py:364
  24.8 2.0 %collective-permute-done.5.refs_3_ = bf16[1568,128]{1,0:T(8,128)(2,1)S(1)} collective-permute-done((bf16[1568,128]{1,0:T(8,128)(2,1)S(1)}, bf16[1568,128]{1,0:T(8,128)(2,1)S(1)}, u32[]{:S(2)}, u32[]{:S(2)}) %collective-permute-start.5) | collective-permute-done | bytes 401440 | tf_op jit(solution)/shard_map/ppermute | solution.py:364
  26.8 2.0 %collective-permute-start.10 = (bf16[1568,128]{1,0:T(8,128)(2,1)S(1)}, bf16[1568,128]{1,0:T(8,128)(2,1)S(1)}, u32[]{:S(2)}, u32[]{:S(2)}) collective-permute-start(bf16[1568,128]{1,0:T(8,128)(2,1)S(1)} %collective-permute-done.4.refs_1_), channel_id=1, source_target_pairs={{0,8},{1,9},{2,10},{3,11},{8,16},{9,17},{10,18},{11,19},{16,24},{1... | collective-permute-start | bytes 1204232 | tf_op jit(solution)/shard_map/ppermute | solution.py:364
  28.8 3.2 %unit_blocks.2.refs_2_.refs_4_.refs_9_ = bf16[256,64,128]{2,1,0:T(8,128)(2,1)S(1)} custom-call(bf16[256,64,128]{2,1,0:T(8,128)(2,1)S(1)} %copy-done.1), custom_call_target="tpu_custom_call" | custom-call | flops 4000000000 | bytes 1 | tf_op jit(solution)/shard_map/unit_blocks/pallas_call | solution.py:45
  32.0 3.5 %score_chunks.5.refs_2_ = f32[12,128]{1,0:T(8,128)S(1)} custom-call(s32[3]{0:T(128)S(1)} %pad_add_fusion.me_ref, bf16[1536,128]{1,0:T(8,128)(2,1)S(1)} %bitcast.9, bf16[1568,128]{1,0:T(8,128)(2,1)S(1)} %pack_stream.1.refs_1_, bf16[256,64,128]{2,1,0:T(8,128)(2,1)S(1)} %unit_blocks.2.refs_2_.refs_4_.refs_9_, ...), custom_call_target="tpu_custom_call" | custom-call | flops 402653184 | bytes 8388608 | tf_op jit(solution)/shard_map/score_chunks/pallas_call | solution.py:286
  35.5 1.6 %collective-permute-start.8 = (bf16[1536,128]{1,0:T(8,128)(2,1)S(1)}, bf16[1536,128]{1,0:T(8,128)(2,1)S(1)}, u32[]{:S(2)}, u32[]{:S(2)}) collective-permute-start(bf16[1536,128]{1,0:T(8,128)(2,1)S(1)} %collective-permute-done.2.refs_0_), channel_id=1, source_target_pairs={{0,8},{1,9},{2,10},{3,11},{8,16},{9,17},{10,18},{11,19},{16,24},{1... | collective-permute-start | bytes 1179656 | tf_op jit(solution)/shard_map/ppermute | solution.py:364
  37.6 5.9 %score_chunks.6 = (f32[12,128]{1,0:T(8,128)S(1)}, f32[12,128]{1,0:T(8,128)S(1)}) custom-call(s32[3]{0:T(128)S(1)} %pad_add_fusion.me_ref, bf16[1536,128]{1,0:T(8,128)(2,1)S(1)} %collective-permute-done.refs_0_, bf16[1568,128]{1,0:T(8,128)(2,1)S(1)} %collective-permute-done.4.refs_1_, bf16[1536,128]{1,0:T(8,128)(2,1)S(1)} %collective-permute-done.1.refs_2_, ...), custom_call_target="tpu_custom_call" | custom-call | flops 805306368 | bytes 8388608 | tf_op jit(solution)/shard_map/score_chunks/pallas_call | solution.py:286
  43.8 2.0 %collective-permute-start.13 = (bf16[1568,128]{1,0:T(8,128)(2,1)S(1)}, bf16[1568,128]{1,0:T(8,128)(2,1)S(1)}, u32[]{:S(2)}, u32[]{:S(2)}) collective-permute-start(bf16[1568,128]{1,0:T(8,128)(2,1)S(1)} %collective-permute-done.10.refs_1_), channel_id=1, source_target_pairs={{0,8},{1,9},{2,10},{3,11},{8,16},{9,17},{10,18},{11,19},{16,24},{1... | collective-permute-start | bytes 1204232 | tf_op jit(solution)/shard_map/ppermute | solution.py:364
  45.9 4.4 %collective-permute-done.8.refs_0_ = bf16[1536,128]{1,0:T(8,128)(2,1)S(1)} collective-permute-done((bf16[1536,128]{1,0:T(8,128)(2,1)S(1)}, bf16[1536,128]{1,0:T(8,128)(2,1)S(1)}, u32[]{:S(2)}, u32[]{:S(2)}) %collective-permute-start.8) | collective-permute-done | bytes 393248 | tf_op jit(solution)/shard_map/ppermute | solution.py:364
  50.2 2.0 %collective-permute-done.9.refs_2_ = bf16[1536,128]{1,0:T(8,128)(2,1)S(1)} collective-permute-done((bf16[1536,128]{1,0:T(8,128)(2,1)S(1)}, bf16[1536,128]{1,0:T(8,128)(2,1)S(1)}, u32[]{:S(2)}, u32[]{:S(2)}) %collective-permute-start.9) | collective-permute-done | bytes 393248 | tf_op jit(solution)/shard_map/ppermute | solution.py:364
  52.3 5.9 %score_chunks.7 = (f32[12,128]{1,0:T(8,128)S(1)}, f32[12,128]{1,0:T(8,128)S(1)}) custom-call(s32[3]{0:T(128)S(1)} %pad_add_fusion.me_ref, bf16[1536,128]{1,0:T(8,128)(2,1)S(1)} %collective-permute-done.2.refs_0_, bf16[1568,128]{1,0:T(8,128)(2,1)S(1)} %collective-permute-done.10.refs_1_, bf16[1536,128]{1,0:T(8,128)(2,1)S(1)} %collective-permute-done.7.refs_2_, ...), custom_call_target="tpu_custom_call" | custom-call | flops 805306368 | bytes 8388608 | tf_op jit(solution)/shard_map/score_chunks/pallas_call | solution.py:286
  59.0 1.7 %collective-permute-start.12 = (bf16[1536,128]{1,0:T(8,128)(2,1)S(1)}, bf16[1536,128]{1,0:T(8,128)(2,1)S(1)}, u32[]{:S(2)}, u32[]{:S(2)}) collective-permute-start(bf16[1536,128]{1,0:T(8,128)(2,1)S(1)} %collective-permute-done.8.refs_0_), channel_id=1, source_target_pairs={{0,8},{1,9},{2,10},{3,11},{8,16},{9,17},{10,18},{11,19},{16,24},{1... | collective-permute-start | bytes 1179656 | tf_op jit(solution)/shard_map/ppermute | solution.py:364
  60.7 6.1 %score_chunks.8 = (f32[12,128]{1,0:T(8,128)S(1)}, f32[12,128]{1,0:T(8,128)S(1)}) custom-call(s32[3]{0:T(128)S(1)} %pad_add_fusion.me_ref, bf16[1536,128]{1,0:T(8,128)(2,1)S(1)} %collective-permute-done.8.refs_0_, bf16[1568,128]{1,0:T(8,128)(2,1)S(1)} %collective-permute-done.13.refs_1_, bf16[1536,128]{1,0:T(8,128)(2,1)S(1)} %collective-permute-done.9.refs_2_, ...), custom_call_target="tpu_custom_call" | custom-call | flops 805306368 | bytes 8388608 | tf_op jit(solution)/shard_map/score_chunks/pallas_call | solution.py:286
  68.0 4.1 %score_chunks.9 = (f32[12,128]{1,0:T(8,128)}, f32[256,128]{1,0:T(8,128)S(1)}) custom-call(s32[3]{0:T(128)S(1)} %pad_add_fusion.me_ref, bf16[1536,128]{1,0:T(8,128)(2,1)S(1)} %collective-permute-done.12.refs_0_, bf16[1568,128]{1,0:T(8,128)(2,1)S(1)} %collective-permute-done.15.refs_1_, f32[12,128]{1,0:T(8,128)S(1)} %score_chunks.5.refs_2_, ...), custom_call_target="tpu_custom_call" | custom-call | flops 402653184 | bytes 8388608 | tf_op jit(solution)/shard_map/score_chunks/pallas_call | solution.py:286
  72.1 14.3 %all_to_all.9.parts_ref = f32[32,8,128]{2,1,0:T(8,128)} all-to-all(f32[32,8,128]{2,1,0:T(8,128)S(1)} %bitcast.10), channel_id=1, replica_groups=mesh['art'=16,'seq'=2] {'art','seq'}, dimensions={0} | all-to-all | bytes 262144 | tf_op jit(solution)/shard_map/all_to_all | solution.py:411
  86.3 1.7 %close.1 = (f32[12,64]{1,0:T(8,128)}, f32[12,64]{1,0:T(8,128)}) custom-call(f32[32,8,128]{2,1,0:T(8,128)} %all_to_all.9.parts_ref), custom_call_target="tpu_custom_call" | custom-call | tf_op jit(solution)/shard_map/close/pallas_call | solution.py:327
  (27 shorter events, 7.1 us)
Async XLA Ops:
  0.6 17.5 %collective-permute-start.6 = (bf16[256,64,128]{2,1,0:T(8,128)(2,1)}, bf16[256,64,128]{2,1,0:T(8,128)(2,1)}, u32[]{:S(2)}, u32[]{:S(2)}) collective-permute-start(bf16[256,64,128]{2,1,0:T(8,128)(2,1)} %blocks_ref), channel_id=1, source_target_pairs={{0,2},{2,0},{4,6},{6,4},{8,10},{10,8},{12,14},{14,12},{16,18},{18,... | collective-permute-start | bytes 12582920 | tf_op jit(solution)/shard_map/ppermute | solution.py:379
  2.2 12.4 %collective-permute-start = (bf16[1536,128]{1,0:T(8,128)(2,1)S(1)}, bf16[1536,128]{1,0:T(8,128)(2,1)S(1)}, u32[]{:S(2)}, u32[]{:S(2)}) collective-permute-start(bf16[1536,128]{1,0:T(8,128)(2,1)S(1)} %bitcast.7), channel_id=1, source_target_pairs={{0,8},{1,9},{2,10},{3,11},{8,16},{9,17},{10,18},{11,19},{16,24},{1... | collective-permute-start | bytes 1179656 | tf_op jit(solution)/shard_map/ppermute | solution.py:364
  4.8 11.2 %collective-permute-start.1 = (bf16[1536,128]{1,0:T(8,128)(2,1)S(1)}, bf16[1536,128]{1,0:T(8,128)(2,1)S(1)}, u32[]{:S(2)}, u32[]{:S(2)}) collective-permute-start(bf16[1536,128]{1,0:T(8,128)(2,1)S(1)} %bitcast.8), channel_id=1, source_target_pairs={{0,4},{1,5},{2,6},{3,7},{8,0},{9,1},{10,2},{11,3},{16,8},{17,9},{1... | collective-permute-start | bytes 1179656 | tf_op jit(solution)/shard_map/ppermute | solution.py:364
  5.8 3.7 %collective-permute-start.3 = (s32[6,128]{1,0:T(8,128)S(1)}, s32[6,128]{1,0:T(8,128)S(1)}, u32[]{:S(2)}, u32[]{:S(2)}) collective-permute-start(s32[6,128]{1,0:T(8,128)S(1)} %reshape.15.refs_0_), channel_id=1, source_target_pairs={{0,1},{1,0},{2,3},{3,2},{8,9},{9,8},{10,11},{11,10},{16,17},{17,16... | collective-permute-start | bytes 9224 | tf_op jit(solution)/shard_map/ppermute | solution.py:364
  9.5 1.1 %copy-start = (bf16[12,1,256,128]{3,2,1,0:T(8,128)(2,1)S(1)}, bf16[12,1,256,128]{3,2,1,0:T(8,128)(2,1)}, u32[]{:S(2)}) copy-start(bf16[12,1,256,128]{3,2,1,0:T(8,128)(2,1)} %param.4) | copy-start | bytes 2359300
  12.5 16.3 %copy-start.1 = (bf16[256,64,128]{2,1,0:T(8,128)(2,1)S(1)}, bf16[256,64,128]{2,1,0:T(8,128)(2,1)}, u32[]{:S(2)}) copy-start(bf16[256,64,128]{2,1,0:T(8,128)(2,1)} %blocks_ref) | copy-start | bytes 12582916
  12.5 12.3 %collective-permute-start.4 = (bf16[1568,128]{1,0:T(8,128)(2,1)S(1)}, bf16[1568,128]{1,0:T(8,128)(2,1)S(1)}, u32[]{:S(2)}, u32[]{:S(2)}) collective-permute-start(bf16[1568,128]{1,0:T(8,128)(2,1)S(1)} %pack_stream.1.refs_1_), channel_id=1, source_target_pairs={{0,8},{1,9},{2,10},{3,11},{8,16},{9,17},{10,18},{11,19},{16,24},{1... | collective-permute-start | bytes 1204232 | tf_op jit(solution)/shard_map/ppermute | solution.py:364
  14.6 12.2 %collective-permute-start.5 = (bf16[1568,128]{1,0:T(8,128)(2,1)S(1)}, bf16[1568,128]{1,0:T(8,128)(2,1)S(1)}, u32[]{:S(2)}, u32[]{:S(2)}) collective-permute-start(bf16[1568,128]{1,0:T(8,128)(2,1)S(1)} %pack_stream.1.refs_1_), channel_id=1, source_target_pairs={{0,4},{1,5},{2,6},{3,7},{8,0},{9,1},{10,2},{11,3},{16,8},{17,9},{1... | collective-permute-start | bytes 1204232 | tf_op jit(solution)/shard_map/ppermute | solution.py:364
  16.1 19.4 %collective-permute-start.2 = (bf16[1536,128]{1,0:T(8,128)(2,1)S(1)}, bf16[1536,128]{1,0:T(8,128)(2,1)S(1)}, u32[]{:S(2)}, u32[]{:S(2)}) collective-permute-start(bf16[1536,128]{1,0:T(8,128)(2,1)S(1)} %collective-permute-done.refs_0_), channel_id=1, source_target_pairs={{0,8},{1,9},{2,10},{3,11},{8,16},{9,17},{10,18},{11,19},{16,24},{1... | collective-permute-start | bytes 1179656 | tf_op jit(solution)/shard_map/ppermute | solution.py:364
  17.6 17.9 %collective-permute-start.7 = (bf16[1536,128]{1,0:T(8,128)(2,1)S(1)}, bf16[1536,128]{1,0:T(8,128)(2,1)S(1)}, u32[]{:S(2)}, u32[]{:S(2)}) collective-permute-start(bf16[1536,128]{1,0:T(8,128)(2,1)S(1)} %collective-permute-done.1.refs_2_), channel_id=1, source_target_pairs={{0,4},{1,5},{2,6},{3,7},{8,0},{9,1},{10,2},{11,3},{16,8},{17,9},{1... | collective-permute-start | bytes 1179656 | tf_op jit(solution)/shard_map/ppermute | solution.py:364
  26.8 17.0 %collective-permute-start.11 = (bf16[1568,128]{1,0:T(8,128)(2,1)S(1)}, bf16[1568,128]{1,0:T(8,128)(2,1)S(1)}, u32[]{:S(2)}, u32[]{:S(2)}) collective-permute-start(bf16[1568,128]{1,0:T(8,128)(2,1)S(1)} %collective-permute-done.5.refs_3_), channel_id=1, source_target_pairs={{0,4},{1,5},{2,6},{3,7},{8,0},{9,1},{10,2},{11,3},{16,8},{17,9},{1... | collective-permute-start | bytes 1204232 | tf_op jit(solution)/shard_map/ppermute | solution.py:364
  26.8 17.0 %collective-permute-start.10 = (bf16[1568,128]{1,0:T(8,128)(2,1)S(1)}, bf16[1568,128]{1,0:T(8,128)(2,1)S(1)}, u32[]{:S(2)}, u32[]{:S(2)}) collective-permute-start(bf16[1568,128]{1,0:T(8,128)(2,1)S(1)} %collective-permute-done.4.refs_1_), channel_id=1, source_target_pairs={{0,8},{1,9},{2,10},{3,11},{8,16},{9,17},{10,18},{11,19},{16,24},{1... | collective-permute-start | bytes 1204232 | tf_op jit(solution)/shard_map/ppermute | solution.py:364
  35.5 14.7 %collective-permute-start.8 = (bf16[1536,128]{1,0:T(8,128)(2,1)S(1)}, bf16[1536,128]{1,0:T(8,128)(2,1)S(1)}, u32[]{:S(2)}, u32[]{:S(2)}) collective-permute-start(bf16[1536,128]{1,0:T(8,128)(2,1)S(1)} %collective-permute-done.2.refs_0_), channel_id=1, source_target_pairs={{0,8},{1,9},{2,10},{3,11},{8,16},{9,17},{10,18},{11,19},{16,24},{1... | collective-permute-start | bytes 1179656 | tf_op jit(solution)/shard_map/ppermute | solution.py:364
  37.1 15.1 %collective-permute-start.9 = (bf16[1536,128]{1,0:T(8,128)(2,1)S(1)}, bf16[1536,128]{1,0:T(8,128)(2,1)S(1)}, u32[]{:S(2)}, u32[]{:S(2)}) collective-permute-start(bf16[1536,128]{1,0:T(8,128)(2,1)S(1)} %collective-permute-done.7.refs_2_), channel_id=1, source_target_pairs={{0,4},{1,5},{2,6},{3,7},{8,0},{9,1},{10,2},{11,3},{16,8},{17,9},{1... | collective-permute-start | bytes 1179656 | tf_op jit(solution)/shard_map/ppermute | solution.py:364
  43.8 14.9 %collective-permute-start.14 = (bf16[1568,128]{1,0:T(8,128)(2,1)S(1)}, bf16[1568,128]{1,0:T(8,128)(2,1)S(1)}, u32[]{:S(2)}, u32[]{:S(2)}) collective-permute-start(bf16[1568,128]{1,0:T(8,128)(2,1)S(1)} %collective-permute-done.11.refs_3_), channel_id=1, source_target_pairs={{0,4},{1,5},{2,6},{3,7},{8,0},{9,1},{10,2},{11,3},{16,8},{17,9},{1... | collective-permute-start | bytes 1204232 | tf_op jit(solution)/shard_map/ppermute | solution.py:364
  43.8 14.9 %collective-permute-start.13 = (bf16[1568,128]{1,0:T(8,128)(2,1)S(1)}, bf16[1568,128]{1,0:T(8,128)(2,1)S(1)}, u32[]{:S(2)}, u32[]{:S(2)}) collective-permute-start(bf16[1568,128]{1,0:T(8,128)(2,1)S(1)} %collective-permute-done.10.refs_1_), channel_id=1, source_target_pairs={{0,8},{1,9},{2,10},{3,11},{8,16},{9,17},{10,18},{11,19},{16,24},{1... | collective-permute-start | bytes 1204232 | tf_op jit(solution)/shard_map/ppermute | solution.py:364
  58.7 9.3 %collective-permute-start.15 = (bf16[1568,128]{1,0:T(8,128)(2,1)S(1)}, bf16[1568,128]{1,0:T(8,128)(2,1)S(1)}, u32[]{:S(2)}, u32[]{:S(2)}) collective-permute-start(bf16[1568,128]{1,0:T(8,128)(2,1)S(1)} %collective-permute-done.14.refs_3_), channel_id=1, source_target_pairs={{0,4},{1,5},{2,6},{3,7},{8,0},{9,1},{10,2},{11,3},{16,8},{17,9},{1... | collective-permute-start | bytes 1204232 | tf_op jit(solution)/shard_map/ppermute | solution.py:364
  59.0 9.0 %collective-permute-start.12 = (bf16[1536,128]{1,0:T(8,128)(2,1)S(1)}, bf16[1536,128]{1,0:T(8,128)(2,1)S(1)}, u32[]{:S(2)}, u32[]{:S(2)}) collective-permute-start(bf16[1536,128]{1,0:T(8,128)(2,1)S(1)} %collective-permute-done.8.refs_0_), channel_id=1, source_target_pairs={{0,8},{1,9},{2,10},{3,11},{8,16},{9,17},{10,18},{11,19},{16,24},{1... | collective-permute-start | bytes 1179656 | tf_op jit(solution)/shard_map/ppermute | solution.py:364

commit v5 on v4

--- a/solution.py
+++ b/solution.py
@@ -67,12 +67,13 @@
 
 
 def pack_kernel(chips, blocks, me_ref, *refs):
-    id_refs, query_ref, out_ref = refs[:-2], refs[-2], refs[-1]
+    id_refs, (query_ref, ahead_ref, behind_ref, lists_ref) = refs[:-4], refs[-4:]
     seqs = len(id_refs)
     core, seq = me_ref[1], me_ref[2]
     per_home, width = id_refs[0].shape
-    rows = query_ref.shape[0]
-    out_ref[0:rows, :] = query_ref[...]
+    rows = query_ref.shape[0] // 2
+    ahead_ref[0:rows, :] = query_ref[rows : 2 * rows, :]
+    behind_ref[0:rows, :] = query_ref[0:rows, :]
 
     lane = lax.broadcasted_iota(jnp.int32, (per_home, width), 1)
     ids = jnp.zeros((per_home, width), jnp.int32)
@@ -131,32 +132,33 @@
     lists = jnp.concatenate([got[0:1], code, got[2:3]], axis=1)
     lists = [lists[:, i * 128 : (i + 1) * 128] for i in range(3 * entries)]
     lists += [starts, jnp.zeros((extra - 3 * entries - 1, 128), jnp.float32)]
-    out_ref[rows : rows + extra, :] = jnp.concatenate(lists, axis=0).astype(jnp.bfloat16)
-
-
-def pack_stream(me, ids, query, chips, blocks):
+    lists = jnp.concatenate(lists, axis=0).astype(jnp.bfloat16)
+    ahead_ref[rows : rows + extra, :] = lists
+    behind_ref[rows : rows + extra, :] = lists
+    lists_ref[...] = lists
+
+
+def pack_streams(me, ids, query, chips, blocks):
     vmem = pl.BlockSpec(memory_space=pltpu.VMEM)
     articles = len(ids) * ids[0].shape[0]
-    half = query.shape[0] // 2
-    rows = half + plan_rows(chips, articles)[1]
+    extra = plan_rows(chips, articles)[1]
+    shapes = [(query.shape[0] // 2 + extra, query.shape[1])] * 2 + [(extra, query.shape[1])]
     return pl.pallas_call(
         functools.partial(pack_kernel, chips, blocks),
-        out_shape=jax.ShapeDtypeStruct((rows, query.shape[1]), jnp.bfloat16),
-        grid=(1,),
-        in_specs=[pl.BlockSpec(memory_space=pltpu.SMEM)]
-        + [vmem] * len(ids)
-        + [pl.BlockSpec((half, query.shape[1]), lambda i: (1, 0))],
-        out_specs=vmem,
+        out_shape=[jax.ShapeDtypeStruct(shape, jnp.bfloat16) for shape in shapes],
+        in_specs=[pl.BlockSpec(memory_space=pltpu.SMEM)] + [vmem] * (len(ids) + 1),
+        out_specs=[vmem] * 3,
         compiler_params=pltpu.CompilerParams(vmem_limit_bytes=32 * 1024 * 1024),
         cost_estimate=pl.CostEstimate(flops=1, bytes_accessed=1, transcendentals=0),
-        name="pack_stream",
+        name="pack_streams",
     )(me, *ids, query)
 
 
 def score_kernel(dims, me_ref, *refs):
-    plans, others, seqs, blocks, wide, deep = dims
+    plans, apart, others, seqs, blocks, wide, deep = dims
     chips = wide * deep
     pair_refs, refs = refs[: 2 * plans], refs[2 * plans :]
+    far_refs, refs = refs[:apart], refs[apart:]
     other_refs, refs = refs[:others], refs[others:]
     own_ref, other_ref, *refs = refs
     out_refs = refs[:-6]
@@ -171,7 +173,8 @@
 
     copies = []
     for p in range(plans):
-        rows = pair_refs[2 * p + 1][begin : begin + extra, :].astype(jnp.float32).astype(jnp.int32)
+        rows = far_refs[0][...] if apart else pair_refs[2 * p + 1][begin : begin + extra, :]
+        rows = rows.astype(jnp.float32).astype(jnp.int32)
         local, code, article, starts = (rows[k * entries : (k + 1) * entries] for k in range(4))
         place = code % 128
         row = jnp.where(place < NC, article * NC + place, articles * NC)
@@ -192,7 +195,8 @@
                 LAST,
                 preferred_element_type=jnp.float32,
             )
-            at = p * (articles // 2) + i
+            late = p % 2 if p < 2 else 1 - p % 2
+            at = p // 2 * articles + late * (articles // 2) + i
             scale_ref[at] = lax.rsqrt(norm + EPS) * (SHARP * math.log2(math.e))
             turned_ref[at] = query.T
         return carry
@@ -271,7 +275,7 @@
             spread_ref[rows, :] = ref[k * per_home : (k + 1) * per_home, :]
 
 
-def score_chunks(me, pairs, others, own, other, tokens, wide, deep, seqs):
+def score_chunks(me, pairs, far, others, own, other, tokens, wide, deep, seqs):
     chips = wide * deep
     plans = len(pairs)
     blocks, keys, width = own.shape
@@ -284,9 +288,9 @@
     work = plans * articles * 8
     smem, vmem = pl.BlockSpec(memory_space=pltpu.SMEM), pl.BlockSpec(memory_space=pltpu.VMEM)
     return pl.pallas_call(
-        functools.partial(score_kernel, (plans, len(others), seqs, blocks, wide, deep)),
+        functools.partial(score_kernel, (plans, len(far), len(others), seqs, blocks, wide, deep)),
         out_shape=shapes,
-        in_specs=[smem] + [vmem] * (2 * plans + len(others) + 2),
+        in_specs=[smem] + [vmem] * (2 * plans + len(far) + len(others) + 2),
         out_specs=[vmem] * len(shapes),
         scratch_shapes=[
             pltpu.VMEM((plans * articles, width, tokens), jnp.bfloat16),
@@ -303,7 +307,7 @@
             transcendentals=int(SCOST / 2 * work * tokens * keys),
         ),
         name="score_chunks",
-    )(me, *[x for pair in pairs for x in pair], *others, own, other)
+    )(me, *[x for pair in pairs for x in pair], *far, *others, own, other)
 
 
 def close_kernel(seqs, parts_ref, relevance_ref, probs_ref, score_ref):
@@ -365,49 +369,49 @@
 
     cut = articles // 2 * tokens
     one = mine[:cut]
-    ahead, behind = [[one, None]], [[one, None]]
-    first = [send(one, 1), send(one, -1)]
+    ahead, behind = [None], [None]
+    first = [send(one, 1), send(mine[cut:], -1)]
 
     ids = (cand_owner * blocks + cand_local).reshape(per_home, seqs * NC)
     ids = [ids] + [send(ids, 0, d) for d in range(1, seqs)]
     me = jnp.stack([art // 2, art % 2, seq]).astype(jnp.int32)
-    two = pack_stream(me, ids, mine, chips, blocks)
-    second = [send(two, 1), send(two, -1)]
+    two, back, lists = pack_streams(me, ids, mine, chips, blocks)
+    second = [send(two, 1), send(back, -1)]
     ahead.append([first[0], second[0]])
     behind.append([first[1], second[1]])
     own = unit_blocks(lax.optimization_barrier((companies, *first))[0])
     other = lax.ppermute(companies, "art", [(i, i ^ 1) for i in range(arts)])
     other = unit_blocks(lax.optimization_barrier((other, *first))[0])
 
-    def score(*pairs, others=()):
-        return score_chunks(me, pairs, others, own, other, tokens, wide, deep, seqs)
+    def score(*pairs, far=(), others=()):
+        return score_chunks(me, pairs, far, others, own, other, tokens, wide, deep, seqs)
 
     def after(array, *things):
         return lax.optimization_barrier((array, *things))[0]
 
     early = list(score((after(one, *second), two)))
     done = early[0]
+    far = send(after(lists, done), half)
     for d in range(1, half):
         a, b = [ahead[d][0], behind[d][0]], [ahead[d][1], behind[d][1]]
         if d == 1:
-            b = [after(x, other) for x in b]
+            b = [after(x, own) for x in b]
         else:
-            fresh = after(ahead[d - 1][0], done, *a)
+            fresh = after(ahead[d - 1][0], done, *a, *([far] if d == 3 else []))
             more = score((fresh, ahead[d - 1][1]), behind[d - 1])
             early += more
             a = [after(x, done if d + 1 < half else more[0]) for x in a]
             b = [after(x, more[0]) for x in b]
             done = more[0]
         a, b = lax.optimization_barrier(a), lax.optimization_barrier(b)
-        if d + 1 == half:
-            ahead[d], behind[d] = [a[0], b[0]], [a[1], b[1]]
         if d + 1 < half:
             ahead.append([send(a[0], 1), send(b[0], 1)])
             behind.append([send(a[1], -1), send(b[1], -1)])
         else:
-            last = (send(a[0], 1), send(b[1], -1))
+            ahead[d][0] = a[0]
+            last = (send(a[0], 1), send(a[1], -1))
     early += score(ahead[half - 1], behind[half - 1])
-    spread = score(last, others=early)[1]
+    spread = score(last, far=(far,), others=early)[1]
     parts = lax.all_to_all(spread, ("art", "seq"), split_axis=0, concat_axis=0, tiled=True)
     return tuple(close(parts.reshape(arts * seqs, -1, 128), articles, seqs))
 

time: 88.3 us -> 87.2 us (0.988)
  waiting for transfers between devices: 16.2 us -> 11.7 us
  starting transfers between devices: 17.4 us -> 21.1 us
  local copies, waits for them, and re-layouts: 2.42 us -> 4.74 us
  Pallas kernels: 36.2 us -> 34.2 us
    ppermute x15 -> x16, waiting for transfers between devices: 16.2 us -> 11.6 us  [send(): return lax.ppermute(array, ('art', 'seq'), turn(step, across))]
    ppermute x15 -> x16, starting transfers between devices: 16.9 us -> 20.5 us  [send(): return lax.ppermute(array, ('art', 'seq'), turn(step, across))]
    unnamed x4, local copies, waits for them, and re-layouts: 1.14 us -> 3.32 us
    pallas_call x6, Pallas kernels: 27.2 us -> 25.2 us  [the longest x5 23.4 us: score_chunks(): pl.pallas_call(functools.partial(score_kernel, (plans, len(far), len(othe...]
  transfers between devices with their start and end apart: 16 -> 17, of which waited for: 9 -> 6; matrix products, arithmetic and copies ran while one was open for 2% -> 3% of each run, Pallas kernels for 35% -> 33%
where the time goes in v5:
time: 87.2 us; the launch traced here: 86.9 us
  Pallas kernels  34.2 us (39%)
  starting transfers between devices  21.1 us (24%)
  blocking collectives  13.7 us (16%)
  waiting for transfers between devices  11.7 us (13%)
  local copies, waits for them, and re-layouts  4.74 us (5%)
    pallas_call x5, Pallas kernels, score_chunks(): pl.pallas_call(functools.partial(score_kernel, (plans, len(far), len(othe...  23.4 us
    ppermute x16, starting transfers between devices, send(): return lax.ppermute(array, ('art', 'seq'), turn(step, across))  20.5 us
    all_to_all x1, blocking collectives, per_device(): lax.all_to_all(spread, ('art', 'seq'), split_axis=0, concat_axis=0, tiled...  13.7 us
    ppermute x16, waiting for transfers between devices, send(): return lax.ppermute(array, ('art', 'seq'), turn(step, across))  11.6 us
    pallas_call x2, Pallas kernels, unit_blocks(): pl.pallas_call(functools.partial(unit_kernel, parts), out_shape=jax.Shape...  7.26 us
    unnamed x4, local copies, waits for them, and re-layouts  3.32 us
    pallas_call x1, Pallas kernels, pack_streams(): pl.pallas_call(functools.partial(pack_kernel, chips, blocks), out_shape=[...  1.85 us
  transfers between devices with their start and end apart: 17, of which 6 were waited for; matrix products, arithmetic and copies ran while one was open for 3% of the time, Pallas kernels for 33%

profile of v5, /device:TPU:0, one launch (start us, length us, event | category | flops | bytes accessed | tf_op | source)
XLA Modules:
  0.0 86.9 jit_solution(18396042045118687886)
XLA Ops:
  2.3 2.6 %collective-permute-start = (bf16[1536,128]{1,0:T(8,128)(2,1)S(1)}, bf16[1536,128]{1,0:T(8,128)(2,1)S(1)}, u32[]{:S(2)}, u32[]{:S(2)}) collective-permute-start(bf16[1536,128]{1,0:T(8,128)(2,1)S(1)} %bitcast.8), channel_id=1, source_target_pairs={{0,8},{1,9},{2,10},{3,11},{8,16},{9,17},{10,18},{11,19},{16,24},{1... | collective-permute-start | bytes 1179656 | tf_op jit(solution)/shard_map/ppermute | solution.py:368
  6.0 2.0 %collective-permute-start.3 = (s32[6,128]{1,0:T(8,128)S(1)}, s32[6,128]{1,0:T(8,128)S(1)}, u32[]{:S(2)}, u32[]{:S(2)}) collective-permute-start(s32[6,128]{1,0:T(8,128)S(1)} %reshape.16.refs_0_), channel_id=1, source_target_pairs={{0,1},{1,0},{2,3},{3,2},{8,9},{9,8},{10,11},{11,10},{16,17},{17,16... | collective-permute-start | bytes 9224 | tf_op jit(solution)/shard_map/ppermute | solution.py:368
  8.1 1.6 %collective-permute-done.3.refs_1_ = s32[6,128]{1,0:T(8,128)S(1)} collective-permute-done((s32[6,128]{1,0:T(8,128)S(1)}, s32[6,128]{1,0:T(8,128)S(1)}, u32[]{:S(2)}, u32[]{:S(2)}) %collective-permute-start.3) | collective-permute-done | bytes 3104 | tf_op jit(solution)/shard_map/ppermute | solution.py:368
  10.8 1.8 %pack_streams.1 = (bf16[1568,128]{1,0:T(8,128)(2,1)S(1)}, bf16[1568,128]{1,0:T(8,128)(2,1)S(1)}, bf16[32,128]{1,0:T(8,128)(2,1)S(1)}) custom-call(s32[3]{0:T(128)S(1)} %pad_add_fusion.me_ref, s32[6,128]{1,0:T(8,128)S(1)} %reshape.16.refs_0_, s32[6,128]{1,0:T(8,128)S(1)} %collective-permute-done.3.refs_1_, bf16[3072,128]{1,0:T(8,128)(2,1)S(1)} %bitcast.7), custom_call_target="tpu_custom_call" | custom-call | flops 1 | bytes 1 | tf_op jit(solution)/shard_map/pack_streams/pallas_call | solution.py:146
  12.6 2.1 %collective-permute-start.4 = (bf16[1568,128]{1,0:T(8,128)(2,1)S(1)}, bf16[1568,128]{1,0:T(8,128)(2,1)S(1)}, u32[]{:S(2)}, u32[]{:S(2)}) collective-permute-start(bf16[1568,128]{1,0:T(8,128)(2,1)S(1)} %get-tuple-element.37.refs_1_), channel_id=1, source_target_pairs={{0,8},{1,9},{2,10},{3,11},{8,16},{9,17},{10,18},{11,19},{16,24},{1... | collective-permute-start | bytes 1204232 | tf_op jit(solution)/shard_map/ppermute | solution.py:368
  14.7 1.5 %collective-permute-done.1.refs_2_ = bf16[1536,128]{1,0:T(8,128)(2,1)S(1)} collective-permute-done((bf16[1536,128]{1,0:T(8,128)(2,1)S(1)}, bf16[1536,128]{1,0:T(8,128)(2,1)S(1)}, u32[]{:S(2)}, u32[]{:S(2)}) %collective-permute-start.1) | collective-permute-done | bytes 393248 | tf_op jit(solution)/shard_map/ppermute | solution.py:368
  16.2 1.6 %collective-permute-start.2 = (bf16[1536,128]{1,0:T(8,128)(2,1)S(1)}, bf16[1536,128]{1,0:T(8,128)(2,1)S(1)}, u32[]{:S(2)}, u32[]{:S(2)}) collective-permute-start(bf16[1536,128]{1,0:T(8,128)(2,1)S(1)} %collective-permute-done.refs_0_), channel_id=1, source_target_pairs={{0,8},{1,9},{2,10},{3,11},{8,16},{9,17},{10,18},{11,19},{16,24},{1... | collective-permute-start | bytes 1179656 | tf_op jit(solution)/shard_map/ppermute | solution.py:368
  18.3 2.2 %copy-done.1 = bf16[256,64,128]{2,1,0:T(8,128)(2,1)S(1)} copy-done((bf16[256,64,128]{2,1,0:T(8,128)(2,1)S(1)}, bf16[256,64,128]{2,1,0:T(8,128)(2,1)}, u32[]{:S(2)}) %copy-start.1) | copy-done | bytes 4194328
  20.4 3.2 %unit_blocks.2.refs_2_.refs_4_.refs_10_ = bf16[256,64,128]{2,1,0:T(8,128)(2,1)S(1)} custom-call(bf16[256,64,128]{2,1,0:T(8,128)(2,1)S(1)} %copy-done.1), custom_call_target="tpu_custom_call" | custom-call | flops 4000000000 | bytes 1 | tf_op jit(solution)/shard_map/unit_blocks/pallas_call | solution.py:45
  24.9 2.0 %collective-permute-done.5.refs_3_ = bf16[1568,128]{1,0:T(8,128)(2,1)S(1)} collective-permute-done((bf16[1568,128]{1,0:T(8,128)(2,1)S(1)}, bf16[1568,128]{1,0:T(8,128)(2,1)S(1)}, u32[]{:S(2)}, u32[]{:S(2)}) %collective-permute-start.5) | collective-permute-done | bytes 401440 | tf_op jit(solution)/shard_map/ppermute | solution.py:368
  26.9 2.0 %collective-permute-start.11 = (bf16[1568,128]{1,0:T(8,128)(2,1)S(1)}, bf16[1568,128]{1,0:T(8,128)(2,1)S(1)}, u32[]{:S(2)}, u32[]{:S(2)}) collective-permute-start(bf16[1568,128]{1,0:T(8,128)(2,1)S(1)} %collective-permute-done.4.refs_1_), channel_id=1, source_target_pairs={{0,8},{1,9},{2,10},{3,11},{8,16},{9,17},{10,18},{11,19},{16,24},{1... | collective-permute-start | bytes 1204232 | tf_op jit(solution)/shard_map/ppermute | solution.py:368
  29.0 4.1 %unit_blocks.3.refs_3_.refs_5_.refs_11_ = bf16[256,64,128]{2,1,0:T(8,128)(2,1)S(1)} custom-call(bf16[256,64,128]{2,1,0:T(8,128)(2,1)} %collective-permute-done.6.blocks_ref), custom_call_target="tpu_custom_call" | custom-call | flops 4000000000 | bytes 1 | tf_op jit(solution)/shard_map/unit_blocks/pallas_call | solution.py:45
  33.1 3.5 %score_chunks.5.refs_3_ = f32[12,128]{1,0:T(8,128)S(1)} custom-call(s32[3]{0:T(128)S(1)} %pad_add_fusion.me_ref, bf16[1536,128]{1,0:T(8,128)(2,1)S(1)} %bitcast.9, bf16[1568,128]{1,0:T(8,128)(2,1)S(1)} %get-tuple-element.37.refs_1_, bf16[256,64,128]{2,1,0:T(8,128)(2,1)S(1)} %unit_blocks.2.refs_2_.refs_4_.refs_10_, ...), custom_call_target="tpu_custom_call" | custom-call | flops 402653184 | bytes 8388608 | tf_op jit(solution)/shard_map/score_chunks/pallas_call | solution.py:290
  36.6 1.6 %collective-permute-start.8 = (bf16[1536,128]{1,0:T(8,128)(2,1)S(1)}, bf16[1536,128]{1,0:T(8,128)(2,1)S(1)}, u32[]{:S(2)}, u32[]{:S(2)}) collective-permute-start(bf16[1536,128]{1,0:T(8,128)(2,1)S(1)} %collective-permute-done.2.refs_0_), channel_id=1, source_target_pairs={{0,8},{1,9},{2,10},{3,11},{8,16},{9,17},{10,18},{11,19},{16,24},{1... | collective-permute-start | bytes 1179656 | tf_op jit(solution)/shard_map/ppermute | solution.py:368
  38.7 3.4 %collective-permute-start.10 = (bf16[32,128]{1,0:T(8,128)(2,1)S(1)}, bf16[32,128]{1,0:T(8,128)(2,1)S(1)}, u32[]{:S(2)}, u32[]{:S(2)}) collective-permute-start(bf16[32,128]{1,0:T(8,128)(2,1)S(1)} %get-tuple-element.50), channel_id=1, source_target_pairs={{0,28},{1,29},{2,30},{3,31},{8,20},{9,21},{10,22},{11,23},{16,12},... | collective-permute-start | bytes 24584 | tf_op jit(solution)/shard_map/ppermute | solution.py:368
  42.1 4.9 %score_chunks.6 = (f32[12,128]{1,0:T(8,128)S(1)}, f32[12,128]{1,0:T(8,128)S(1)}) custom-call(s32[3]{0:T(128)S(1)} %pad_add_fusion.me_ref, bf16[1536,128]{1,0:T(8,128)(2,1)S(1)} %collective-permute-done.refs_0_, bf16[1568,128]{1,0:T(8,128)(2,1)S(1)} %collective-permute-done.4.refs_1_, bf16[1536,128]{1,0:T(8,128)(2,1)S(1)} %collective-permute-done.1.refs_2_, ...), custom_call_target="tpu_custom_call" | custom-call | flops 805306368 | bytes 8388608 | tf_op jit(solution)/shard_map/score_chunks/pallas_call | solution.py:290
  47.1 2.0 %collective-permute-start.16 = (bf16[1568,128]{1,0:T(8,128)(2,1)S(1)}, bf16[1568,128]{1,0:T(8,128)(2,1)S(1)}, u32[]{:S(2)}, u32[]{:S(2)}) collective-permute-start(bf16[1568,128]{1,0:T(8,128)(2,1)S(1)} %collective-permute-done.12.refs_3_), channel_id=1, source_target_pairs={{0,4},{1,5},{2,6},{3,7},{8,0},{9,1},{10,2},{11,3},{16,8},{17,9},{1... | collective-permute-start | bytes 1204232 | tf_op jit(solution)/shard_map/ppermute | solution.py:368
  49.1 4.9 %collective-permute-done.10.refs_2_ = bf16[32,128]{1,0:T(8,128)(2,1)S(1)} collective-permute-done((bf16[32,128]{1,0:T(8,128)(2,1)S(1)}, bf16[32,128]{1,0:T(8,128)(2,1)S(1)}, u32[]{:S(2)}, u32[]{:S(2)}) %collective-permute-start.10) | collective-permute-done | bytes 8224 | tf_op jit(solution)/shard_map/ppermute | solution.py:368
  54.0 4.9 %score_chunks.7 = (f32[12,128]{1,0:T(8,128)S(1)}, f32[12,128]{1,0:T(8,128)S(1)}) custom-call(s32[3]{0:T(128)S(1)} %pad_add_fusion.me_ref, bf16[1536,128]{1,0:T(8,128)(2,1)S(1)} %collective-permute-done.2.refs_0_, bf16[1568,128]{1,0:T(8,128)(2,1)S(1)} %collective-permute-done.11.refs_1_, bf16[1536,128]{1,0:T(8,128)(2,1)S(1)} %collective-permute-done.7.refs_2_, ...), custom_call_target="tpu_custom_call" | custom-call | flops 805306368 | bytes 8388608 | tf_op jit(solution)/shard_map/score_chunks/pallas_call | solution.py:290
  59.0 2.1 %collective-permute-start.14 = (bf16[1536,128]{1,0:T(8,128)(2,1)S(1)}, bf16[1536,128]{1,0:T(8,128)(2,1)S(1)}, u32[]{:S(2)}, u32[]{:S(2)}) collective-permute-start(bf16[1536,128]{1,0:T(8,128)(2,1)S(1)} %collective-permute-done.9.refs_2_), channel_id=1, source_target_pairs={{0,4},{1,5},{2,6},{3,7},{8,0},{9,1},{10,2},{11,3},{16,8},{17,9},{1... | collective-permute-start | bytes 1179656 | tf_op jit(solution)/shard_map/ppermute | solution.py:368
  61.1 6.1 %score_chunks.8 = (f32[12,128]{1,0:T(8,128)S(1)}, f32[12,128]{1,0:T(8,128)S(1)}) custom-call(s32[3]{0:T(128)S(1)} %pad_add_fusion.me_ref, bf16[1536,128]{1,0:T(8,128)(2,1)S(1)} %collective-permute-done.8.refs_0_, bf16[1568,128]{1,0:T(8,128)(2,1)S(1)} %collective-permute-done.15.refs_1_, bf16[1536,128]{1,0:T(8,128)(2,1)S(1)} %collective-permute-done.9.refs_2_, ...), custom_call_target="tpu_custom_call" | custom-call | flops 805306368 | bytes 8388608 | tf_op jit(solution)/shard_map/score_chunks/pallas_call | solution.py:290
  67.5 4.1 %score_chunks.9 = (f32[12,128]{1,0:T(8,128)}, f32[256,128]{1,0:T(8,128)S(1)}) custom-call(s32[3]{0:T(128)S(1)} %pad_add_fusion.me_ref, bf16[1536,128]{1,0:T(8,128)(2,1)S(1)} %collective-permute-done.13.refs_0_, bf16[1536,128]{1,0:T(8,128)(2,1)S(1)} %collective-permute-done.14.refs_1_, bf16[32,128]{1,0:T(8,128)(2,1)S(1)} %collective-permute-done.10.refs_2_, ...), custom_call_target="tpu_custom_call" | custom-call | flops 402653184 | bytes 8388608 | tf_op jit(solution)/shard_map/score_chunks/pallas_call | solution.py:290
  71.5 13.7 %all_to_all.9.parts_ref = f32[32,8,128]{2,1,0:T(8,128)} all-to-all(f32[32,8,128]{2,1,0:T(8,128)S(1)} %bitcast.10), channel_id=1, replica_groups=mesh['art'=16,'seq'=2] {'art','seq'}, dimensions={0} | all-to-all | bytes 262144 | tf_op jit(solution)/shard_map/all_to_all | solution.py:415
  85.2 1.7 %close.1 = (f32[12,64]{1,0:T(8,128)}, f32[12,64]{1,0:T(8,128)}) custom-call(f32[32,8,128]{2,1,0:T(8,128)} %all_to_all.9.parts_ref), custom_call_target="tpu_custom_call" | custom-call | tf_op jit(solution)/shard_map/close/pallas_call | solution.py:331
  (29 shorter events, 6.6 us)
Async XLA Ops:
  0.6 28.3 %collective-permute-start.6 = (bf16[256,64,128]{2,1,0:T(8,128)(2,1)}, bf16[256,64,128]{2,1,0:T(8,128)(2,1)}, u32[]{:S(2)}, u32[]{:S(2)}) collective-permute-start(bf16[256,64,128]{2,1,0:T(8,128)(2,1)} %blocks_ref), channel_id=1, source_target_pairs={{0,2},{2,0},{4,6},{6,4},{8,10},{10,8},{12,14},{14,12},{16,18},{18,... | collective-permute-start | bytes 12582920 | tf_op jit(solution)/shard_map/ppermute | solution.py:383
  2.3 12.4 %collective-permute-start = (bf16[1536,128]{1,0:T(8,128)(2,1)S(1)}, bf16[1536,128]{1,0:T(8,128)(2,1)S(1)}, u32[]{:S(2)}, u32[]{:S(2)}) collective-permute-start(bf16[1536,128]{1,0:T(8,128)(2,1)S(1)} %bitcast.8), channel_id=1, source_target_pairs={{0,8},{1,9},{2,10},{3,11},{8,16},{9,17},{10,18},{11,19},{16,24},{1... | collective-permute-start | bytes 1179656 | tf_op jit(solution)/shard_map/ppermute | solution.py:368
  5.0 11.3 %collective-permute-start.1 = (bf16[1536,128]{1,0:T(8,128)(2,1)S(1)}, bf16[1536,128]{1,0:T(8,128)(2,1)S(1)}, u32[]{:S(2)}, u32[]{:S(2)}) collective-permute-start(bf16[1536,128]{1,0:T(8,128)(2,1)S(1)} %bitcast.11), channel_id=1, source_target_pairs={{0,4},{1,5},{2,6},{3,7},{8,0},{9,1},{10,2},{11,3},{16,8},{17,9},{1... | collective-permute-start | bytes 1179656 | tf_op jit(solution)/shard_map/ppermute | solution.py:368
  6.0 3.7 %collective-permute-start.3 = (s32[6,128]{1,0:T(8,128)S(1)}, s32[6,128]{1,0:T(8,128)S(1)}, u32[]{:S(2)}, u32[]{:S(2)}) collective-permute-start(s32[6,128]{1,0:T(8,128)S(1)} %reshape.16.refs_0_), channel_id=1, source_target_pairs={{0,1},{1,0},{2,3},{3,2},{8,9},{9,8},{10,11},{11,10},{16,17},{17,16... | collective-permute-start | bytes 9224 | tf_op jit(solution)/shard_map/ppermute | solution.py:368
  9.7 1.1 %copy-start = (bf16[12,1,256,128]{3,2,1,0:T(8,128)(2,1)S(1)}, bf16[12,1,256,128]{3,2,1,0:T(8,128)(2,1)}, u32[]{:S(2)}) copy-start(bf16[12,1,256,128]{3,2,1,0:T(8,128)(2,1)} %param.4) | copy-start | bytes 2359300
  12.6 12.3 %collective-permute-start.4 = (bf16[1568,128]{1,0:T(8,128)(2,1)S(1)}, bf16[1568,128]{1,0:T(8,128)(2,1)S(1)}, u32[]{:S(2)}, u32[]{:S(2)}) collective-permute-start(bf16[1568,128]{1,0:T(8,128)(2,1)S(1)} %get-tuple-element.37.refs_1_), channel_id=1, source_target_pairs={{0,8},{1,9},{2,10},{3,11},{8,16},{9,17},{10,18},{11,19},{16,24},{1... | collective-permute-start | bytes 1204232 | tf_op jit(solution)/shard_map/ppermute | solution.py:368
  14.7 12.2 %collective-permute-start.5 = (bf16[1568,128]{1,0:T(8,128)(2,1)S(1)}, bf16[1568,128]{1,0:T(8,128)(2,1)S(1)}, u32[]{:S(2)}, u32[]{:S(2)}) collective-permute-start(bf16[1568,128]{1,0:T(8,128)(2,1)S(1)} %get-tuple-element.38), channel_id=1, source_target_pairs={{0,4},{1,5},{2,6},{3,7},{8,0},{9,1},{10,2},{11,3},{16,8},{17,9},{1... | collective-permute-start | bytes 1204232 | tf_op jit(solution)/shard_map/ppermute | solution.py:368
  16.2 20.4 %collective-permute-start.2 = (bf16[1536,128]{1,0:T(8,128)(2,1)S(1)}, bf16[1536,128]{1,0:T(8,128)(2,1)S(1)}, u32[]{:S(2)}, u32[]{:S(2)}) collective-permute-start(bf16[1536,128]{1,0:T(8,128)(2,1)S(1)} %collective-permute-done.refs_0_), channel_id=1, source_target_pairs={{0,8},{1,9},{2,10},{3,11},{8,16},{9,17},{10,18},{11,19},{16,24},{1... | collective-permute-start | bytes 1179656 | tf_op jit(solution)/shard_map/ppermute | solution.py:368
  17.8 18.8 %collective-permute-start.7 = (bf16[1536,128]{1,0:T(8,128)(2,1)S(1)}, bf16[1536,128]{1,0:T(8,128)(2,1)S(1)}, u32[]{:S(2)}, u32[]{:S(2)}) collective-permute-start(bf16[1536,128]{1,0:T(8,128)(2,1)S(1)} %collective-permute-done.1.refs_2_), channel_id=1, source_target_pairs={{0,4},{1,5},{2,6},{3,7},{8,0},{9,1},{10,2},{11,3},{16,8},{17,9},{1... | collective-permute-start | bytes 1179656 | tf_op jit(solution)/shard_map/ppermute | solution.py:368
  18.2 2.2 %copy-start.1 = (bf16[256,64,128]{2,1,0:T(8,128)(2,1)S(1)}, bf16[256,64,128]{2,1,0:T(8,128)(2,1)}, u32[]{:S(2)}) copy-start(bf16[256,64,128]{2,1,0:T(8,128)(2,1)} %blocks_ref) | copy-start | bytes 12582916
  26.9 20.1 %collective-permute-start.12 = (bf16[1568,128]{1,0:T(8,128)(2,1)S(1)}, bf16[1568,128]{1,0:T(8,128)(2,1)S(1)}, u32[]{:S(2)}, u32[]{:S(2)}) collective-permute-start(bf16[1568,128]{1,0:T(8,128)(2,1)S(1)} %collective-permute-done.5.refs_3_), channel_id=1, source_target_pairs={{0,4},{1,5},{2,6},{3,7},{8,0},{9,1},{10,2},{11,3},{16,8},{17,9},{1... | collective-permute-start | bytes 1204232 | tf_op jit(solution)/shard_map/ppermute | solution.py:368
  26.9 20.1 %collective-permute-start.11 = (bf16[1568,128]{1,0:T(8,128)(2,1)S(1)}, bf16[1568,128]{1,0:T(8,128)(2,1)S(1)}, u32[]{:S(2)}, u32[]{:S(2)}) collective-permute-start(bf16[1568,128]{1,0:T(8,128)(2,1)S(1)} %collective-permute-done.4.refs_1_), channel_id=1, source_target_pairs={{0,8},{1,9},{2,10},{3,11},{8,16},{9,17},{10,18},{11,19},{16,24},{1... | collective-permute-start | bytes 1204232 | tf_op jit(solution)/shard_map/ppermute | solution.py:368
  36.6 17.4 %collective-permute-start.8 = (bf16[1536,128]{1,0:T(8,128)(2,1)S(1)}, bf16[1536,128]{1,0:T(8,128)(2,1)S(1)}, u32[]{:S(2)}, u32[]{:S(2)}) collective-permute-start(bf16[1536,128]{1,0:T(8,128)(2,1)S(1)} %collective-permute-done.2.refs_0_), channel_id=1, source_target_pairs={{0,8},{1,9},{2,10},{3,11},{8,16},{9,17},{10,18},{11,19},{16,24},{1... | collective-permute-start | bytes 1179656 | tf_op jit(solution)/shard_map/ppermute | solution.py:368
  38.2 15.8 %collective-permute-start.9 = (bf16[1536,128]{1,0:T(8,128)(2,1)S(1)}, bf16[1536,128]{1,0:T(8,128)(2,1)S(1)}, u32[]{:S(2)}, u32[]{:S(2)}) collective-permute-start(bf16[1536,128]{1,0:T(8,128)(2,1)S(1)} %collective-permute-done.7.refs_2_), channel_id=1, source_target_pairs={{0,4},{1,5},{2,6},{3,7},{8,0},{9,1},{10,2},{11,3},{16,8},{17,9},{1... | collective-permute-start | bytes 1179656 | tf_op jit(solution)/shard_map/ppermute | solution.py:368
  38.7 15.3 %collective-permute-start.10 = (bf16[32,128]{1,0:T(8,128)(2,1)S(1)}, bf16[32,128]{1,0:T(8,128)(2,1)S(1)}, u32[]{:S(2)}, u32[]{:S(2)}) collective-permute-start(bf16[32,128]{1,0:T(8,128)(2,1)S(1)} %get-tuple-element.50), channel_id=1, source_target_pairs={{0,28},{1,29},{2,30},{3,31},{8,20},{9,21},{10,22},{11,23},{16,12},... | collective-permute-start | bytes 24584 | tf_op jit(solution)/shard_map/ppermute | solution.py:368
  47.0 14.1 %collective-permute-start.15 = (bf16[1568,128]{1,0:T(8,128)(2,1)S(1)}, bf16[1568,128]{1,0:T(8,128)(2,1)S(1)}, u32[]{:S(2)}, u32[]{:S(2)}) collective-permute-start(bf16[1568,128]{1,0:T(8,128)(2,1)S(1)} %collective-permute-done.11.refs_1_), channel_id=1, source_target_pairs={{0,8},{1,9},{2,10},{3,11},{8,16},{9,17},{10,18},{11,19},{16,24},{1... | collective-permute-start | bytes 1204232 | tf_op jit(solution)/shard_map/ppermute | solution.py:368
  47.1 14.0 %collective-permute-start.16 = (bf16[1568,128]{1,0:T(8,128)(2,1)S(1)}, bf16[1568,128]{1,0:T(8,128)(2,1)S(1)}, u32[]{:S(2)}, u32[]{:S(2)}) collective-permute-start(bf16[1568,128]{1,0:T(8,128)(2,1)S(1)} %collective-permute-done.12.refs_3_), channel_id=1, source_target_pairs={{0,4},{1,5},{2,6},{3,7},{8,0},{9,1},{10,2},{11,3},{16,8},{17,9},{1... | collective-permute-start | bytes 1204232 | tf_op jit(solution)/shard_map/ppermute | solution.py:368
  58.9 8.3 %collective-permute-start.13 = (bf16[1536,128]{1,0:T(8,128)(2,1)S(1)}, bf16[1536,128]{1,0:T(8,128)(2,1)S(1)}, u32[]{:S(2)}, u32[]{:S(2)}) collective-permute-start(bf16[1536,128]{1,0:T(8,128)(2,1)S(1)} %collective-permute-done.8.refs_0_), channel_id=1, source_target_pairs={{0,8},{1,9},{2,10},{3,11},{8,16},{9,17},{10,18},{11,19},{16,24},{1... | collective-permute-start | bytes 1179656 | tf_op jit(solution)/shard_map/ppermute | solution.py:368
  59.0 8.5 %collective-permute-start.14 = (bf16[1536,128]{1,0:T(8,128)(2,1)S(1)}, bf16[1536,128]{1,0:T(8,128)(2,1)S(1)}, u32[]{:S(2)}, u32[]{:S(2)}) collective-permute-start(bf16[1536,128]{1,0:T(8,128)(2,1)S(1)} %collective-permute-done.9.refs_2_), channel_id=1, source_target_pairs={{0,4},{1,5},{2,6},{3,7},{8,0},{9,1},{10,2},{11,3},{16,8},{17,9},{1... | collective-permute-start | bytes 1179656 | tf_op jit(solution)/shard_map/ppermute | solution.py:368

commit v6 on v5

--- a/solution.py
+++ b/solution.py
@@ -67,13 +67,13 @@
 
 
 def pack_kernel(chips, blocks, me_ref, *refs):
-    id_refs, (query_ref, ahead_ref, behind_ref, lists_ref) = refs[:-4], refs[-4:]
+    id_refs, (first_ref, second_ref, ahead_ref, behind_ref, lists_ref) = refs[:-5], refs[-5:]
     seqs = len(id_refs)
     core, seq = me_ref[1], me_ref[2]
     per_home, width = id_refs[0].shape
-    rows = query_ref.shape[0] // 2
-    ahead_ref[0:rows, :] = query_ref[rows : 2 * rows, :]
-    behind_ref[0:rows, :] = query_ref[0:rows, :]
+    rows = first_ref.shape[0]
+    ahead_ref[0:rows, :] = second_ref[...]
+    behind_ref[0:rows, :] = first_ref[...]
 
     lane = lax.broadcasted_iota(jnp.int32, (per_home, width), 1)
     ids = jnp.zeros((per_home, width), jnp.int32)
@@ -138,20 +138,20 @@
     lists_ref[...] = lists
 
 
-def pack_streams(me, ids, query, chips, blocks):
+def pack_streams(me, ids, first, second, chips, blocks):
     vmem = pl.BlockSpec(memory_space=pltpu.VMEM)
     articles = len(ids) * ids[0].shape[0]
     extra = plan_rows(chips, articles)[1]
-    shapes = [(query.shape[0] // 2 + extra, query.shape[1])] * 2 + [(extra, query.shape[1])]
+    shapes = [(first.shape[0] + extra, first.shape[1])] * 2 + [(extra, first.shape[1])]
     return pl.pallas_call(
         functools.partial(pack_kernel, chips, blocks),
         out_shape=[jax.ShapeDtypeStruct(shape, jnp.bfloat16) for shape in shapes],
-        in_specs=[pl.BlockSpec(memory_space=pltpu.SMEM)] + [vmem] * (len(ids) + 1),
+        in_specs=[pl.BlockSpec(memory_space=pltpu.SMEM)] + [vmem] * (len(ids) + 2),
         out_specs=[vmem] * 3,
         compiler_params=pltpu.CompilerParams(vmem_limit_bytes=32 * 1024 * 1024),
         cost_estimate=pl.CostEstimate(flops=1, bytes_accessed=1, transcendentals=0),
         name="pack_streams",
-    )(me, *ids, query)
+    )(me, *ids, first, second)
 
 
 def score_kernel(dims, me_ref, *refs):
@@ -368,14 +368,14 @@
         return lax.ppermute(array, ("art", "seq"), turn(step, across))
 
     cut = articles // 2 * tokens
-    one = mine[:cut]
+    one, rest = mine[:cut], mine[cut:]
     ahead, behind = [None], [None]
-    first = [send(one, 1), send(mine[cut:], -1)]
+    first = [send(one, 1), send(rest, -1)]
 
     ids = (cand_owner * blocks + cand_local).reshape(per_home, seqs * NC)
     ids = [ids] + [send(ids, 0, d) for d in range(1, seqs)]
     me = jnp.stack([art // 2, art % 2, seq]).astype(jnp.int32)
-    two, back, lists = pack_streams(me, ids, mine, chips, blocks)
+    two, back, lists = pack_streams(me, ids, one, rest, chips, blocks)
     second = [send(two, 1), send(back, -1)]
     ahead.append([first[0], second[0]])
     behind.append([first[1], second[1]])

time: 87.2 us -> 86.9 us (level)
  waiting for transfers between devices: 11.7 us -> 13.8 us
  local copies, waits for them, and re-layouts: 4.74 us -> 3.61 us
  Pallas kernels: 34.2 us -> 33.2 us
    ppermute x16, waiting for transfers between devices: 11.6 us -> 13.8 us  [send(): return lax.ppermute(array, ('art', 'seq'), turn(step, across))]
    unnamed x4 -> x2, local copies, waits for them, and re-layouts: 3.32 us -> 2.19 us
    pallas_call x5, Pallas kernels: 23.4 us -> 22.4 us  [score_chunks(): pl.pallas_call(functools.partial(score_kernel, (plans, len(far), len(othe...]
  transfers between devices with their start and end apart: 17 -> 17, of which waited for: 6 -> 7; matrix products, arithmetic and copies ran while one was open for 3% -> 3% of each run, Pallas kernels for 33% -> 32%
where the time goes in v6:
time: 86.9 us; the launch traced here: 86.6 us
  Pallas kernels  33.2 us (38%)
  starting transfers between devices  21.1 us (24%)
  waiting for transfers between devices  13.8 us (16%)
  blocking collectives  13.4 us (15%)
  local copies, waits for them, and re-layouts  3.61 us (4%)
    pallas_call x5, Pallas kernels, score_chunks(): pl.pallas_call(functools.partial(score_kernel, (plans, len(far), len(othe...  22.4 us
    ppermute x16, starting transfers between devices, send(): return lax.ppermute(array, ('art', 'seq'), turn(step, across))  20.5 us
    ppermute x16, waiting for transfers between devices, send(): return lax.ppermute(array, ('art', 'seq'), turn(step, across))  13.8 us
    all_to_all x1, blocking collectives, per_device(): lax.all_to_all(spread, ('art', 'seq'), split_axis=0, concat_axis=0, tiled...  13.4 us
    pallas_call x2, Pallas kernels, unit_blocks(): pl.pallas_call(functools.partial(unit_kernel, parts), out_shape=jax.Shape...  7.26 us
    unnamed x2, local copies, waits for them, and re-layouts  2.19 us
    pallas_call x1, Pallas kernels, pack_streams(): pl.pallas_call(functools.partial(pack_kernel, chips, blocks), out_shape=[...  1.85 us
  transfers between devices with their start and end apart: 17, of which 7 were waited for; matrix products, arithmetic and copies ran while one was open for 3% of the time, Pallas kernels for 32%

profile of v6, /device:TPU:0, one launch (start us, length us, event | category | flops | bytes accessed | tf_op | source)
XLA Modules:
  0.0 86.6 jit_solution(8191784364045065447)
XLA Ops:
  2.3 2.6 %collective-permute-start = (bf16[1536,128]{1,0:T(8,128)(2,1)S(1)}, bf16[1536,128]{1,0:T(8,128)(2,1)S(1)}, u32[]{:S(2)}, u32[]{:S(2)}) collective-permute-start(bf16[1536,128]{1,0:T(8,128)(2,1)S(1)} %bitcast.6), channel_id=1, source_target_pairs={{0,8},{1,9},{2,10},{3,11},{8,16},{9,17},{10,18},{11,19},{16,24},{1... | collective-permute-start | bytes 1179656 | tf_op jit(solution)/shard_map/ppermute | solution.py:368
  6.0 2.0 %collective-permute-start.3 = (s32[6,128]{1,0:T(8,128)S(1)}, s32[6,128]{1,0:T(8,128)S(1)}, u32[]{:S(2)}, u32[]{:S(2)}) collective-permute-start(s32[6,128]{1,0:T(8,128)S(1)} %reshape.14.refs_0_), channel_id=1, source_target_pairs={{0,1},{1,0},{2,3},{3,2},{8,9},{9,8},{10,11},{11,10},{16,17},{17,16... | collective-permute-start | bytes 9224 | tf_op jit(solution)/shard_map/ppermute | solution.py:368
  8.1 1.6 %collective-permute-done.3.refs_1_ = s32[6,128]{1,0:T(8,128)S(1)} collective-permute-done((s32[6,128]{1,0:T(8,128)S(1)}, s32[6,128]{1,0:T(8,128)S(1)}, u32[]{:S(2)}, u32[]{:S(2)}) %collective-permute-start.3) | collective-permute-done | bytes 3104 | tf_op jit(solution)/shard_map/ppermute | solution.py:368
  9.7 1.8 %pack_streams.1 = (bf16[1568,128]{1,0:T(8,128)(2,1)S(1)}, bf16[1568,128]{1,0:T(8,128)(2,1)S(1)}, bf16[32,128]{1,0:T(8,128)(2,1)S(1)}) custom-call(s32[3]{0:T(128)S(1)} %pad_add_fusion.me_ref, s32[6,128]{1,0:T(8,128)S(1)} %reshape.14.refs_0_, s32[6,128]{1,0:T(8,128)S(1)} %collective-permute-done.3.refs_1_, bf16[1536,128]{1,0:T(8,128)(2,1)S(1)} %bitcast.7, ...), custom_call_target="tpu_custom_call" | custom-call | flops 1 | bytes 1 | tf_op jit(solution)/shard_map/pack_streams/pallas_call | solution.py:146
  11.5 2.1 %collective-permute-start.4 = (bf16[1568,128]{1,0:T(8,128)(2,1)S(1)}, bf16[1568,128]{1,0:T(8,128)(2,1)S(1)}, u32[]{:S(2)}, u32[]{:S(2)}) collective-permute-start(bf16[1568,128]{1,0:T(8,128)(2,1)S(1)} %get-tuple-element.37.refs_1_), channel_id=1, source_target_pairs={{0,8},{1,9},{2,10},{3,11},{8,16},{9,17},{10,18},{11,19},{16,24},{1... | collective-permute-start | bytes 1204232 | tf_op jit(solution)/shard_map/ppermute | solution.py:368
  14.9 2.0 %collective-permute-done.1.refs_2_ = bf16[1536,128]{1,0:T(8,128)(2,1)S(1)} collective-permute-done((bf16[1536,128]{1,0:T(8,128)(2,1)S(1)}, bf16[1536,128]{1,0:T(8,128)(2,1)S(1)}, u32[]{:S(2)}, u32[]{:S(2)}) %collective-permute-start.1) | collective-permute-done | bytes 393248 | tf_op jit(solution)/shard_map/ppermute | solution.py:368
  16.9 1.6 %collective-permute-start.2 = (bf16[1536,128]{1,0:T(8,128)(2,1)S(1)}, bf16[1536,128]{1,0:T(8,128)(2,1)S(1)}, u32[]{:S(2)}, u32[]{:S(2)}) collective-permute-start(bf16[1536,128]{1,0:T(8,128)(2,1)S(1)} %collective-permute-done.refs_0_), channel_id=1, source_target_pairs={{0,8},{1,9},{2,10},{3,11},{8,16},{9,17},{10,18},{11,19},{16,24},{1... | collective-permute-start | bytes 1179656 | tf_op jit(solution)/shard_map/ppermute | solution.py:368
  18.9 2.2 %copy-done = bf16[256,64,128]{2,1,0:T(8,128)(2,1)S(1)} copy-done((bf16[256,64,128]{2,1,0:T(8,128)(2,1)S(1)}, bf16[256,64,128]{2,1,0:T(8,128)(2,1)}, u32[]{:S(2)}) %copy-start) | copy-done | bytes 4194328
  21.1 3.2 %unit_blocks.2.refs_2_.refs_4_.refs_10_ = bf16[256,64,128]{2,1,0:T(8,128)(2,1)S(1)} custom-call(bf16[256,64,128]{2,1,0:T(8,128)(2,1)S(1)} %copy-done), custom_call_target="tpu_custom_call" | custom-call | flops 4000000000 | bytes 1 | tf_op jit(solution)/shard_map/unit_blocks/pallas_call | solution.py:45
  24.3 1.5 %collective-permute-done.5.refs_3_ = bf16[1568,128]{1,0:T(8,128)(2,1)S(1)} collective-permute-done((bf16[1568,128]{1,0:T(8,128)(2,1)S(1)}, bf16[1568,128]{1,0:T(8,128)(2,1)S(1)}, u32[]{:S(2)}, u32[]{:S(2)}) %collective-permute-start.5) | collective-permute-done | bytes 401440 | tf_op jit(solution)/shard_map/ppermute | solution.py:368
  25.8 1.6 %collective-permute-start.11 = (bf16[1568,128]{1,0:T(8,128)(2,1)S(1)}, bf16[1568,128]{1,0:T(8,128)(2,1)S(1)}, u32[]{:S(2)}, u32[]{:S(2)}) collective-permute-start(bf16[1568,128]{1,0:T(8,128)(2,1)S(1)} %collective-permute-done.4.refs_1_), channel_id=1, source_target_pairs={{0,8},{1,9},{2,10},{3,11},{8,16},{9,17},{10,18},{11,19},{16,24},{1... | collective-permute-start | bytes 1204232 | tf_op jit(solution)/shard_map/ppermute | solution.py:368
  27.8 4.1 %unit_blocks.3.refs_3_.refs_5_.refs_11_ = bf16[256,64,128]{2,1,0:T(8,128)(2,1)S(1)} custom-call(bf16[256,64,128]{2,1,0:T(8,128)(2,1)} %collective-permute-done.6.blocks_ref), custom_call_target="tpu_custom_call" | custom-call | flops 4000000000 | bytes 1 | tf_op jit(solution)/shard_map/unit_blocks/pallas_call | solution.py:45
  31.9 3.5 %score_chunks.5.refs_3_ = f32[12,128]{1,0:T(8,128)S(1)} custom-call(s32[3]{0:T(128)S(1)} %pad_add_fusion.me_ref, bf16[1536,128]{1,0:T(8,128)(2,1)S(1)} %bitcast.8, bf16[1568,128]{1,0:T(8,128)(2,1)S(1)} %get-tuple-element.37.refs_1_, bf16[256,64,128]{2,1,0:T(8,128)(2,1)S(1)} %unit_blocks.2.refs_2_.refs_4_.refs_10_, ...), custom_call_target="tpu_custom_call" | custom-call | flops 402653184 | bytes 8388608 | tf_op jit(solution)/shard_map/score_chunks/pallas_call | solution.py:290
  37.5 3.4 %collective-permute-start.10 = (bf16[32,128]{1,0:T(8,128)(2,1)S(1)}, bf16[32,128]{1,0:T(8,128)(2,1)S(1)}, u32[]{:S(2)}, u32[]{:S(2)}) collective-permute-start(bf16[32,128]{1,0:T(8,128)(2,1)S(1)} %get-tuple-element.50), channel_id=1, source_target_pairs={{0,28},{1,29},{2,30},{3,31},{8,20},{9,21},{10,22},{11,23},{16,12},... | collective-permute-start | bytes 24584 | tf_op jit(solution)/shard_map/ppermute | solution.py:368
  41.0 4.9 %score_chunks.6 = (f32[12,128]{1,0:T(8,128)S(1)}, f32[12,128]{1,0:T(8,128)S(1)}) custom-call(s32[3]{0:T(128)S(1)} %pad_add_fusion.me_ref, bf16[1536,128]{1,0:T(8,128)(2,1)S(1)} %collective-permute-done.refs_0_, bf16[1568,128]{1,0:T(8,128)(2,1)S(1)} %collective-permute-done.4.refs_1_, bf16[1536,128]{1,0:T(8,128)(2,1)S(1)} %collective-permute-done.1.refs_2_, ...), custom_call_target="tpu_custom_call" | custom-call | flops 805306368 | bytes 8388608 | tf_op jit(solution)/shard_map/score_chunks/pallas_call | solution.py:290
  45.9 2.0 %collective-permute-start.16 = (bf16[1568,128]{1,0:T(8,128)(2,1)S(1)}, bf16[1568,128]{1,0:T(8,128)(2,1)S(1)}, u32[]{:S(2)}, u32[]{:S(2)}) collective-permute-start(bf16[1568,128]{1,0:T(8,128)(2,1)S(1)} %collective-permute-done.12.refs_3_), channel_id=1, source_target_pairs={{0,4},{1,5},{2,6},{3,7},{8,0},{9,1},{10,2},{11,3},{16,8},{17,9},{1... | collective-permute-start | bytes 1204232 | tf_op jit(solution)/shard_map/ppermute | solution.py:368
  47.9 4.9 %collective-permute-done.10.refs_2_ = bf16[32,128]{1,0:T(8,128)(2,1)S(1)} collective-permute-done((bf16[32,128]{1,0:T(8,128)(2,1)S(1)}, bf16[32,128]{1,0:T(8,128)(2,1)S(1)}, u32[]{:S(2)}, u32[]{:S(2)}) %collective-permute-start.10) | collective-permute-done | bytes 8224 | tf_op jit(solution)/shard_map/ppermute | solution.py:368
  52.8 4.9 %score_chunks.7 = (f32[12,128]{1,0:T(8,128)S(1)}, f32[12,128]{1,0:T(8,128)S(1)}) custom-call(s32[3]{0:T(128)S(1)} %pad_add_fusion.me_ref, bf16[1536,128]{1,0:T(8,128)(2,1)S(1)} %collective-permute-done.2.refs_0_, bf16[1568,128]{1,0:T(8,128)(2,1)S(1)} %collective-permute-done.11.refs_1_, bf16[1536,128]{1,0:T(8,128)(2,1)S(1)} %collective-permute-done.7.refs_2_, ...), custom_call_target="tpu_custom_call" | custom-call | flops 805306368 | bytes 8388608 | tf_op jit(solution)/shard_map/score_chunks/pallas_call | solution.py:290
  57.8 2.1 %collective-permute-start.14 = (bf16[1536,128]{1,0:T(8,128)(2,1)S(1)}, bf16[1536,128]{1,0:T(8,128)(2,1)S(1)}, u32[]{:S(2)}, u32[]{:S(2)}) collective-permute-start(bf16[1536,128]{1,0:T(8,128)(2,1)S(1)} %collective-permute-done.9.refs_2_), channel_id=1, source_target_pairs={{0,4},{1,5},{2,6},{3,7},{8,0},{9,1},{10,2},{11,3},{16,8},{17,9},{1... | collective-permute-start | bytes 1179656 | tf_op jit(solution)/shard_map/ppermute | solution.py:368
  59.9 5.0 %score_chunks.8 = (f32[12,128]{1,0:T(8,128)S(1)}, f32[12,128]{1,0:T(8,128)S(1)}) custom-call(s32[3]{0:T(128)S(1)} %pad_add_fusion.me_ref, bf16[1536,128]{1,0:T(8,128)(2,1)S(1)} %collective-permute-done.8.refs_0_, bf16[1568,128]{1,0:T(8,128)(2,1)S(1)} %collective-permute-done.15.refs_1_, bf16[1536,128]{1,0:T(8,128)(2,1)S(1)} %collective-permute-done.9.refs_2_, ...), custom_call_target="tpu_custom_call" | custom-call | flops 805306368 | bytes 8388608 | tf_op jit(solution)/shard_map/score_chunks/pallas_call | solution.py:290
  65.0 2.2 %collective-permute-done.13.refs_0_ = bf16[1536,128]{1,0:T(8,128)(2,1)S(1)} collective-permute-done((bf16[1536,128]{1,0:T(8,128)(2,1)S(1)}, bf16[1536,128]{1,0:T(8,128)(2,1)S(1)}, u32[]{:S(2)}, u32[]{:S(2)}) %collective-permute-start.13) | collective-permute-done | bytes 393248 | tf_op jit(solution)/shard_map/ppermute | solution.py:368
  67.5 4.1 %score_chunks.9 = (f32[12,128]{1,0:T(8,128)}, f32[256,128]{1,0:T(8,128)S(1)}) custom-call(s32[3]{0:T(128)S(1)} %pad_add_fusion.me_ref, bf16[1536,128]{1,0:T(8,128)(2,1)S(1)} %collective-permute-done.13.refs_0_, bf16[1536,128]{1,0:T(8,128)(2,1)S(1)} %collective-permute-done.14.refs_1_, bf16[32,128]{1,0:T(8,128)(2,1)S(1)} %collective-permute-done.10.refs_2_, ...), custom_call_target="tpu_custom_call" | custom-call | flops 402653184 | bytes 8388608 | tf_op jit(solution)/shard_map/score_chunks/pallas_call | solution.py:290
  71.5 13.4 %all_to_all.9.parts_ref = f32[32,8,128]{2,1,0:T(8,128)} all-to-all(f32[32,8,128]{2,1,0:T(8,128)S(1)} %bitcast.11), channel_id=1, replica_groups=mesh['art'=16,'seq'=2] {'art','seq'}, dimensions={0} | all-to-all | bytes 262144 | tf_op jit(solution)/shard_map/all_to_all | solution.py:415
  84.9 1.7 %close.1 = (f32[12,64]{1,0:T(8,128)}, f32[12,64]{1,0:T(8,128)}) custom-call(f32[32,8,128]{2,1,0:T(8,128)} %all_to_all.9.parts_ref), custom_call_target="tpu_custom_call" | custom-call | tf_op jit(solution)/shard_map/close/pallas_call | solution.py:331
  (27 shorter events, 7.5 us)
Async XLA Ops:
  0.6 27.2 %collective-permute-start.6 = (bf16[256,64,128]{2,1,0:T(8,128)(2,1)}, bf16[256,64,128]{2,1,0:T(8,128)(2,1)}, u32[]{:S(2)}, u32[]{:S(2)}) collective-permute-start(bf16[256,64,128]{2,1,0:T(8,128)(2,1)} %blocks_ref), channel_id=1, source_target_pairs={{0,2},{2,0},{4,6},{6,4},{8,10},{10,8},{12,14},{14,12},{16,18},{18,... | collective-permute-start | bytes 12582920 | tf_op jit(solution)/shard_map/ppermute | solution.py:383
  2.3 12.6 %collective-permute-start = (bf16[1536,128]{1,0:T(8,128)(2,1)S(1)}, bf16[1536,128]{1,0:T(8,128)(2,1)S(1)}, u32[]{:S(2)}, u32[]{:S(2)}) collective-permute-start(bf16[1536,128]{1,0:T(8,128)(2,1)S(1)} %bitcast.6), channel_id=1, source_target_pairs={{0,8},{1,9},{2,10},{3,11},{8,16},{9,17},{10,18},{11,19},{16,24},{1... | collective-permute-start | bytes 1179656 | tf_op jit(solution)/shard_map/ppermute | solution.py:368
  5.0 11.9 %collective-permute-start.1 = (bf16[1536,128]{1,0:T(8,128)(2,1)S(1)}, bf16[1536,128]{1,0:T(8,128)(2,1)S(1)}, u32[]{:S(2)}, u32[]{:S(2)}) collective-permute-start(bf16[1536,128]{1,0:T(8,128)(2,1)S(1)} %bitcast.9), channel_id=1, source_target_pairs={{0,4},{1,5},{2,6},{3,7},{8,0},{9,1},{10,2},{11,3},{16,8},{17,9},{1... | collective-permute-start | bytes 1179656 | tf_op jit(solution)/shard_map/ppermute | solution.py:368
  6.0 3.7 %collective-permute-start.3 = (s32[6,128]{1,0:T(8,128)S(1)}, s32[6,128]{1,0:T(8,128)S(1)}, u32[]{:S(2)}, u32[]{:S(2)}) collective-permute-start(s32[6,128]{1,0:T(8,128)S(1)} %reshape.14.refs_0_), channel_id=1, source_target_pairs={{0,1},{1,0},{2,3},{3,2},{8,9},{9,8},{10,11},{11,10},{16,17},{17,16... | collective-permute-start | bytes 9224 | tf_op jit(solution)/shard_map/ppermute | solution.py:368
  11.5 12.8 %collective-permute-start.4 = (bf16[1568,128]{1,0:T(8,128)(2,1)S(1)}, bf16[1568,128]{1,0:T(8,128)(2,1)S(1)}, u32[]{:S(2)}, u32[]{:S(2)}) collective-permute-start(bf16[1568,128]{1,0:T(8,128)(2,1)S(1)} %get-tuple-element.37.refs_1_), channel_id=1, source_target_pairs={{0,8},{1,9},{2,10},{3,11},{8,16},{9,17},{10,18},{11,19},{16,24},{1... | collective-permute-start | bytes 1204232 | tf_op jit(solution)/shard_map/ppermute | solution.py:368
  13.6 12.2 %collective-permute-start.5 = (bf16[1568,128]{1,0:T(8,128)(2,1)S(1)}, bf16[1568,128]{1,0:T(8,128)(2,1)S(1)}, u32[]{:S(2)}, u32[]{:S(2)}) collective-permute-start(bf16[1568,128]{1,0:T(8,128)(2,1)S(1)} %get-tuple-element.38), channel_id=1, source_target_pairs={{0,4},{1,5},{2,6},{3,7},{8,0},{9,1},{10,2},{11,3},{16,8},{17,9},{1... | collective-permute-start | bytes 1204232 | tf_op jit(solution)/shard_map/ppermute | solution.py:368
  16.9 18.5 %collective-permute-start.2 = (bf16[1536,128]{1,0:T(8,128)(2,1)S(1)}, bf16[1536,128]{1,0:T(8,128)(2,1)S(1)}, u32[]{:S(2)}, u32[]{:S(2)}) collective-permute-start(bf16[1536,128]{1,0:T(8,128)(2,1)S(1)} %collective-permute-done.refs_0_), channel_id=1, source_target_pairs={{0,8},{1,9},{2,10},{3,11},{8,16},{9,17},{10,18},{11,19},{16,24},{1... | collective-permute-start | bytes 1179656 | tf_op jit(solution)/shard_map/ppermute | solution.py:368
  18.5 17.0 %collective-permute-start.7 = (bf16[1536,128]{1,0:T(8,128)(2,1)S(1)}, bf16[1536,128]{1,0:T(8,128)(2,1)S(1)}, u32[]{:S(2)}, u32[]{:S(2)}) collective-permute-start(bf16[1536,128]{1,0:T(8,128)(2,1)S(1)} %collective-permute-done.1.refs_2_), channel_id=1, source_target_pairs={{0,4},{1,5},{2,6},{3,7},{8,0},{9,1},{10,2},{11,3},{16,8},{17,9},{1... | collective-permute-start | bytes 1179656 | tf_op jit(solution)/shard_map/ppermute | solution.py:368
  18.9 2.2 %copy-start = (bf16[256,64,128]{2,1,0:T(8,128)(2,1)S(1)}, bf16[256,64,128]{2,1,0:T(8,128)(2,1)}, u32[]{:S(2)}) copy-start(bf16[256,64,128]{2,1,0:T(8,128)(2,1)} %blocks_ref) | copy-start | bytes 12582916
  25.8 20.1 %collective-permute-start.11 = (bf16[1568,128]{1,0:T(8,128)(2,1)S(1)}, bf16[1568,128]{1,0:T(8,128)(2,1)S(1)}, u32[]{:S(2)}, u32[]{:S(2)}) collective-permute-start(bf16[1568,128]{1,0:T(8,128)(2,1)S(1)} %collective-permute-done.4.refs_1_), channel_id=1, source_target_pairs={{0,8},{1,9},{2,10},{3,11},{8,16},{9,17},{10,18},{11,19},{16,24},{1... | collective-permute-start | bytes 1204232 | tf_op jit(solution)/shard_map/ppermute | solution.py:368
  27.4 18.5 %collective-permute-start.12 = (bf16[1568,128]{1,0:T(8,128)(2,1)S(1)}, bf16[1568,128]{1,0:T(8,128)(2,1)S(1)}, u32[]{:S(2)}, u32[]{:S(2)}) collective-permute-start(bf16[1568,128]{1,0:T(8,128)(2,1)S(1)} %collective-permute-done.5.refs_3_), channel_id=1, source_target_pairs={{0,4},{1,5},{2,6},{3,7},{8,0},{9,1},{10,2},{11,3},{16,8},{17,9},{1... | collective-permute-start | bytes 1204232 | tf_op jit(solution)/shard_map/ppermute | solution.py:368
  35.5 17.4 %collective-permute-start.8 = (bf16[1536,128]{1,0:T(8,128)(2,1)S(1)}, bf16[1536,128]{1,0:T(8,128)(2,1)S(1)}, u32[]{:S(2)}, u32[]{:S(2)}) collective-permute-start(bf16[1536,128]{1,0:T(8,128)(2,1)S(1)} %collective-permute-done.2.refs_0_), channel_id=1, source_target_pairs={{0,8},{1,9},{2,10},{3,11},{8,16},{9,17},{10,18},{11,19},{16,24},{1... | collective-permute-start | bytes 1179656 | tf_op jit(solution)/shard_map/ppermute | solution.py:368
  36.1 16.7 %collective-permute-start.9 = (bf16[1536,128]{1,0:T(8,128)(2,1)S(1)}, bf16[1536,128]{1,0:T(8,128)(2,1)S(1)}, u32[]{:S(2)}, u32[]{:S(2)}) collective-permute-start(bf16[1536,128]{1,0:T(8,128)(2,1)S(1)} %collective-permute-done.7.refs_2_), channel_id=1, source_target_pairs={{0,4},{1,5},{2,6},{3,7},{8,0},{9,1},{10,2},{11,3},{16,8},{17,9},{1... | collective-permute-start | bytes 1179656 | tf_op jit(solution)/shard_map/ppermute | solution.py:368
  37.5 15.3 %collective-permute-start.10 = (bf16[32,128]{1,0:T(8,128)(2,1)S(1)}, bf16[32,128]{1,0:T(8,128)(2,1)S(1)}, u32[]{:S(2)}, u32[]{:S(2)}) collective-permute-start(bf16[32,128]{1,0:T(8,128)(2,1)S(1)} %get-tuple-element.50), channel_id=1, source_target_pairs={{0,28},{1,29},{2,30},{3,31},{8,20},{9,21},{10,22},{11,23},{16,12},... | collective-permute-start | bytes 24584 | tf_op jit(solution)/shard_map/ppermute | solution.py:368
  45.9 14.1 %collective-permute-start.15 = (bf16[1568,128]{1,0:T(8,128)(2,1)S(1)}, bf16[1568,128]{1,0:T(8,128)(2,1)S(1)}, u32[]{:S(2)}, u32[]{:S(2)}) collective-permute-start(bf16[1568,128]{1,0:T(8,128)(2,1)S(1)} %collective-permute-done.11.refs_1_), channel_id=1, source_target_pairs={{0,8},{1,9},{2,10},{3,11},{8,16},{9,17},{10,18},{11,19},{16,24},{1... | collective-permute-start | bytes 1204232 | tf_op jit(solution)/shard_map/ppermute | solution.py:368
  45.9 14.0 %collective-permute-start.16 = (bf16[1568,128]{1,0:T(8,128)(2,1)S(1)}, bf16[1568,128]{1,0:T(8,128)(2,1)S(1)}, u32[]{:S(2)}, u32[]{:S(2)}) collective-permute-start(bf16[1568,128]{1,0:T(8,128)(2,1)S(1)} %collective-permute-done.12.refs_3_), channel_id=1, source_target_pairs={{0,4},{1,5},{2,6},{3,7},{8,0},{9,1},{10,2},{11,3},{16,8},{17,9},{1... | collective-permute-start | bytes 1204232 | tf_op jit(solution)/shard_map/ppermute | solution.py:368
  57.7 9.4 %collective-permute-start.13 = (bf16[1536,128]{1,0:T(8,128)(2,1)S(1)}, bf16[1536,128]{1,0:T(8,128)(2,1)S(1)}, u32[]{:S(2)}, u32[]{:S(2)}) collective-permute-start(bf16[1536,128]{1,0:T(8,128)(2,1)S(1)} %collective-permute-done.8.refs_0_), channel_id=1, source_target_pairs={{0,8},{1,9},{2,10},{3,11},{8,16},{9,17},{10,18},{11,19},{16,24},{1... | collective-permute-start | bytes 1179656 | tf_op jit(solution)/shard_map/ppermute | solution.py:368
  57.8 9.7 %collective-permute-start.14 = (bf16[1536,128]{1,0:T(8,128)(2,1)S(1)}, bf16[1536,128]{1,0:T(8,128)(2,1)S(1)}, u32[]{:S(2)}, u32[]{:S(2)}) collective-permute-start(bf16[1536,128]{1,0:T(8,128)(2,1)S(1)} %collective-permute-done.9.refs_2_), channel_id=1, source_target_pairs={{0,4},{1,5},{2,6},{3,7},{8,0},{9,1},{10,2},{11,3},{16,8},{17,9},{1... | collective-permute-start | bytes 1179656 | tf_op jit(solution)/shard_map/ppermute | solution.py:368

commit v7 on v6

--- a/solution.py
+++ b/solution.py
@@ -54,7 +54,7 @@
         compiler_params=pltpu.CompilerParams(vmem_limit_bytes=32 * 1024 * 1024),
         cost_estimate=pl.CostEstimate(flops=UCOST, bytes_accessed=1, transcendentals=0),
         name="unit_blocks",
-    )(blocks)
+    )(pltpu.with_memory_space_constraint(blocks, pltpu.HBM))
 
 
 def mask(m):

time: 86.9 us -> 86.9 us (level)
  local copies, waits for them, and re-layouts: 3.61 us -> 1.42 us
  waiting for transfers between devices: 13.8 us -> 15.2 us
  Pallas kernels: 33.2 us -> 34.1 us
    unnamed x2 -> x0, local copies, waits for them, and re-layouts: 2.19 us -> none
    ppermute x16, waiting for transfers between devices: 13.8 us -> 15.2 us  [send(): return lax.ppermute(array, ('art', 'seq'), turn(step, across))]
    pallas_call x2, Pallas kernels: 7.26 us -> 8.2 us  [unit_blocks(): pl.pallas_call(functools.partial(unit_kernel, parts), out_shape=jax.Shape...]
  transfers between devices with their start and end apart: 17 -> 17, of which waited for: 7 -> 8; matrix products, arithmetic and copies ran while one was open for 3% -> 3% of each run, Pallas kernels for 32% -> 33%
where the time goes in v7:
time: 86.9 us; the launch traced here: 86.6 us
  Pallas kernels  34.1 us (39%)
  starting transfers between devices  21.1 us (24%)
  waiting for transfers between devices  15.2 us (17%)
  blocking collectives  13.2 us (15%)
  local copies, waits for them, and re-layouts  1.42 us (2%)
    pallas_call x5, Pallas kernels, score_chunks(): pl.pallas_call(functools.partial(score_kernel, (plans, len(far), len(othe...  22.4 us
    ppermute x16, starting transfers between devices, send(): return lax.ppermute(array, ('art', 'seq'), turn(step, across))  20.5 us
    ppermute x16, waiting for transfers between devices, send(): return lax.ppermute(array, ('art', 'seq'), turn(step, across))  15.2 us
    all_to_all x1, blocking collectives, per_device(): lax.all_to_all(spread, ('art', 'seq'), split_axis=0, concat_axis=0, tiled...  13.2 us
    pallas_call x2, Pallas kernels, unit_blocks(): pl.pallas_call(functools.partial(unit_kernel, parts), out_shape=jax.Shape...  8.2 us
    pallas_call x1, Pallas kernels, pack_streams(): pl.pallas_call(functools.partial(pack_kernel, chips, blocks), out_shape=[...  1.85 us
  transfers between devices with their start and end apart: 17, of which 8 were waited for; matrix products, arithmetic and copies ran while one was open for 3% of the time, Pallas kernels for 33%

profile of v7, /device:TPU:0, one launch (start us, length us, event | category | flops | bytes accessed | tf_op | source)
XLA Modules:
  0.0 86.6 jit_solution(11678862632653097472)
XLA Ops:
  2.3 2.6 %collective-permute-start = (bf16[1536,128]{1,0:T(8,128)(2,1)S(1)}, bf16[1536,128]{1,0:T(8,128)(2,1)S(1)}, u32[]{:S(2)}, u32[]{:S(2)}) collective-permute-start(bf16[1536,128]{1,0:T(8,128)(2,1)S(1)} %bitcast.6), channel_id=1, source_target_pairs={{0,8},{1,9},{2,10},{3,11},{8,16},{9,17},{10,18},{11,19},{16,24},{1... | collective-permute-start | bytes 1179656 | tf_op jit(solution)/shard_map/ppermute | solution.py:368
  6.0 2.0 %collective-permute-start.3 = (s32[6,128]{1,0:T(8,128)S(1)}, s32[6,128]{1,0:T(8,128)S(1)}, u32[]{:S(2)}, u32[]{:S(2)}) collective-permute-start(s32[6,128]{1,0:T(8,128)S(1)} %reshape.14.refs_0_), channel_id=1, source_target_pairs={{0,1},{1,0},{2,3},{3,2},{8,9},{9,8},{10,11},{11,10},{16,17},{17,16... | collective-permute-start | bytes 9224 | tf_op jit(solution)/shard_map/ppermute | solution.py:368
  8.1 1.6 %collective-permute-done.3.refs_1_ = s32[6,128]{1,0:T(8,128)S(1)} collective-permute-done((s32[6,128]{1,0:T(8,128)S(1)}, s32[6,128]{1,0:T(8,128)S(1)}, u32[]{:S(2)}, u32[]{:S(2)}) %collective-permute-start.3) | collective-permute-done | bytes 3104 | tf_op jit(solution)/shard_map/ppermute | solution.py:368
  9.7 1.8 %pack_streams.1 = (bf16[1568,128]{1,0:T(8,128)(2,1)S(1)}, bf16[1568,128]{1,0:T(8,128)(2,1)S(1)}, bf16[32,128]{1,0:T(8,128)(2,1)S(1)}) custom-call(s32[3]{0:T(128)S(1)} %pad_add_fusion.me_ref, s32[6,128]{1,0:T(8,128)S(1)} %reshape.14.refs_0_, s32[6,128]{1,0:T(8,128)S(1)} %collective-permute-done.3.refs_1_, bf16[1536,128]{1,0:T(8,128)(2,1)S(1)} %bitcast.7, ...), custom_call_target="tpu_custom_call" | custom-call | flops 1 | bytes 1 | tf_op jit(solution)/shard_map/pack_streams/pallas_call | solution.py:146
  11.5 2.1 %collective-permute-start.4 = (bf16[1568,128]{1,0:T(8,128)(2,1)S(1)}, bf16[1568,128]{1,0:T(8,128)(2,1)S(1)}, u32[]{:S(2)}, u32[]{:S(2)}) collective-permute-start(bf16[1568,128]{1,0:T(8,128)(2,1)S(1)} %get-tuple-element.37.refs_1_), channel_id=1, source_target_pairs={{0,8},{1,9},{2,10},{3,11},{8,16},{9,17},{10,18},{11,19},{16,24},{1... | collective-permute-start | bytes 1204232 | tf_op jit(solution)/shard_map/ppermute | solution.py:368
  13.6 1.3 %collective-permute-done.refs_0_ = bf16[1536,128]{1,0:T(8,128)(2,1)S(1)} collective-permute-done((bf16[1536,128]{1,0:T(8,128)(2,1)S(1)}, bf16[1536,128]{1,0:T(8,128)(2,1)S(1)}, u32[]{:S(2)}, u32[]{:S(2)}) %collective-permute-start) | collective-permute-done | bytes 393248 | tf_op jit(solution)/shard_map/ppermute | solution.py:368
  14.9 2.0 %collective-permute-done.1.refs_2_ = bf16[1536,128]{1,0:T(8,128)(2,1)S(1)} collective-permute-done((bf16[1536,128]{1,0:T(8,128)(2,1)S(1)}, bf16[1536,128]{1,0:T(8,128)(2,1)S(1)}, u32[]{:S(2)}, u32[]{:S(2)}) %collective-permute-start.1) | collective-permute-done | bytes 393248 | tf_op jit(solution)/shard_map/ppermute | solution.py:368
  16.9 1.6 %collective-permute-start.2 = (bf16[1536,128]{1,0:T(8,128)(2,1)S(1)}, bf16[1536,128]{1,0:T(8,128)(2,1)S(1)}, u32[]{:S(2)}, u32[]{:S(2)}) collective-permute-start(bf16[1536,128]{1,0:T(8,128)(2,1)S(1)} %collective-permute-done.refs_0_), channel_id=1, source_target_pairs={{0,8},{1,9},{2,10},{3,11},{8,16},{9,17},{10,18},{11,19},{16,24},{1... | collective-permute-start | bytes 1179656 | tf_op jit(solution)/shard_map/ppermute | solution.py:368
  18.9 4.1 %unit_blocks.2.refs_2_.refs_4_.refs_10_ = bf16[256,64,128]{2,1,0:T(8,128)(2,1)S(1)} custom-call(bf16[256,64,128]{2,1,0:T(8,128)(2,1)} %blocks_ref), custom_call_target="tpu_custom_call" | custom-call | flops 4000000000 | bytes 1 | tf_op jit(solution)/shard_map/unit_blocks/pallas_call | solution.py:45
  23.8 2.0 %collective-permute-done.5.refs_3_ = bf16[1568,128]{1,0:T(8,128)(2,1)S(1)} collective-permute-done((bf16[1568,128]{1,0:T(8,128)(2,1)S(1)}, bf16[1568,128]{1,0:T(8,128)(2,1)S(1)}, u32[]{:S(2)}, u32[]{:S(2)}) %collective-permute-start.5) | collective-permute-done | bytes 401440 | tf_op jit(solution)/shard_map/ppermute | solution.py:368
  25.8 1.6 %collective-permute-start.11 = (bf16[1568,128]{1,0:T(8,128)(2,1)S(1)}, bf16[1568,128]{1,0:T(8,128)(2,1)S(1)}, u32[]{:S(2)}, u32[]{:S(2)}) collective-permute-start(bf16[1568,128]{1,0:T(8,128)(2,1)S(1)} %collective-permute-done.4.refs_1_), channel_id=1, source_target_pairs={{0,8},{1,9},{2,10},{3,11},{8,16},{9,17},{10,18},{11,19},{16,24},{1... | collective-permute-start | bytes 1204232 | tf_op jit(solution)/shard_map/ppermute | solution.py:368
  27.8 4.1 %unit_blocks.3.refs_3_.refs_5_.refs_11_ = bf16[256,64,128]{2,1,0:T(8,128)(2,1)S(1)} custom-call(bf16[256,64,128]{2,1,0:T(8,128)(2,1)} %collective-permute-done.6.blocks_ref), custom_call_target="tpu_custom_call" | custom-call | flops 4000000000 | bytes 1 | tf_op jit(solution)/shard_map/unit_blocks/pallas_call | solution.py:45
  31.9 3.5 %score_chunks.5.refs_3_ = f32[12,128]{1,0:T(8,128)S(1)} custom-call(s32[3]{0:T(128)S(1)} %pad_add_fusion.me_ref, bf16[1536,128]{1,0:T(8,128)(2,1)S(1)} %bitcast.8, bf16[1568,128]{1,0:T(8,128)(2,1)S(1)} %get-tuple-element.37.refs_1_, bf16[256,64,128]{2,1,0:T(8,128)(2,1)S(1)} %unit_blocks.2.refs_2_.refs_4_.refs_10_, ...), custom_call_target="tpu_custom_call" | custom-call | flops 402653184 | bytes 8388608 | tf_op jit(solution)/shard_map/score_chunks/pallas_call | solution.py:290
  35.5 1.6 %collective-permute-start.8 = (bf16[1536,128]{1,0:T(8,128)(2,1)S(1)}, bf16[1536,128]{1,0:T(8,128)(2,1)S(1)}, u32[]{:S(2)}, u32[]{:S(2)}) collective-permute-start(bf16[1536,128]{1,0:T(8,128)(2,1)S(1)} %collective-permute-done.2.refs_0_), channel_id=1, source_target_pairs={{0,8},{1,9},{2,10},{3,11},{8,16},{9,17},{10,18},{11,19},{16,24},{1... | collective-permute-start | bytes 1179656 | tf_op jit(solution)/shard_map/ppermute | solution.py:368
  37.5 3.4 %collective-permute-start.10 = (bf16[32,128]{1,0:T(8,128)(2,1)S(1)}, bf16[32,128]{1,0:T(8,128)(2,1)S(1)}, u32[]{:S(2)}, u32[]{:S(2)}) collective-permute-start(bf16[32,128]{1,0:T(8,128)(2,1)S(1)} %get-tuple-element.50), channel_id=1, source_target_pairs={{0,28},{1,29},{2,30},{3,31},{8,20},{9,21},{10,22},{11,23},{16,12},... | collective-permute-start | bytes 24584 | tf_op jit(solution)/shard_map/ppermute | solution.py:368
  41.0 4.9 %score_chunks.6 = (f32[12,128]{1,0:T(8,128)S(1)}, f32[12,128]{1,0:T(8,128)S(1)}) custom-call(s32[3]{0:T(128)S(1)} %pad_add_fusion.me_ref, bf16[1536,128]{1,0:T(8,128)(2,1)S(1)} %collective-permute-done.refs_0_, bf16[1568,128]{1,0:T(8,128)(2,1)S(1)} %collective-permute-done.4.refs_1_, bf16[1536,128]{1,0:T(8,128)(2,1)S(1)} %collective-permute-done.1.refs_2_, ...), custom_call_target="tpu_custom_call" | custom-call | flops 805306368 | bytes 8388608 | tf_op jit(solution)/shard_map/score_chunks/pallas_call | solution.py:290
  46.5 1.5 %collective-permute-start.16 = (bf16[1568,128]{1,0:T(8,128)(2,1)S(1)}, bf16[1568,128]{1,0:T(8,128)(2,1)S(1)}, u32[]{:S(2)}, u32[]{:S(2)}) collective-permute-start(bf16[1568,128]{1,0:T(8,128)(2,1)S(1)} %collective-permute-done.12.refs_3_), channel_id=1, source_target_pairs={{0,4},{1,5},{2,6},{3,7},{8,0},{9,1},{10,2},{11,3},{16,8},{17,9},{1... | collective-permute-start | bytes 1204232 | tf_op jit(solution)/shard_map/ppermute | solution.py:368
  47.9 4.9 %collective-permute-done.10.refs_2_ = bf16[32,128]{1,0:T(8,128)(2,1)S(1)} collective-permute-done((bf16[32,128]{1,0:T(8,128)(2,1)S(1)}, bf16[32,128]{1,0:T(8,128)(2,1)S(1)}, u32[]{:S(2)}, u32[]{:S(2)}) %collective-permute-start.10) | collective-permute-done | bytes 8224 | tf_op jit(solution)/shard_map/ppermute | solution.py:368
  52.8 4.9 %score_chunks.7 = (f32[12,128]{1,0:T(8,128)S(1)}, f32[12,128]{1,0:T(8,128)S(1)}) custom-call(s32[3]{0:T(128)S(1)} %pad_add_fusion.me_ref, bf16[1536,128]{1,0:T(8,128)(2,1)S(1)} %collective-permute-done.2.refs_0_, bf16[1568,128]{1,0:T(8,128)(2,1)S(1)} %collective-permute-done.11.refs_1_, bf16[1536,128]{1,0:T(8,128)(2,1)S(1)} %collective-permute-done.7.refs_2_, ...), custom_call_target="tpu_custom_call" | custom-call | flops 805306368 | bytes 8388608 | tf_op jit(solution)/shard_map/score_chunks/pallas_call | solution.py:290
  59.9 5.0 %score_chunks.8 = (f32[12,128]{1,0:T(8,128)S(1)}, f32[12,128]{1,0:T(8,128)S(1)}) custom-call(s32[3]{0:T(128)S(1)} %pad_add_fusion.me_ref, bf16[1536,128]{1,0:T(8,128)(2,1)S(1)} %collective-permute-done.8.refs_0_, bf16[1568,128]{1,0:T(8,128)(2,1)S(1)} %collective-permute-done.15.refs_1_, bf16[1536,128]{1,0:T(8,128)(2,1)S(1)} %collective-permute-done.9.refs_2_, ...), custom_call_target="tpu_custom_call" | custom-call | flops 805306368 | bytes 8388608 | tf_op jit(solution)/shard_map/score_chunks/pallas_call | solution.py:290
  65.0 2.2 %collective-permute-done.13.refs_0_ = bf16[1536,128]{1,0:T(8,128)(2,1)S(1)} collective-permute-done((bf16[1536,128]{1,0:T(8,128)(2,1)S(1)}, bf16[1536,128]{1,0:T(8,128)(2,1)S(1)}, u32[]{:S(2)}, u32[]{:S(2)}) %collective-permute-start.13) | collective-permute-done | bytes 393248 | tf_op jit(solution)/shard_map/ppermute | solution.py:368
  67.6 4.1 %score_chunks.9 = (f32[12,128]{1,0:T(8,128)}, f32[256,128]{1,0:T(8,128)S(1)}) custom-call(s32[3]{0:T(128)S(1)} %pad_add_fusion.me_ref, bf16[1536,128]{1,0:T(8,128)(2,1)S(1)} %collective-permute-done.13.refs_0_, bf16[1536,128]{1,0:T(8,128)(2,1)S(1)} %collective-permute-done.14.refs_1_, bf16[32,128]{1,0:T(8,128)(2,1)S(1)} %collective-permute-done.10.refs_2_, ...), custom_call_target="tpu_custom_call" | custom-call | flops 402653184 | bytes 8388608 | tf_op jit(solution)/shard_map/score_chunks/pallas_call | solution.py:290
  71.7 13.2 %all_to_all.9.parts_ref = f32[32,8,128]{2,1,0:T(8,128)} all-to-all(f32[32,8,128]{2,1,0:T(8,128)S(1)} %bitcast.11), channel_id=1, replica_groups=mesh['art'=16,'seq'=2] {'art','seq'}, dimensions={0} | all-to-all | bytes 262144 | tf_op jit(solution)/shard_map/all_to_all | solution.py:415
  84.9 1.7 %close.1 = (f32[12,64]{1,0:T(8,128)}, f32[12,64]{1,0:T(8,128)}) custom-call(f32[32,8,128]{2,1,0:T(8,128)} %all_to_all.9.parts_ref), custom_call_target="tpu_custom_call" | custom-call | tf_op jit(solution)/shard_map/close/pallas_call | solution.py:331
  (25 shorter events, 8.2 us)
Async XLA Ops:
  0.6 27.2 %collective-permute-start.6 = (bf16[256,64,128]{2,1,0:T(8,128)(2,1)}, bf16[256,64,128]{2,1,0:T(8,128)(2,1)}, u32[]{:S(2)}, u32[]{:S(2)}) collective-permute-start(bf16[256,64,128]{2,1,0:T(8,128)(2,1)} %blocks_ref), channel_id=1, source_target_pairs={{0,2},{2,0},{4,6},{6,4},{8,10},{10,8},{12,14},{14,12},{16,18},{18,... | collective-permute-start | bytes 12582920 | tf_op jit(solution)/shard_map/ppermute | solution.py:383
  2.3 12.6 %collective-permute-start = (bf16[1536,128]{1,0:T(8,128)(2,1)S(1)}, bf16[1536,128]{1,0:T(8,128)(2,1)S(1)}, u32[]{:S(2)}, u32[]{:S(2)}) collective-permute-start(bf16[1536,128]{1,0:T(8,128)(2,1)S(1)} %bitcast.6), channel_id=1, source_target_pairs={{0,8},{1,9},{2,10},{3,11},{8,16},{9,17},{10,18},{11,19},{16,24},{1... | collective-permute-start | bytes 1179656 | tf_op jit(solution)/shard_map/ppermute | solution.py:368
  5.0 11.9 %collective-permute-start.1 = (bf16[1536,128]{1,0:T(8,128)(2,1)S(1)}, bf16[1536,128]{1,0:T(8,128)(2,1)S(1)}, u32[]{:S(2)}, u32[]{:S(2)}) collective-permute-start(bf16[1536,128]{1,0:T(8,128)(2,1)S(1)} %bitcast.9), channel_id=1, source_target_pairs={{0,4},{1,5},{2,6},{3,7},{8,0},{9,1},{10,2},{11,3},{16,8},{17,9},{1... | collective-permute-start | bytes 1179656 | tf_op jit(solution)/shard_map/ppermute | solution.py:368
  6.0 3.7 %collective-permute-start.3 = (s32[6,128]{1,0:T(8,128)S(1)}, s32[6,128]{1,0:T(8,128)S(1)}, u32[]{:S(2)}, u32[]{:S(2)}) collective-permute-start(s32[6,128]{1,0:T(8,128)S(1)} %reshape.14.refs_0_), channel_id=1, source_target_pairs={{0,1},{1,0},{2,3},{3,2},{8,9},{9,8},{10,11},{11,10},{16,17},{17,16... | collective-permute-start | bytes 9224 | tf_op jit(solution)/shard_map/ppermute | solution.py:368
  11.5 12.3 %collective-permute-start.4 = (bf16[1568,128]{1,0:T(8,128)(2,1)S(1)}, bf16[1568,128]{1,0:T(8,128)(2,1)S(1)}, u32[]{:S(2)}, u32[]{:S(2)}) collective-permute-start(bf16[1568,128]{1,0:T(8,128)(2,1)S(1)} %get-tuple-element.37.refs_1_), channel_id=1, source_target_pairs={{0,8},{1,9},{2,10},{3,11},{8,16},{9,17},{10,18},{11,19},{16,24},{1... | collective-permute-start | bytes 1204232 | tf_op jit(solution)/shard_map/ppermute | solution.py:368
  13.6 12.2 %collective-permute-start.5 = (bf16[1568,128]{1,0:T(8,128)(2,1)S(1)}, bf16[1568,128]{1,0:T(8,128)(2,1)S(1)}, u32[]{:S(2)}, u32[]{:S(2)}) collective-permute-start(bf16[1568,128]{1,0:T(8,128)(2,1)S(1)} %get-tuple-element.38), channel_id=1, source_target_pairs={{0,4},{1,5},{2,6},{3,7},{8,0},{9,1},{10,2},{11,3},{16,8},{17,9},{1... | collective-permute-start | bytes 1204232 | tf_op jit(solution)/shard_map/ppermute | solution.py:368
  16.9 18.5 %collective-permute-start.2 = (bf16[1536,128]{1,0:T(8,128)(2,1)S(1)}, bf16[1536,128]{1,0:T(8,128)(2,1)S(1)}, u32[]{:S(2)}, u32[]{:S(2)}) collective-permute-start(bf16[1536,128]{1,0:T(8,128)(2,1)S(1)} %collective-permute-done.refs_0_), channel_id=1, source_target_pairs={{0,8},{1,9},{2,10},{3,11},{8,16},{9,17},{10,18},{11,19},{16,24},{1... | collective-permute-start | bytes 1179656 | tf_op jit(solution)/shard_map/ppermute | solution.py:368
  18.5 17.0 %collective-permute-start.7 = (bf16[1536,128]{1,0:T(8,128)(2,1)S(1)}, bf16[1536,128]{1,0:T(8,128)(2,1)S(1)}, u32[]{:S(2)}, u32[]{:S(2)}) collective-permute-start(bf16[1536,128]{1,0:T(8,128)(2,1)S(1)} %collective-permute-done.1.refs_2_), channel_id=1, source_target_pairs={{0,4},{1,5},{2,6},{3,7},{8,0},{9,1},{10,2},{11,3},{16,8},{17,9},{1... | collective-permute-start | bytes 1179656 | tf_op jit(solution)/shard_map/ppermute | solution.py:368
  25.8 20.1 %collective-permute-start.11 = (bf16[1568,128]{1,0:T(8,128)(2,1)S(1)}, bf16[1568,128]{1,0:T(8,128)(2,1)S(1)}, u32[]{:S(2)}, u32[]{:S(2)}) collective-permute-start(bf16[1568,128]{1,0:T(8,128)(2,1)S(1)} %collective-permute-done.4.refs_1_), channel_id=1, source_target_pairs={{0,8},{1,9},{2,10},{3,11},{8,16},{9,17},{10,18},{11,19},{16,24},{1... | collective-permute-start | bytes 1204232 | tf_op jit(solution)/shard_map/ppermute | solution.py:368
  27.4 18.5 %collective-permute-start.12 = (bf16[1568,128]{1,0:T(8,128)(2,1)S(1)}, bf16[1568,128]{1,0:T(8,128)(2,1)S(1)}, u32[]{:S(2)}, u32[]{:S(2)}) collective-permute-start(bf16[1568,128]{1,0:T(8,128)(2,1)S(1)} %collective-permute-done.5.refs_3_), channel_id=1, source_target_pairs={{0,4},{1,5},{2,6},{3,7},{8,0},{9,1},{10,2},{11,3},{16,8},{17,9},{1... | collective-permute-start | bytes 1204232 | tf_op jit(solution)/shard_map/ppermute | solution.py:368
  35.5 17.4 %collective-permute-start.8 = (bf16[1536,128]{1,0:T(8,128)(2,1)S(1)}, bf16[1536,128]{1,0:T(8,128)(2,1)S(1)}, u32[]{:S(2)}, u32[]{:S(2)}) collective-permute-start(bf16[1536,128]{1,0:T(8,128)(2,1)S(1)} %collective-permute-done.2.refs_0_), channel_id=1, source_target_pairs={{0,8},{1,9},{2,10},{3,11},{8,16},{9,17},{10,18},{11,19},{16,24},{1... | collective-permute-start | bytes 1179656 | tf_op jit(solution)/shard_map/ppermute | solution.py:368
  37.1 15.7 %collective-permute-start.9 = (bf16[1536,128]{1,0:T(8,128)(2,1)S(1)}, bf16[1536,128]{1,0:T(8,128)(2,1)S(1)}, u32[]{:S(2)}, u32[]{:S(2)}) collective-permute-start(bf16[1536,128]{1,0:T(8,128)(2,1)S(1)} %collective-permute-done.7.refs_2_), channel_id=1, source_target_pairs={{0,4},{1,5},{2,6},{3,7},{8,0},{9,1},{10,2},{11,3},{16,8},{17,9},{1... | collective-permute-start | bytes 1179656 | tf_op jit(solution)/shard_map/ppermute | solution.py:368
  37.5 15.3 %collective-permute-start.10 = (bf16[32,128]{1,0:T(8,128)(2,1)S(1)}, bf16[32,128]{1,0:T(8,128)(2,1)S(1)}, u32[]{:S(2)}, u32[]{:S(2)}) collective-permute-start(bf16[32,128]{1,0:T(8,128)(2,1)S(1)} %get-tuple-element.50), channel_id=1, source_target_pairs={{0,28},{1,29},{2,30},{3,31},{8,20},{9,21},{10,22},{11,23},{16,12},... | collective-permute-start | bytes 24584 | tf_op jit(solution)/shard_map/ppermute | solution.py:368
  45.9 14.1 %collective-permute-start.15 = (bf16[1568,128]{1,0:T(8,128)(2,1)S(1)}, bf16[1568,128]{1,0:T(8,128)(2,1)S(1)}, u32[]{:S(2)}, u32[]{:S(2)}) collective-permute-start(bf16[1568,128]{1,0:T(8,128)(2,1)S(1)} %collective-permute-done.11.refs_1_), channel_id=1, source_target_pairs={{0,8},{1,9},{2,10},{3,11},{8,16},{9,17},{10,18},{11,19},{16,24},{1... | collective-permute-start | bytes 1204232 | tf_op jit(solution)/shard_map/ppermute | solution.py:368
  46.5 13.4 %collective-permute-start.16 = (bf16[1568,128]{1,0:T(8,128)(2,1)S(1)}, bf16[1568,128]{1,0:T(8,128)(2,1)S(1)}, u32[]{:S(2)}, u32[]{:S(2)}) collective-permute-start(bf16[1568,128]{1,0:T(8,128)(2,1)S(1)} %collective-permute-done.12.refs_3_), channel_id=1, source_target_pairs={{0,4},{1,5},{2,6},{3,7},{8,0},{9,1},{10,2},{11,3},{16,8},{17,9},{1... | collective-permute-start | bytes 1204232 | tf_op jit(solution)/shard_map/ppermute | solution.py:368
  57.7 9.4 %collective-permute-start.13 = (bf16[1536,128]{1,0:T(8,128)(2,1)S(1)}, bf16[1536,128]{1,0:T(8,128)(2,1)S(1)}, u32[]{:S(2)}, u32[]{:S(2)}) collective-permute-start(bf16[1536,128]{1,0:T(8,128)(2,1)S(1)} %collective-permute-done.8.refs_0_), channel_id=1, source_target_pairs={{0,8},{1,9},{2,10},{3,11},{8,16},{9,17},{10,18},{11,19},{16,24},{1... | collective-permute-start | bytes 1179656 | tf_op jit(solution)/shard_map/ppermute | solution.py:368
  58.9 8.8 %collective-permute-start.14 = (bf16[1536,128]{1,0:T(8,128)(2,1)S(1)}, bf16[1536,128]{1,0:T(8,128)(2,1)S(1)}, u32[]{:S(2)}, u32[]{:S(2)}) collective-permute-start(bf16[1536,128]{1,0:T(8,128)(2,1)S(1)} %collective-permute-done.9.refs_2_), channel_id=1, source_target_pairs={{0,4},{1,5},{2,6},{3,7},{8,0},{9,1},{10,2},{11,3},{16,8},{17,9},{1... | collective-permute-start | bytes 1179656 | tf_op jit(solution)/shard_map/ppermute | solution.py:368

commit v8 on v7

--- a/solution.py
+++ b/solution.py
@@ -15,7 +15,7 @@
 GROUP = 4
 UCOST = 4000000000
 SCOST = 2.0
-UNROLL = 20
+UNROLL = 24
 PREP = 3
 LAST = (((1,), (1,)), ((), ()))
 

time: 86.9 us -> 87.1 us (level)
  Pallas kernels: 34.1 us -> 36.4 us
  starting transfers between devices: 21.1 us -> 19.9 us
    pallas_call x5, Pallas kernels: 22.4 us -> 24.6 us  [score_chunks(): pl.pallas_call(functools.partial(score_kernel, (plans, len(far), len(othe...]
    ppermute x16, starting transfers between devices: 20.5 us -> 19.4 us  [send(): return lax.ppermute(array, ('art', 'seq'), turn(step, across))]
  transfers between devices with their start and end apart: 17 -> 17, of which waited for: 8 -> 8; matrix products, arithmetic and copies ran while one was open for 3% -> 3% of each run, Pallas kernels for 33% -> 35%
where the time goes in v8:
time: 87.1 us; the launch traced here: 86.8 us
  Pallas kernels  36.4 us (42%)
  starting transfers between devices  19.9 us (23%)
  waiting for transfers between devices  15.2 us (17%)
  blocking collectives  12.4 us (14%)
  local copies, waits for them, and re-layouts  1.42 us (2%)
    pallas_call x5, Pallas kernels, score_chunks(): pl.pallas_call(functools.partial(score_kernel, (plans, len(far), len(othe...  24.6 us
    ppermute x16, starting transfers between devices, send(): return lax.ppermute(array, ('art', 'seq'), turn(step, across))  19.4 us
    ppermute x16, waiting for transfers between devices, send(): return lax.ppermute(array, ('art', 'seq'), turn(step, across))  15.1 us
    all_to_all x1, blocking collectives, per_device(): lax.all_to_all(spread, ('art', 'seq'), split_axis=0, concat_axis=0, tiled...  12.4 us
    pallas_call x2, Pallas kernels, unit_blocks(): pl.pallas_call(functools.partial(unit_kernel, parts), out_shape=jax.Shape...  8.2 us
    pallas_call x1, Pallas kernels, pack_streams(): pl.pallas_call(functools.partial(pack_kernel, chips, blocks), out_shape=[...  1.85 us
  transfers between devices with their start and end apart: 17, of which 8 were waited for; matrix products, arithmetic and copies ran while one was open for 3% of the time, Pallas kernels for 35%

profile of v8, /device:TPU:0, one launch (start us, length us, event | category | flops | bytes accessed | tf_op | source)
XLA Modules:
  0.0 86.8 jit_solution(17289189757903125632)
XLA Ops:
  2.3 2.6 %collective-permute-start = (bf16[1536,128]{1,0:T(8,128)(2,1)S(1)}, bf16[1536,128]{1,0:T(8,128)(2,1)S(1)}, u32[]{:S(2)}, u32[]{:S(2)}) collective-permute-start(bf16[1536,128]{1,0:T(8,128)(2,1)S(1)} %bitcast.6), channel_id=1, source_target_pairs={{0,8},{1,9},{2,10},{3,11},{8,16},{9,17},{10,18},{11,19},{16,24},{1... | collective-permute-start | bytes 1179656 | tf_op jit(solution)/shard_map/ppermute | solution.py:368
  6.0 2.0 %collective-permute-start.3 = (s32[6,128]{1,0:T(8,128)S(1)}, s32[6,128]{1,0:T(8,128)S(1)}, u32[]{:S(2)}, u32[]{:S(2)}) collective-permute-start(s32[6,128]{1,0:T(8,128)S(1)} %reshape.14.refs_0_), channel_id=1, source_target_pairs={{0,1},{1,0},{2,3},{3,2},{8,9},{9,8},{10,11},{11,10},{16,17},{17,16... | collective-permute-start | bytes 9224 | tf_op jit(solution)/shard_map/ppermute | solution.py:368
  8.1 1.6 %collective-permute-done.3.refs_1_ = s32[6,128]{1,0:T(8,128)S(1)} collective-permute-done((s32[6,128]{1,0:T(8,128)S(1)}, s32[6,128]{1,0:T(8,128)S(1)}, u32[]{:S(2)}, u32[]{:S(2)}) %collective-permute-start.3) | collective-permute-done | bytes 3104 | tf_op jit(solution)/shard_map/ppermute | solution.py:368
  9.7 1.8 %pack_streams.1 = (bf16[1568,128]{1,0:T(8,128)(2,1)S(1)}, bf16[1568,128]{1,0:T(8,128)(2,1)S(1)}, bf16[32,128]{1,0:T(8,128)(2,1)S(1)}) custom-call(s32[3]{0:T(128)S(1)} %pad_add_fusion.me_ref, s32[6,128]{1,0:T(8,128)S(1)} %reshape.14.refs_0_, s32[6,128]{1,0:T(8,128)S(1)} %collective-permute-done.3.refs_1_, bf16[1536,128]{1,0:T(8,128)(2,1)S(1)} %bitcast.7, ...), custom_call_target="tpu_custom_call" | custom-call | flops 1 | bytes 1 | tf_op jit(solution)/shard_map/pack_streams/pallas_call | solution.py:146
  11.5 2.1 %collective-permute-start.4 = (bf16[1568,128]{1,0:T(8,128)(2,1)S(1)}, bf16[1568,128]{1,0:T(8,128)(2,1)S(1)}, u32[]{:S(2)}, u32[]{:S(2)}) collective-permute-start(bf16[1568,128]{1,0:T(8,128)(2,1)S(1)} %get-tuple-element.37.refs_1_), channel_id=1, source_target_pairs={{0,8},{1,9},{2,10},{3,11},{8,16},{9,17},{10,18},{11,19},{16,24},{1... | collective-permute-start | bytes 1204232 | tf_op jit(solution)/shard_map/ppermute | solution.py:368
  14.9 2.0 %collective-permute-done.1.refs_2_ = bf16[1536,128]{1,0:T(8,128)(2,1)S(1)} collective-permute-done((bf16[1536,128]{1,0:T(8,128)(2,1)S(1)}, bf16[1536,128]{1,0:T(8,128)(2,1)S(1)}, u32[]{:S(2)}, u32[]{:S(2)}) %collective-permute-start.1) | collective-permute-done | bytes 393248 | tf_op jit(solution)/shard_map/ppermute | solution.py:368
  16.9 1.6 %collective-permute-start.2 = (bf16[1536,128]{1,0:T(8,128)(2,1)S(1)}, bf16[1536,128]{1,0:T(8,128)(2,1)S(1)}, u32[]{:S(2)}, u32[]{:S(2)}) collective-permute-start(bf16[1536,128]{1,0:T(8,128)(2,1)S(1)} %collective-permute-done.refs_0_), channel_id=1, source_target_pairs={{0,8},{1,9},{2,10},{3,11},{8,16},{9,17},{10,18},{11,19},{16,24},{1... | collective-permute-start | bytes 1179656 | tf_op jit(solution)/shard_map/ppermute | solution.py:368
  18.9 4.1 %unit_blocks.2.refs_2_.refs_4_.refs_10_ = bf16[256,64,128]{2,1,0:T(8,128)(2,1)S(1)} custom-call(bf16[256,64,128]{2,1,0:T(8,128)(2,1)} %blocks_ref), custom_call_target="tpu_custom_call" | custom-call | flops 4000000000 | bytes 1 | tf_op jit(solution)/shard_map/unit_blocks/pallas_call | solution.py:45
  23.8 2.0 %collective-permute-done.5.refs_3_ = bf16[1568,128]{1,0:T(8,128)(2,1)S(1)} collective-permute-done((bf16[1568,128]{1,0:T(8,128)(2,1)S(1)}, bf16[1568,128]{1,0:T(8,128)(2,1)S(1)}, u32[]{:S(2)}, u32[]{:S(2)}) %collective-permute-start.5) | collective-permute-done | bytes 401440 | tf_op jit(solution)/shard_map/ppermute | solution.py:368
  25.8 1.6 %collective-permute-start.11 = (bf16[1568,128]{1,0:T(8,128)(2,1)S(1)}, bf16[1568,128]{1,0:T(8,128)(2,1)S(1)}, u32[]{:S(2)}, u32[]{:S(2)}) collective-permute-start(bf16[1568,128]{1,0:T(8,128)(2,1)S(1)} %collective-permute-done.4.refs_1_), channel_id=1, source_target_pairs={{0,8},{1,9},{2,10},{3,11},{8,16},{9,17},{10,18},{11,19},{16,24},{1... | collective-permute-start | bytes 1204232 | tf_op jit(solution)/shard_map/ppermute | solution.py:368
  27.8 4.1 %unit_blocks.3.refs_3_.refs_5_.refs_11_ = bf16[256,64,128]{2,1,0:T(8,128)(2,1)S(1)} custom-call(bf16[256,64,128]{2,1,0:T(8,128)(2,1)} %collective-permute-done.6.blocks_ref), custom_call_target="tpu_custom_call" | custom-call | flops 4000000000 | bytes 1 | tf_op jit(solution)/shard_map/unit_blocks/pallas_call | solution.py:45
  31.9 3.8 %score_chunks.5.refs_3_ = f32[12,128]{1,0:T(8,128)S(1)} custom-call(s32[3]{0:T(128)S(1)} %pad_add_fusion.me_ref, bf16[1536,128]{1,0:T(8,128)(2,1)S(1)} %bitcast.8, bf16[1568,128]{1,0:T(8,128)(2,1)S(1)} %get-tuple-element.37.refs_1_, bf16[256,64,128]{2,1,0:T(8,128)(2,1)S(1)} %unit_blocks.2.refs_2_.refs_4_.refs_10_, ...), custom_call_target="tpu_custom_call" | custom-call | flops 402653184 | bytes 8388608 | tf_op jit(solution)/shard_map/score_chunks/pallas_call | solution.py:290
  35.8 1.6 %collective-permute-start.8 = (bf16[1536,128]{1,0:T(8,128)(2,1)S(1)}, bf16[1536,128]{1,0:T(8,128)(2,1)S(1)}, u32[]{:S(2)}, u32[]{:S(2)}) collective-permute-start(bf16[1536,128]{1,0:T(8,128)(2,1)S(1)} %collective-permute-done.2.refs_0_), channel_id=1, source_target_pairs={{0,8},{1,9},{2,10},{3,11},{8,16},{9,17},{10,18},{11,19},{16,24},{1... | collective-permute-start | bytes 1179656 | tf_op jit(solution)/shard_map/ppermute | solution.py:368
  37.9 2.3 %collective-permute-start.10 = (bf16[32,128]{1,0:T(8,128)(2,1)S(1)}, bf16[32,128]{1,0:T(8,128)(2,1)S(1)}, u32[]{:S(2)}, u32[]{:S(2)}) collective-permute-start(bf16[32,128]{1,0:T(8,128)(2,1)S(1)} %get-tuple-element.50), channel_id=1, source_target_pairs={{0,28},{1,29},{2,30},{3,31},{8,20},{9,21},{10,22},{11,23},{16,12},... | collective-permute-start | bytes 24584 | tf_op jit(solution)/shard_map/ppermute | solution.py:368
  40.1 5.4 %score_chunks.6 = (f32[12,128]{1,0:T(8,128)S(1)}, f32[12,128]{1,0:T(8,128)S(1)}) custom-call(s32[3]{0:T(128)S(1)} %pad_add_fusion.me_ref, bf16[1536,128]{1,0:T(8,128)(2,1)S(1)} %collective-permute-done.refs_0_, bf16[1568,128]{1,0:T(8,128)(2,1)S(1)} %collective-permute-done.4.refs_1_, bf16[1536,128]{1,0:T(8,128)(2,1)S(1)} %collective-permute-done.1.refs_2_, ...), custom_call_target="tpu_custom_call" | custom-call | flops 805306368 | bytes 8388608 | tf_op jit(solution)/shard_map/score_chunks/pallas_call | solution.py:290
  45.6 1.9 %collective-permute-start.15 = (bf16[1568,128]{1,0:T(8,128)(2,1)S(1)}, bf16[1568,128]{1,0:T(8,128)(2,1)S(1)}, u32[]{:S(2)}, u32[]{:S(2)}) collective-permute-start(bf16[1568,128]{1,0:T(8,128)(2,1)S(1)} %collective-permute-done.11.refs_1_), channel_id=1, source_target_pairs={{0,8},{1,9},{2,10},{3,11},{8,16},{9,17},{10,18},{11,19},{16,24},{1... | collective-permute-start | bytes 1204232 | tf_op jit(solution)/shard_map/ppermute | solution.py:368
  47.6 5.2 %collective-permute-done.10.refs_2_ = bf16[32,128]{1,0:T(8,128)(2,1)S(1)} collective-permute-done((bf16[32,128]{1,0:T(8,128)(2,1)S(1)}, bf16[32,128]{1,0:T(8,128)(2,1)S(1)}, u32[]{:S(2)}, u32[]{:S(2)}) %collective-permute-start.10) | collective-permute-done | bytes 8224 | tf_op jit(solution)/shard_map/ppermute | solution.py:368
  52.8 5.4 %score_chunks.7 = (f32[12,128]{1,0:T(8,128)S(1)}, f32[12,128]{1,0:T(8,128)S(1)}) custom-call(s32[3]{0:T(128)S(1)} %pad_add_fusion.me_ref, bf16[1536,128]{1,0:T(8,128)(2,1)S(1)} %collective-permute-done.2.refs_0_, bf16[1568,128]{1,0:T(8,128)(2,1)S(1)} %collective-permute-done.11.refs_1_, bf16[1536,128]{1,0:T(8,128)(2,1)S(1)} %collective-permute-done.7.refs_2_, ...), custom_call_target="tpu_custom_call" | custom-call | flops 805306368 | bytes 8388608 | tf_op jit(solution)/shard_map/score_chunks/pallas_call | solution.py:290
  58.2 1.3 %collective-permute-start.13 = (bf16[1536,128]{1,0:T(8,128)(2,1)S(1)}, bf16[1536,128]{1,0:T(8,128)(2,1)S(1)}, u32[]{:S(2)}, u32[]{:S(2)}) collective-permute-start(bf16[1536,128]{1,0:T(8,128)(2,1)S(1)} %collective-permute-done.8.refs_0_), channel_id=1, source_target_pairs={{0,8},{1,9},{2,10},{3,11},{8,16},{9,17},{10,18},{11,19},{16,24},{1... | collective-permute-start | bytes 1179656 | tf_op jit(solution)/shard_map/ppermute | solution.py:368
  60.5 5.6 %score_chunks.8 = (f32[12,128]{1,0:T(8,128)S(1)}, f32[12,128]{1,0:T(8,128)S(1)}) custom-call(s32[3]{0:T(128)S(1)} %pad_add_fusion.me_ref, bf16[1536,128]{1,0:T(8,128)(2,1)S(1)} %collective-permute-done.8.refs_0_, bf16[1568,128]{1,0:T(8,128)(2,1)S(1)} %collective-permute-done.15.refs_1_, bf16[1536,128]{1,0:T(8,128)(2,1)S(1)} %collective-permute-done.9.refs_2_, ...), custom_call_target="tpu_custom_call" | custom-call | flops 805306368 | bytes 8388608 | tf_op jit(solution)/shard_map/score_chunks/pallas_call | solution.py:290
  66.0 1.6 %collective-permute-done.13.refs_0_ = bf16[1536,128]{1,0:T(8,128)(2,1)S(1)} collective-permute-done((bf16[1536,128]{1,0:T(8,128)(2,1)S(1)}, bf16[1536,128]{1,0:T(8,128)(2,1)S(1)}, u32[]{:S(2)}, u32[]{:S(2)}) %collective-permute-start.13) | collective-permute-done | bytes 393248 | tf_op jit(solution)/shard_map/ppermute | solution.py:368
  68.3 4.4 %score_chunks.9 = (f32[12,128]{1,0:T(8,128)}, f32[256,128]{1,0:T(8,128)S(1)}) custom-call(s32[3]{0:T(128)S(1)} %pad_add_fusion.me_ref, bf16[1536,128]{1,0:T(8,128)(2,1)S(1)} %collective-permute-done.13.refs_0_, bf16[1536,128]{1,0:T(8,128)(2,1)S(1)} %collective-permute-done.14.refs_1_, bf16[32,128]{1,0:T(8,128)(2,1)S(1)} %collective-permute-done.10.refs_2_, ...), custom_call_target="tpu_custom_call" | custom-call | flops 402653184 | bytes 8388608 | tf_op jit(solution)/shard_map/score_chunks/pallas_call | solution.py:290
  72.7 12.4 %all_to_all.9.parts_ref = f32[32,8,128]{2,1,0:T(8,128)} all-to-all(f32[32,8,128]{2,1,0:T(8,128)S(1)} %bitcast.11), channel_id=1, replica_groups=mesh['art'=16,'seq'=2] {'art','seq'}, dimensions={0} | all-to-all | bytes 262144 | tf_op jit(solution)/shard_map/all_to_all | solution.py:415
  85.1 1.7 %close.1 = (f32[12,64]{1,0:T(8,128)}, f32[12,64]{1,0:T(8,128)}) custom-call(f32[32,8,128]{2,1,0:T(8,128)} %all_to_all.9.parts_ref), custom_call_target="tpu_custom_call" | custom-call | tf_op jit(solution)/shard_map/close/pallas_call | solution.py:331
  (25 shorter events, 7.8 us)
Async XLA Ops:
  0.6 27.2 %collective-permute-start.6 = (bf16[256,64,128]{2,1,0:T(8,128)(2,1)}, bf16[256,64,128]{2,1,0:T(8,128)(2,1)}, u32[]{:S(2)}, u32[]{:S(2)}) collective-permute-start(bf16[256,64,128]{2,1,0:T(8,128)(2,1)} %blocks_ref), channel_id=1, source_target_pairs={{0,2},{2,0},{4,6},{6,4},{8,10},{10,8},{12,14},{14,12},{16,18},{18,... | collective-permute-start | bytes 12582920 | tf_op jit(solution)/shard_map/ppermute | solution.py:383
  2.3 12.6 %collective-permute-start = (bf16[1536,128]{1,0:T(8,128)(2,1)S(1)}, bf16[1536,128]{1,0:T(8,128)(2,1)S(1)}, u32[]{:S(2)}, u32[]{:S(2)}) collective-permute-start(bf16[1536,128]{1,0:T(8,128)(2,1)S(1)} %bitcast.6), channel_id=1, source_target_pairs={{0,8},{1,9},{2,10},{3,11},{8,16},{9,17},{10,18},{11,19},{16,24},{1... | collective-permute-start | bytes 1179656 | tf_op jit(solution)/shard_map/ppermute | solution.py:368
  5.0 11.9 %collective-permute-start.1 = (bf16[1536,128]{1,0:T(8,128)(2,1)S(1)}, bf16[1536,128]{1,0:T(8,128)(2,1)S(1)}, u32[]{:S(2)}, u32[]{:S(2)}) collective-permute-start(bf16[1536,128]{1,0:T(8,128)(2,1)S(1)} %bitcast.9), channel_id=1, source_target_pairs={{0,4},{1,5},{2,6},{3,7},{8,0},{9,1},{10,2},{11,3},{16,8},{17,9},{1... | collective-permute-start | bytes 1179656 | tf_op jit(solution)/shard_map/ppermute | solution.py:368
  6.0 3.7 %collective-permute-start.3 = (s32[6,128]{1,0:T(8,128)S(1)}, s32[6,128]{1,0:T(8,128)S(1)}, u32[]{:S(2)}, u32[]{:S(2)}) collective-permute-start(s32[6,128]{1,0:T(8,128)S(1)} %reshape.14.refs_0_), channel_id=1, source_target_pairs={{0,1},{1,0},{2,3},{3,2},{8,9},{9,8},{10,11},{11,10},{16,17},{17,16... | collective-permute-start | bytes 9224 | tf_op jit(solution)/shard_map/ppermute | solution.py:368
  11.5 12.3 %collective-permute-start.4 = (bf16[1568,128]{1,0:T(8,128)(2,1)S(1)}, bf16[1568,128]{1,0:T(8,128)(2,1)S(1)}, u32[]{:S(2)}, u32[]{:S(2)}) collective-permute-start(bf16[1568,128]{1,0:T(8,128)(2,1)S(1)} %get-tuple-element.37.refs_1_), channel_id=1, source_target_pairs={{0,8},{1,9},{2,10},{3,11},{8,16},{9,17},{10,18},{11,19},{16,24},{1... | collective-permute-start | bytes 1204232 | tf_op jit(solution)/shard_map/ppermute | solution.py:368
  13.6 12.2 %collective-permute-start.5 = (bf16[1568,128]{1,0:T(8,128)(2,1)S(1)}, bf16[1568,128]{1,0:T(8,128)(2,1)S(1)}, u32[]{:S(2)}, u32[]{:S(2)}) collective-permute-start(bf16[1568,128]{1,0:T(8,128)(2,1)S(1)} %get-tuple-element.38), channel_id=1, source_target_pairs={{0,4},{1,5},{2,6},{3,7},{8,0},{9,1},{10,2},{11,3},{16,8},{17,9},{1... | collective-permute-start | bytes 1204232 | tf_op jit(solution)/shard_map/ppermute | solution.py:368
  16.9 18.9 %collective-permute-start.2 = (bf16[1536,128]{1,0:T(8,128)(2,1)S(1)}, bf16[1536,128]{1,0:T(8,128)(2,1)S(1)}, u32[]{:S(2)}, u32[]{:S(2)}) collective-permute-start(bf16[1536,128]{1,0:T(8,128)(2,1)S(1)} %collective-permute-done.refs_0_), channel_id=1, source_target_pairs={{0,8},{1,9},{2,10},{3,11},{8,16},{9,17},{10,18},{11,19},{16,24},{1... | collective-permute-start | bytes 1179656 | tf_op jit(solution)/shard_map/ppermute | solution.py:368
  18.5 17.3 %collective-permute-start.7 = (bf16[1536,128]{1,0:T(8,128)(2,1)S(1)}, bf16[1536,128]{1,0:T(8,128)(2,1)S(1)}, u32[]{:S(2)}, u32[]{:S(2)}) collective-permute-start(bf16[1536,128]{1,0:T(8,128)(2,1)S(1)} %collective-permute-done.1.refs_2_), channel_id=1, source_target_pairs={{0,4},{1,5},{2,6},{3,7},{8,0},{9,1},{10,2},{11,3},{16,8},{17,9},{1... | collective-permute-start | bytes 1179656 | tf_op jit(solution)/shard_map/ppermute | solution.py:368
  25.8 19.8 %collective-permute-start.11 = (bf16[1568,128]{1,0:T(8,128)(2,1)S(1)}, bf16[1568,128]{1,0:T(8,128)(2,1)S(1)}, u32[]{:S(2)}, u32[]{:S(2)}) collective-permute-start(bf16[1568,128]{1,0:T(8,128)(2,1)S(1)} %collective-permute-done.4.refs_1_), channel_id=1, source_target_pairs={{0,8},{1,9},{2,10},{3,11},{8,16},{9,17},{10,18},{11,19},{16,24},{1... | collective-permute-start | bytes 1204232 | tf_op jit(solution)/shard_map/ppermute | solution.py:368
  27.4 18.2 %collective-permute-start.12 = (bf16[1568,128]{1,0:T(8,128)(2,1)S(1)}, bf16[1568,128]{1,0:T(8,128)(2,1)S(1)}, u32[]{:S(2)}, u32[]{:S(2)}) collective-permute-start(bf16[1568,128]{1,0:T(8,128)(2,1)S(1)} %collective-permute-done.5.refs_3_), channel_id=1, source_target_pairs={{0,4},{1,5},{2,6},{3,7},{8,0},{9,1},{10,2},{11,3},{16,8},{17,9},{1... | collective-permute-start | bytes 1204232 | tf_op jit(solution)/shard_map/ppermute | solution.py:368
  35.8 17.0 %collective-permute-start.8 = (bf16[1536,128]{1,0:T(8,128)(2,1)S(1)}, bf16[1536,128]{1,0:T(8,128)(2,1)S(1)}, u32[]{:S(2)}, u32[]{:S(2)}) collective-permute-start(bf16[1536,128]{1,0:T(8,128)(2,1)S(1)} %collective-permute-done.2.refs_0_), channel_id=1, source_target_pairs={{0,8},{1,9},{2,10},{3,11},{8,16},{9,17},{10,18},{11,19},{16,24},{1... | collective-permute-start | bytes 1179656 | tf_op jit(solution)/shard_map/ppermute | solution.py:368
  37.4 15.4 %collective-permute-start.9 = (bf16[1536,128]{1,0:T(8,128)(2,1)S(1)}, bf16[1536,128]{1,0:T(8,128)(2,1)S(1)}, u32[]{:S(2)}, u32[]{:S(2)}) collective-permute-start(bf16[1536,128]{1,0:T(8,128)(2,1)S(1)} %collective-permute-done.7.refs_2_), channel_id=1, source_target_pairs={{0,4},{1,5},{2,6},{3,7},{8,0},{9,1},{10,2},{11,3},{16,8},{17,9},{1... | collective-permute-start | bytes 1179656 | tf_op jit(solution)/shard_map/ppermute | solution.py:368
  37.9 15.0 %collective-permute-start.10 = (bf16[32,128]{1,0:T(8,128)(2,1)S(1)}, bf16[32,128]{1,0:T(8,128)(2,1)S(1)}, u32[]{:S(2)}, u32[]{:S(2)}) collective-permute-start(bf16[32,128]{1,0:T(8,128)(2,1)S(1)} %get-tuple-element.50), channel_id=1, source_target_pairs={{0,28},{1,29},{2,30},{3,31},{8,20},{9,21},{10,22},{11,23},{16,12},... | collective-permute-start | bytes 24584 | tf_op jit(solution)/shard_map/ppermute | solution.py:368
  45.6 14.9 %collective-permute-start.15 = (bf16[1568,128]{1,0:T(8,128)(2,1)S(1)}, bf16[1568,128]{1,0:T(8,128)(2,1)S(1)}, u32[]{:S(2)}, u32[]{:S(2)}) collective-permute-start(bf16[1568,128]{1,0:T(8,128)(2,1)S(1)} %collective-permute-done.11.refs_1_), channel_id=1, source_target_pairs={{0,8},{1,9},{2,10},{3,11},{8,16},{9,17},{10,18},{11,19},{16,24},{1... | collective-permute-start | bytes 1204232 | tf_op jit(solution)/shard_map/ppermute | solution.py:368
  47.5 12.9 %collective-permute-start.16 = (bf16[1568,128]{1,0:T(8,128)(2,1)S(1)}, bf16[1568,128]{1,0:T(8,128)(2,1)S(1)}, u32[]{:S(2)}, u32[]{:S(2)}) collective-permute-start(bf16[1568,128]{1,0:T(8,128)(2,1)S(1)} %collective-permute-done.12.refs_3_), channel_id=1, source_target_pairs={{0,4},{1,5},{2,6},{3,7},{8,0},{9,1},{10,2},{11,3},{16,8},{17,9},{1... | collective-permute-start | bytes 1204232 | tf_op jit(solution)/shard_map/ppermute | solution.py:368
  58.2 9.4 %collective-permute-start.13 = (bf16[1536,128]{1,0:T(8,128)(2,1)S(1)}, bf16[1536,128]{1,0:T(8,128)(2,1)S(1)}, u32[]{:S(2)}, u32[]{:S(2)}) collective-permute-start(bf16[1536,128]{1,0:T(8,128)(2,1)S(1)} %collective-permute-done.8.refs_0_), channel_id=1, source_target_pairs={{0,8},{1,9},{2,10},{3,11},{8,16},{9,17},{10,18},{11,19},{16,24},{1... | collective-permute-start | bytes 1179656 | tf_op jit(solution)/shard_map/ppermute | solution.py:368
  59.6 8.7 %collective-permute-start.14 = (bf16[1536,128]{1,0:T(8,128)(2,1)S(1)}, bf16[1536,128]{1,0:T(8,128)(2,1)S(1)}, u32[]{:S(2)}, u32[]{:S(2)}) collective-permute-start(bf16[1536,128]{1,0:T(8,128)(2,1)S(1)} %collective-permute-done.9.refs_2_), channel_id=1, source_target_pairs={{0,4},{1,5},{2,6},{3,7},{8,0},{9,1},{10,2},{11,3},{16,8},{17,9},{1... | collective-permute-start | bytes 1179656 | tf_op jit(solution)/shard_map/ppermute | solution.py:368
